TPU v7x, 32 devices: a whole 2x2x4 slice. The times are simulated.
32 devices in a mesh: section: 2 (over x), dp: 4 (over z), mp: 4 (over y, core).
Axes of the slice: x: 2, y: 2, z: 4, core: 2. Of those that a mesh axis runs over, the one named last changes fastest.
Arguments:
- block_input: bfloat16 [2, 1024, 12, 1024], P('section', 'mp', 'dp'), may hold values from -6 to 6
- cotangent: bfloat16 [2, 1024, 12, 1024], P('section', 'mp', 'dp'), may hold values from -6 to 6
- segments: int32 [2, 12, 1024], P(None, 'dp'), may hold values from 0 to 2, as said below
- attn_weight: bfloat16 [2, 1024, 3, 1024], P('section', None, None, 'mp'), may hold values from -0.1875 to 0.1875
- attn_out: bfloat16 [2, 1024, 1024], P('section', 'mp'), may hold values from -1.5 to 1.5
- ffn_in: bfloat16 [2, 1024, 2, 2816], P('section', None, None, 'mp'), may hold values from -0.1875 to 0.1875
- ffn_out: bfloat16 [2, 2816, 1024], P('section', 'mp'), may hold values from -0.109375 to 0.109375
- cross_weight: bfloat16 [2, 1024, 2, 1024], P('section', None, None, 'mp'), may hold values from -1 to 1
- gains: float32 [2, 3, 1024], P('section'), may hold values from 0.1 to 1.9
Outputs:
- block_out: bfloat16 [2, 1024, 12, 1024], P('section', 'mp', 'dp')
- input_grad: float32 [2, 1024, 12, 1024], P('section', 'mp', 'dp')
- attn_weight_grad: float32 [2, 1024, 3, 1024], P('section', 'dp', None, 'mp')
- attn_out_grad: float32 [2, 1024, 1024], P('section', 'mp', 'dp')
- ffn_in_grad: float32 [2, 1024, 2, 2816], P('section', 'dp', None, 'mp')
- ffn_out_grad: float32 [2, 2816, 1024], P('section', 'mp', 'dp')
- cross_weight_grad: float32 [2, 1024, 2, 1024], P('section', 'dp', None, 'mp')
- gains_grad: float32 [2, 3, 1024], P('section', None, ('dp', 'mp'))
Inputs may be any that keep to these rules, and one draw needn't show every extreme that they name: `segments`: each row holds documents 0, 1 and 2 in order of position; documents 0 and 2 each have at least 1 and fewer than 128 positions, document 1 all positions between.
All inputs are finite; a program needn't handle non-finite values.
Results may differ from a plain program's by a relative error of at most 0.025.
Values may be sent and summed in bfloat16 or wider, within the bound.
A program may use at most 448 MiB of HBM per device.

v0:
```python
import jax
import jax.numpy as jnp
from jax import lax
from jax.sharding import PartitionSpec as P

DK = 64
LEN = 1024
MICRO = 3
ROWS_MB = 1


eps = 1e-06
neg_fill = -1e30


def from_behind(block, axis, distance):
    devices = range(lax.axis_size(axis))
    route = [(i - distance, i) for i in devices if i - distance in devices]
    return lax.ppermute(block, axis, route)


def norm_scale(tensor, scale_gain):
    return tensor * lax.rsqrt(jnp.mean(tensor * tensor, axis=-1, keepdims=True) + eps) * scale_gain


def norm_back(tensor, scale_gain, gradient):
    _, pull_back = jax.vjp(norm_scale, tensor, scale_gain)
    return pull_back(gradient)


def gathered_normed(tensor, scale_gain):
    normed = norm_scale(tensor, scale_gain).astype(jnp.bfloat16)
    return (normed, lax.all_gather(normed, "mp", axis=0, tiled=True))


def summed_rows(branch_term):
    return lax.psum_scatter(
        branch_term.astype(jnp.bfloat16), "mp", scatter_dimension=0, tiled=True
    ).astype(jnp.float32)


def gathered_grad(gradient):
    return lax.all_gather(gradient.astype(jnp.bfloat16), "mp", axis=0, tiled=True)


def summed_grads(branch_term):
    return lax.psum_scatter(
        branch_term.astype(jnp.bfloat16), "mp", scatter_dimension=0, tiled=True
    ).astype(jnp.float32)


def split_heads(tensor):
    return tensor.reshape(tensor.shape[:-1] + (tensor.shape[-1] // DK, DK))


def join_heads(tensor):
    return tensor.reshape(tensor.shape[:-2] + (tensor.shape[-2] * tensor.shape[-1],))


def block_rows(length):
    return 512 if length % 512 == 0 else length


def make_allowed(seg_query, seg_key, open_all):

    def allowed(start_row, block_size):
        seg_rows = lax.slice_in_dim(seg_query, start_row, start_row + block_size, axis=1)
        same_doc = seg_rows[:, :, None] == seg_key[:, None, :]
        query_place = start_row + lax.broadcasted_iota(jnp.int32, (block_size, seg_key.shape[1]), 0)
        key_place = lax.broadcasted_iota(jnp.int32, (block_size, seg_key.shape[1]), 1)
        return same_doc & jnp.logical_or(key_place <= query_place, open_all)[None]

    return allowed


def attend(queries, key_heads, value_heads, allowed):
    scale = queries.shape[-1] ** (-0.5)
    block_size = block_rows(queries.shape[0])
    outputs, log_parts = ([], [])
    for start_row in range(0, queries.shape[0], block_size):
        query_block = queries[start_row : start_row + block_size]
        scores = (
            jnp.einsum(
                "qrhd,krhd->rhqk", query_block, key_heads, preferred_element_type=jnp.float32
            )
            * scale
        )
        scores = jnp.where(allowed(start_row, block_size)[:, None], scores, neg_fill)
        row_max = jnp.max(scores, axis=-1, keepdims=True)
        exponent = jnp.exp(scores - row_max)
        row_total = jnp.sum(exponent, axis=-1, keepdims=True)
        weights_low = (exponent / row_total).astype(jnp.bfloat16)
        outputs.append(
            jnp.einsum(
                "rhqk,krhd->qrhd", weights_low, value_heads, preferred_element_type=jnp.float32
            )
        )
        log_parts.append((row_max + jnp.log(row_total))[..., 0])
    return (jnp.concatenate(outputs, 0), jnp.concatenate(log_parts, 2))


def attend_back(queries, key_heads, value_heads, log_total, grad_heads, allowed):
    scale = queries.shape[-1] ** (-0.5)
    block_size = block_rows(queries.shape[0])
    grad_query = []
    grad_key = jnp.zeros(key_heads.shape, jnp.float32)
    grad_value = jnp.zeros(value_heads.shape, jnp.float32)
    for start_row in range(0, queries.shape[0], block_size):
        query_block = queries[start_row : start_row + block_size]
        grad_block = grad_heads[start_row : start_row + block_size]
        log_block = log_total[:, :, start_row : start_row + block_size]
        scores = (
            jnp.einsum(
                "qrhd,krhd->rhqk", query_block, key_heads, preferred_element_type=jnp.float32
            )
            * scale
        )
        scores = jnp.where(allowed(start_row, block_size)[:, None], scores, neg_fill)
        weights = jnp.exp(scores - log_block[..., None])
        grad_value = grad_value + jnp.einsum(
            "rhqk,qrhd->krhd",
            weights.astype(jnp.bfloat16),
            grad_block,
            preferred_element_type=jnp.float32,
        )
        grad_weights = jnp.einsum(
            "qrhd,krhd->rhqk", grad_block, value_heads, preferred_element_type=jnp.float32
        )
        centred = grad_weights - jnp.sum(weights * grad_weights, axis=-1, keepdims=True)
        grad_scores = (weights * centred).astype(jnp.bfloat16)
        grad_query.append(
            jnp.einsum(
                "rhqk,krhd->qrhd", grad_scores, key_heads, preferred_element_type=jnp.float32
            )
            * scale
        )
        grad_key = (
            grad_key
            + jnp.einsum(
                "rhqk,qrhd->krhd", grad_scores, query_block, preferred_element_type=jnp.float32
            )
            * scale
        )
    return (jnp.concatenate(grad_query, 0), grad_key, grad_value)


def choose(encoder_side, enc_on, dec_on, enc_fn, dec_fn, blank_fn, *operands):
    if enc_on and dec_on:
        return lax.cond(encoder_side, enc_fn, dec_fn, *operands)
    if enc_on:
        return lax.cond(encoder_side, enc_fn, blank_fn, *operands)
    return lax.cond(encoder_side, blank_fn, dec_fn, *operands)


def body(
    block_input, cotangent, segments, attn_weight, attn_out, ffn_in, ffn_out, cross_weight, gains
):
    encoder_side = lax.axis_index("section") == 0
    w_qkv = attn_weight[0]
    w_out = attn_out[0]
    w_in = ffn_in[0]
    w_down = ffn_out[0]
    w_cross = cross_weight[0]
    gain_rows = gains[0]
    inputs = block_input[0].astype(jnp.float32)
    cot_rows = cotangent[0].astype(jnp.float32)
    micro_count = MICRO
    row_count = ROWS_MB
    full_shape = (LEN, row_count, inputs.shape[2])
    zero_pair = jnp.zeros((LEN, row_count, 2, w_cross.shape[2]), jnp.bfloat16)

    def zeros_of(*shaped):
        return tuple((jnp.zeros(item.shape, jnp.float32) for item in shaped))

    def blank_term(gathered):
        return jnp.zeros(full_shape, jnp.float32)

    def project_qkv(gathered):
        return split_heads(
            jnp.einsum("lrd,dch->lrch", gathered, w_qkv, preferred_element_type=jnp.float32).astype(
                jnp.bfloat16
            )
        )

    def self_forward(gathered, allowed):
        qkv_heads = project_qkv(gathered)
        mixture, _ = attend(qkv_heads[:, :, 0], qkv_heads[:, :, 1], qkv_heads[:, :, 2], allowed)
        mixture = join_heads(mixture.astype(jnp.bfloat16))
        return jnp.einsum("lrh,hd->lrd", mixture, w_out, preferred_element_type=jnp.float32)

    def ffn_forward(gathered):
        gate_up = jnp.einsum("lrd,dcf->lrcf", gathered, w_in, preferred_element_type=jnp.float32)
        hidden = (jax.nn.gelu(gate_up[:, :, 0], approximate=True) * gate_up[:, :, 1]).astype(
            jnp.bfloat16
        )
        return jnp.einsum("lrf,fd->lrd", hidden, w_down, preferred_element_type=jnp.float32)

    def cross_attend(gathered, pair_input, allowed):
        queries = split_heads(
            jnp.einsum(
                "lrd,dh->lrh", gathered, w_cross[:, 0], preferred_element_type=jnp.float32
            ).astype(jnp.bfloat16)
        )
        pair_heads = split_heads(pair_input)
        mixture, log_total = attend(queries, pair_heads[:, :, 0], pair_heads[:, :, 1], allowed)
        return (queries, pair_heads, mixture, log_total)

    def cross_forward(gathered, pair_input, allowed):
        _, _, mixture, _ = cross_attend(gathered, pair_input, allowed)
        return jnp.einsum(
            "lrh,dh->lrd",
            join_heads(mixture.astype(jnp.bfloat16)),
            w_cross[:, 1],
            preferred_element_type=jnp.float32,
        )

    def self_backward(gathered, gradient, allowed):
        qkv_heads = project_qkv(gathered)
        queries, key_heads, value_heads = (
            qkv_heads[:, :, 0],
            qkv_heads[:, :, 1],
            qkv_heads[:, :, 2],
        )
        mixture, log_total = attend(queries, key_heads, value_heads, allowed)
        mixture = join_heads(mixture.astype(jnp.bfloat16))
        grad_out = jnp.einsum("lrh,lrd->hd", mixture, gradient, preferred_element_type=jnp.float32)
        grad_mix = split_heads(
            jnp.einsum("lrd,hd->lrh", gradient, w_out, preferred_element_type=jnp.float32).astype(
                jnp.bfloat16
            )
        )
        grad_q, grad_k, grad_v = attend_back(
            queries, key_heads, value_heads, log_total, grad_mix, allowed
        )
        grad_qkv = join_heads(jnp.stack([grad_q, grad_k, grad_v], 2).astype(jnp.bfloat16))
        grad_normed = jnp.einsum(
            "lrch,dch->lrd", grad_qkv, w_qkv, preferred_element_type=jnp.float32
        )
        grad_weight = jnp.einsum(
            "lrd,lrch->dch", gathered, grad_qkv, preferred_element_type=jnp.float32
        )
        return (grad_normed, grad_weight, grad_out)

    def ffn_backward(gathered, gradient):
        gate_up = jnp.einsum("lrd,dcf->lrcf", gathered, w_in, preferred_element_type=jnp.float32)
        activated, gelu_pull = jax.vjp(
            lambda gate: jax.nn.gelu(gate, approximate=True), gate_up[:, :, 0]
        )
        hidden = (activated * gate_up[:, :, 1]).astype(jnp.bfloat16)
        grad_down = jnp.einsum("lrf,lrd->fd", hidden, gradient, preferred_element_type=jnp.float32)
        grad_hidden = jnp.einsum(
            "lrd,fd->lrf", gradient, w_down, preferred_element_type=jnp.float32
        )
        grad_gate = gelu_pull(grad_hidden * gate_up[:, :, 1])[0]
        grad_pair = jnp.stack([grad_gate, grad_hidden * activated], 2).astype(jnp.bfloat16)
        grad_normed = jnp.einsum(
            "lrcf,dcf->lrd", grad_pair, w_in, preferred_element_type=jnp.float32
        )
        grad_in = jnp.einsum(
            "lrd,lrcf->dcf", gathered, grad_pair, preferred_element_type=jnp.float32
        )
        return (grad_normed, grad_in, grad_down)

    def cross_backward(gathered, gradient, pair_input, allowed):
        queries, pair_heads, mixture, log_total = cross_attend(gathered, pair_input, allowed)
        mixture = join_heads(mixture.astype(jnp.bfloat16))
        grad_wo = jnp.einsum("lrd,lrh->dh", gradient, mixture, preferred_element_type=jnp.float32)
        grad_mix = split_heads(
            jnp.einsum(
                "lrd,dh->lrh", gradient, w_cross[:, 1], preferred_element_type=jnp.float32
            ).astype(jnp.bfloat16)
        )
        grad_q, grad_k, grad_v = attend_back(
            queries, pair_heads[:, :, 0], pair_heads[:, :, 1], log_total, grad_mix, allowed
        )
        grad_query = join_heads(grad_q.astype(jnp.bfloat16))
        grad_normed = jnp.einsum(
            "lrh,dh->lrd", grad_query, w_cross[:, 0], preferred_element_type=jnp.float32
        )
        grad_wq = jnp.einsum(
            "lrd,lrh->dh", gathered, grad_query, preferred_element_type=jnp.float32
        )
        grad_pair = join_heads(jnp.stack([grad_k, grad_v], 2).astype(jnp.bfloat16))
        return (grad_normed, jnp.stack([grad_wq, grad_wo], 1), grad_pair)

    def pair_backward(gathered, pair_grad):
        grad_normed = jnp.einsum(
            "lrch,dch->lrd", pair_grad, w_cross, preferred_element_type=jnp.float32
        )
        grad_cross = jnp.einsum(
            "lrd,lrch->dch", gathered, pair_grad, preferred_element_type=jnp.float32
        )
        return (grad_normed, grad_cross)

    def masks_for(seg_pair):
        own_seg = jnp.where(encoder_side, seg_pair[0], seg_pair[1])
        return (
            make_allowed(own_seg, own_seg, encoder_side),
            make_allowed(seg_pair[1], seg_pair[0], True),
        )

    def prelude(step_input, pair_input, seg_pair, enc_on, dec_on):
        self_mask, cross_mask = masks_for(seg_pair)
        _, gathered_one = gathered_normed(step_input, gain_rows[0])
        term_one = choose(
            encoder_side,
            enc_on,
            dec_on,
            lambda gathered: self_forward(gathered, self_mask),
            lambda gathered: self_forward(gathered, self_mask),
            blank_term,
            gathered_one,
        )
        mid_one = step_input + summed_rows(term_one)
        _, gathered_two = gathered_normed(mid_one, gain_rows[1])
        term_two = choose(
            encoder_side,
            enc_on,
            dec_on,
            ffn_forward,
            lambda gathered: cross_forward(gathered, pair_input, cross_mask),
            blank_term,
            gathered_two,
        )
        mid_two = mid_one + summed_rows(term_two)
        normed_three, gathered_three = gathered_normed(mid_two, gain_rows[2])
        return (gathered_one, gathered_two, gathered_three, mid_one, mid_two, normed_three)

    def enc_final(gathered, pair_input):
        pair_out = jnp.einsum(
            "lrd,dch->lrch", gathered, w_cross, preferred_element_type=jnp.float32
        )
        return (jnp.zeros(full_shape, jnp.float32), pair_out.astype(jnp.bfloat16))

    def dec_final(gathered, pair_input):
        return (ffn_forward(gathered), zero_pair)

    def blank_final(gathered, pair_input):
        return (jnp.zeros(full_shape, jnp.float32), zero_pair)

    def put_rows(buffer, batch_index, active, fresh):
        previous = lax.dynamic_slice_in_dim(buffer, batch_index * row_count, row_count, 1)
        return lax.dynamic_update_slice_in_dim(
            buffer, jnp.where(active, fresh, previous), batch_index * row_count, 1
        )

    out_buffer = jnp.zeros(inputs.shape, jnp.bfloat16)
    pair_send = zero_pair
    kept_states, pair_store = ([], [])
    for turn in range(micro_count + 1):
        enc_on, dec_on = (turn < micro_count, turn >= 1)
        pair_input = from_behind(pair_send, "section", 1)
        batch_index = jnp.clip(jnp.where(encoder_side, turn, turn - 1), 0, micro_count - 1)
        step_input = lax.dynamic_slice_in_dim(inputs, batch_index * row_count, row_count, 1)
        seg_pair = lax.dynamic_slice_in_dim(segments, batch_index * row_count, row_count, 1)
        state = prelude(step_input, pair_input, seg_pair, enc_on, dec_on)
        term_three, pair_send = choose(
            encoder_side, enc_on, dec_on, enc_final, dec_final, blank_final, state[2], pair_input
        )
        result = state[4] + summed_rows(term_three)
        fresh = jnp.where(encoder_side, state[5], result.astype(jnp.bfloat16))
        active = jnp.where(encoder_side, enc_on, dec_on)
        out_buffer = put_rows(out_buffer, batch_index, active, fresh)
        kept_states.append(state)
        pair_store.append(pair_input)

    def blank_first(gathered, gradient, pair_grad):
        return (jnp.zeros(full_shape, jnp.float32),) + zeros_of(w_in, w_down, w_cross)

    def enc_first(gathered, gradient, pair_grad):
        grad_normed, grad_cross = pair_backward(gathered, pair_grad)
        return (grad_normed,) + zeros_of(w_in, w_down) + (grad_cross,)

    def dec_first(gathered, gradient, pair_grad):
        return ffn_backward(gathered, gradient) + zeros_of(w_cross)

    grad_buffer = jnp.zeros(inputs.shape, jnp.float32)
    sum_qkv, sum_out, sum_in, sum_down, sum_cross = zeros_of(w_qkv, w_out, w_in, w_down, w_cross)
    sum_gain = jnp.zeros(gain_rows.shape, jnp.float32)
    back_send = zero_pair
    for turn in range(micro_count + 1):
        enc_on, dec_on = (turn >= 1, turn < micro_count)
        pair_grad = from_behind(back_send, "section", -1)
        batch_index = jnp.clip(
            jnp.where(encoder_side, micro_count - turn, micro_count - 1 - turn), 0, micro_count - 1
        )
        step_input = lax.dynamic_slice_in_dim(inputs, batch_index * row_count, row_count, 1)
        step_cot = lax.dynamic_slice_in_dim(cot_rows, batch_index * row_count, row_count, 1)
        seg_pair = lax.dynamic_slice_in_dim(segments, batch_index * row_count, row_count, 1)
        pair_input = pair_store[micro_count - turn]
        state = prelude(step_input, pair_input, seg_pair, enc_on, dec_on)
        gathered_one, gathered_two, gathered_three, mid_one, mid_two, _ = state
        self_mask, cross_mask = masks_for(seg_pair)
        active = jnp.where(encoder_side, enc_on, dec_on)
        weight_on = jnp.where(active, 1.0, 0.0)
        grad_full = gathered_grad(step_cot)
        grad_normed, grad_in_a, grad_down_a, grad_cross_a = choose(
            encoder_side,
            enc_on,
            dec_on,
            enc_first,
            dec_first,
            blank_first,
            gathered_three,
            grad_full,
            pair_grad,
        )
        grad_three = summed_grads(grad_normed)
        toward = jnp.where(encoder_side, step_cot + grad_three, grad_three)
        grad_part, gain_three = norm_back(mid_two, gain_rows[2], toward)
        grad_mid_two = jnp.where(encoder_side, 0.0, step_cot) + grad_part

        def enc_second(gathered, gradient, pair_value):
            return ffn_backward(gathered, gradient) + zeros_of(w_cross) + (zero_pair,)

        def dec_second(gathered, gradient, pair_value):
            grad_normed, grad_cross, grad_pair = cross_backward(
                gathered, gradient, pair_value, cross_mask
            )
            return (grad_normed,) + zeros_of(w_in, w_down) + (grad_cross, grad_pair)

        def blank_second(gathered, gradient, pair_value):
            return (
                (jnp.zeros(full_shape, jnp.float32),)
                + zeros_of(w_in, w_down, w_cross)
                + (zero_pair,)
            )

        grad_two_full = gathered_grad(grad_mid_two)
        grad_normed, grad_in_b, grad_down_b, grad_cross_b, back_send = choose(
            encoder_side,
            enc_on,
            dec_on,
            enc_second,
            dec_second,
            blank_second,
            gathered_two,
            grad_two_full,
            pair_input,
        )
        grad_two = summed_grads(grad_normed)
        grad_part, gain_two = norm_back(mid_one, gain_rows[1], grad_two)
        grad_mid_one = grad_mid_two + grad_part

        def self_third(gathered, gradient):
            return self_backward(gathered, gradient, self_mask)

        def blank_third(gathered, gradient):
            return (jnp.zeros(full_shape, jnp.float32),) + zeros_of(w_qkv, w_out)

        grad_one_full = gathered_grad(grad_mid_one)
        grad_normed, grad_qkv, grad_out = choose(
            encoder_side,
            enc_on,
            dec_on,
            self_third,
            self_third,
            blank_third,
            gathered_one,
            grad_one_full,
        )
        grad_one = summed_grads(grad_normed)
        grad_part, gain_one = norm_back(step_input, gain_rows[0], grad_one)
        grad_buffer = put_rows(grad_buffer, batch_index, active, grad_mid_one + grad_part)
        sum_qkv = sum_qkv + grad_qkv
        sum_out = sum_out + grad_out
        sum_in = sum_in + grad_in_a + grad_in_b
        sum_down = sum_down + grad_down_a + grad_down_b
        sum_cross = sum_cross + grad_cross_a + grad_cross_b
        sum_gain = sum_gain + jnp.stack([gain_one, gain_two, gain_three]) * weight_on
    totals = (
        lax.psum_scatter(
            sum_qkv.astype(jnp.bfloat16), "dp", scatter_dimension=0, tiled=True
        ).astype(jnp.float32),
        lax.psum_scatter(
            sum_out.astype(jnp.bfloat16), "dp", scatter_dimension=1, tiled=True
        ).astype(jnp.float32),
        lax.psum_scatter(sum_in.astype(jnp.bfloat16), "dp", scatter_dimension=0, tiled=True).astype(
            jnp.float32
        ),
        lax.psum_scatter(
            sum_down.astype(jnp.bfloat16), "dp", scatter_dimension=1, tiled=True
        ).astype(jnp.float32),
        lax.psum_scatter(
            sum_cross.astype(jnp.bfloat16), "dp", scatter_dimension=0, tiled=True
        ).astype(jnp.float32),
    )
    gain_total = lax.psum_scatter(sum_gain, ("dp", "mp"), scatter_dimension=1, tiled=True)
    return (
        out_buffer[None],
        grad_buffer[None],
        totals[0][None],
        totals[1][None],
        totals[2][None],
        totals[3][None],
        totals[4][None],
        gain_total[None],
    )


def solution(mesh):
    in_specs = (
        P("section", "mp", "dp", None),
        P("section", "mp", "dp", None),
        P(None, "dp", None),
        P("section", None, None, "mp"),
        P("section", "mp", None),
        P("section", None, None, "mp"),
        P("section", "mp", None),
        P("section", None, None, "mp"),
        P("section", None, None),
    )
    out_specs = (
        P("section", "mp", "dp", None),
        P("section", "mp", "dp", None),
        P("section", "dp", None, "mp"),
        P("section", "mp", "dp"),
        P("section", "dp", None, "mp"),
        P("section", "mp", "dp"),
        P("section", "dp", None, "mp"),
        P("section", None, ("dp", "mp")),
    )
    return jax.shard_map(body, mesh=mesh, in_specs=in_specs, out_specs=out_specs, check_vma=False)
```

profile of v0, /device:TPU:2, one launch (start us, length us, event | category | flops | bytes accessed | tf_op | source)
XLA Modules:
  0.0 2325.8 jit_solution(9921825591643513380)
XLA Ops:
  16.1 21.2 all-gather.40.cloned.1.call-done
  37.3 31.7 %conditional.34 = (bf16[1024,1024]{1,0:T(8,128)(2,1)S(1)}) conditional(s32[]{:T(128)} %convert_element_type.1160, (bf16[1024,1,1024]{2,0,1:T(8,128)(2,1)}, bf16[1024,3,256]{2,0,1:T(8,128)(2,1)}, s32[1,1024]{1,0:T(1,128)}, pred[]{:T(512)}, bf16[256,1024]{1,0:T(8,128)(2,1)S(1)}) %tuple.841, (bf16[1024,1,1024]{2,0,1:T(8,128)(2,1)}, ...), branch_computations={%region_40.45_spmd, %region_45.50_spmd} | conditional | flops 3252685312 | bytes 53530660 | solution.py:149
  70.5 36.3 %conditional.30 = (bf16[1024,1024]{1,0:T(8,128)(2,1)S(1)}) conditional(s32[]{:T(128)} %convert_element_type.1160, (bf16[1024,1,1024]{2,0,1:T(8,128)(2,1)}, bf16[1024,3,256]{2,0,1:T(8,128)(2,1)}, s32[1,1024]{1,0:T(1,128)S(1)}, pred[]{:T(512)}, bf16[256,1024]{1,0:T(8,128)(2,1)S(1)}) %tuple.843, (bf16[1024,1,1024]{2,0,1:T(8,128)(2,1)}, ...), branch_computations={%region_14.0_spmd, %region_19.24_spmd} | conditional | flops 3252685312 | bytes 53530660 | solution.py:149
  122.3 41.7 %conditional.40 = (bf16[1024,1,1024]{2,0,1:T(8,128)(2,1)}) conditional(s32[]{:T(128)} %convert_element_type.1160, (bf16[1024,1,1024]{2,0,1:T(8,128)(2,1)}, bf16[1024,3,256]{2,0,1:T(8,128)(2,1)}, s32[1,1024]{1,0:T(1,128)S(1)}, pred[]{:T(512)}, bf16[256,1024]{1,0:T(8,128)(2,1)}) %tuple.847, () %tuple.269), branch_computations={%region_83.88_spmd, %region_88.89_spmd} | conditional | flops 3252685312 | bytes 49336356 | solution.py:152
  164.3 15.0 reduce-scatter.39.cloned.1.call-done
  179.3 34.0 %reduce-scatter.79.cloned.1.call-done = bf16[256,1,1024]{2,0,1:T(8,128)(2,1)} async-done(((bf16[1024,1,1024]{2,0,1:T(8,128)(2,1)}), bf16[256,1,1024]{2,0,1:T(8,128)(2,1)}) %reduce-scatter.79.cloned.1.call-update) | async-done | bytes 524304 | tf_op jit(solution)/shard_map/reduce_scatter | solution.py:37
  213.3 34.1 %reduce-scatter.35.cloned.1.call-done = bf16[256,1,1024]{2,0,1:T(8,128)(2,1)} async-done(((bf16[1024,1,1024]{2,0,1:T(8,128)(2,1)}), bf16[256,1,1024]{2,0,1:T(8,128)(2,1)}) %reduce-scatter.35.cloned.1.call-update) | async-done | bytes 524304 | tf_op jit(solution)/shard_map/reduce_scatter | solution.py:37
  247.4 34.0 %reduce-scatter.57.cloned.1.call-done = bf16[256,1,1024]{2,0,1:T(8,128)(2,1)} async-done(((bf16[1024,1,1024]{2,0,1:T(8,128)(2,1)}), bf16[256,1,1024]{2,0,1:T(8,128)(2,1)}) %reduce-scatter.57.cloned.1.call-update) | async-done | bytes 524304 | tf_op jit(solution)/shard_map/reduce_scatter | solution.py:37
  288.1 22.7 all-gather.30.cloned.1.call-done
  312.5 38.4 %reduce-scatter.37.cloned.1.call-done = bf16[256,1,1024]{2,0,1:T(8,128)(2,1)} async-done(((bf16[1024,1,1024]{2,0,1:T(8,128)(2,1)}), bf16[256,1,1024]{2,0,1:T(8,128)(2,1)}) %reduce-scatter.37.cloned.1.call-update) | async-done | bytes 524304 | tf_op jit(solution)/shard_map/reduce_scatter | solution.py:37
  355.2 21.8 all-gather.36.cloned.1.call-done
  378.9 22.8 all-gather.34.cloned.1.call-done
  405.9 31.3 %conditional.32 = (bf16[1024,1024]{1,0:T(8,128)(2,1)}) conditional(s32[]{:T(128)} %convert_element_type.1160, (s32[1,1024]{1,0:T(1,128)S(1)}, s32[1,1,1024]{2,1,0:T(1,128)S(1)}, bf16[1024,1,1024]{2,0,1:T(8,128)(2,1)}, bf16[1024,2,256]{2,0,1:T(8,128)(2,1)S(1)}, bf16[1024,1,2,256]{0,3,2,1:T(8,128)(2,1)}) %tuple.824, ...), branch_computations={%region_28.33_spmd, %region_33.34_spmd} | conditional | flops 4436393984 | bytes 47235108 | solution.py:149
  437.3 31.5 %reduce-scatter.41.cloned.1.call-done = bf16[256,1,1024]{2,0,1:T(8,128)(2,1)} async-done(((bf16[1024,1,1024]{2,0,1:T(8,128)(2,1)}), bf16[256,1,1024]{2,0,1:T(8,128)(2,1)}) %reduce-scatter.41.cloned.1.call-update) | async-done | bytes 524304 | tf_op jit(solution)/shard_map/reduce_scatter | solution.py:37
  472.7 22.1 all-gather.38.cloned.1.call-done
  519.5 14.4 collective-permute-done.1
  533.9 30.9 %conditional.35 = (bf16[1024,1024]{1,0:T(8,128)(2,1)}) conditional(s32[]{:T(128)} %convert_element_type.1160, (s32[1,1024]{1,0:T(1,128)S(1)}, s32[1,1,1024]{2,1,0:T(1,128)S(1)}, bf16[1024,1,1024]{2,0,1:T(8,128)(2,1)}, bf16[1024,2,256]{2,0,1:T(8,128)(2,1)S(1)}, bf16[1024,1,2,256]{0,3,2,1:T(8,128)(2,1)}) %tuple.826, ...), branch_computations={%region_52.57_spmd, %region_57.58_spmd} | conditional | flops 4436393984 | bytes 47235108 | solution.py:149
  564.8 31.5 %reduce-scatter.47.cloned.1.call-done = bf16[256,1,1024]{2,0,1:T(8,128)(2,1)} async-done(((bf16[1024,1,1024]{2,0,1:T(8,128)(2,1)}), bf16[256,1,1024]{2,0,1:T(8,128)(2,1)}) %reduce-scatter.47.cloned.1.call-update) | async-done | bytes 524304 | tf_op jit(solution)/shard_map/reduce_scatter | solution.py:37
  600.4 22.0 all-gather.44.cloned.1.call-done
  661.0 30.1 %conditional.41 = (bf16[1024,1,1024]{2,0,1:T(8,128)(2,1)}) conditional(s32[]{:T(128)} %convert_element_type.1160, (s32[1,1024]{1,0:T(1,128)S(1)}, s32[1,1,1024]{2,1,0:T(1,128)S(1)}, bf16[1024,1,1024]{2,0,1:T(8,128)(2,1)}, bf16[1024,2,256]{2,0,1:T(8,128)(2,1)S(1)}, bf16[1024,1,2,256]{0,3,2,1:T(8,128)(2,1)}) %tuple.818, () %tuple.271), branch_computations={%region_91.96_spmd, %region_96.97_spmd} | conditional | flops 2175272960 | bytes 46186504 | solution.py:152
  696.0 26.7 %reduce-scatter.59.cloned.1.call-done = bf16[256,1,1024]{2,0,1:T(8,128)(2,1)} async-done(((bf16[1024,1,1024]{2,0,1:T(8,128)(2,1)}), bf16[256,1,1024]{2,0,1:T(8,128)(2,1)}) %reduce-scatter.59.cloned.1.call-update) | async-done | bytes 524304 | tf_op jit(solution)/shard_map/reduce_scatter | solution.py:37
  726.0 21.5 all-gather.52.cloned.1.call-done
  747.5 24.8 %all-gather.56.cloned.1.call-done = bf16[1024,1,1024]{2,0,1:T(8,128)(2,1)} async-done(((bf16[256,1,1024]{2,0,1:T(8,128)(2,1)}), bf16[1024,1,1024]{2,0,1:T(8,128)(2,1)}) %all-gather.56.cloned.1.call-update) | async-done | bytes 2097168 | tf_op jit(solution)/shard_map/all_gather | solution.py:33
  772.4 23.4 %conditional.42 = (bf16[1024,1,1024]{2,0,1:T(8,128)(2,1)}, f32[1024,2,704]{0,2,1:T(8,128)}, f32[704,1024]{1,0:T(8,128)}) conditional(s32[]{:T(128)} %convert_element_type.1160, (bf16[1024,1,1024]{2,0,1:T(8,128)(2,1)}, bf16[704,1024]{1,0:T(8,128)(2,1)}, bf16[1024,1,1024]{2,0,1:T(8,128)(2,1)}, bf16[1024,2,704]{0,2,1:T(8,128)(2,1)}) %tuple.860, ...), branch_computations={%region_99.100_spmd, %region_100.101_spmd} | conditional | flops 11838554112 | bytes 86376584 | solution.py:152
  795.8 31.5 %reduce-scatter.61.cloned.1.call-done = bf16[256,1,1024]{2,0,1:T(8,128)(2,1)} async-done(((bf16[1024,1,1024]{2,0,1:T(8,128)(2,1)}), bf16[256,1,1024]{2,0,1:T(8,128)(2,1)}) %reduce-scatter.61.cloned.1.call-update) | async-done | bytes 524304 | tf_op jit(solution)/shard_map/reduce_scatter | solution.py:47
  833.4 22.0 all-gather.58.cloned.1.call-done
  855.4 52.6 %conditional.43 = (bf16[1024,1,1024]{2,0,1:T(8,128)(2,1)}, bf16[1024,1,2,256]{0,3,2,1:T(8,128)(2,1)S(1)}, f32[]{:T(128)}, f32[1024,2,256]{2,1,0:T(2,128)}) conditional(s32[]{:T(128)} %convert_element_type.1160, (s32[1,1024]{1,0:T(1,128)S(1)}, s32[1,1,1024]{2,1,0:T(1,128)S(1)}, bf16[1024,1,1024]{2,0,1:T(8,128)(2,1)}, ...), branch_computations={%region_103.110_spmd, %region_110.111_spmd} | conditional | flops 5984739328 | bytes 240353472 | solution.py:152
  910.0 23.0 collective-permute-done.3
  933.9 24.9 %conditional.45 = (f32[1024,2,704]{0,2,1:T(8,128)}, f32[704,1024]{1,0:T(8,128)}, f32[1024,2,256]{2,1,0:T(2,128)}, bf16[1024,1024]{1,0:T(8,128)(2,1)}) conditional(s32[]{:T(128)} %convert_element_type.1160, (bf16[1024,1,1024]{2,0,1:T(8,128)(2,1)}, bf16[704,1024]{1,0:T(8,128)(2,1)}, bf16[1024,1,1024]{2,0,1:T(8,128)(2,1)}, ...), branch_computations={%region_123.124_spmd, %region_124.125_spmd} | conditional | flops 11838554112 | bytes 88473752 | solution.py:149
  958.9 31.5 %reduce-scatter.67.cloned.1.call-done = bf16[256,1,1024]{2,0,1:T(8,128)(2,1)} async-done(((bf16[1024,1,1024]{2,0,1:T(8,128)(2,1)}), bf16[256,1,1024]{2,0,1:T(8,128)(2,1)}) %reduce-scatter.67.cloned.1.call-update) | async-done | bytes 524304 | tf_op jit(solution)/shard_map/reduce_scatter | solution.py:47
  995.3 21.9 all-gather.64.cloned.1.call-done
  1017.3 58.7 %conditional.46 = (f32[704,1024]{1,0:T(8,128)}, bf16[1024,1,2,256]{0,3,2,1:T(8,128)(2,1)S(1)}, bf16[1024,1024]{1,0:T(8,128)(2,1)}, f32[1024,2,704]{0,2,1:T(8,128)}, f32[1024,2,256]{2,1,0:T(2,128)}) conditional(s32[]{:T(128)} %convert_element_type.1160, (s32[1,1024]{1,0:T(1,128)S(1)}, s32[1,1,1024]{2,1,0:T(1,128)S(1)}, ...), branch_computations={%region_127.134_spmd, %region_134.135_spmd} | conditional | flops 11838554112 | bytes 253198560 | solution.py:149
  1077.9 23.0 collective-permute-done.4
  1101.8 25.2 %conditional.48 = (f32[1024,2,704]{0,2,1:T(8,128)}, f32[704,1024]{1,0:T(8,128)}, f32[1024,2,256]{2,1,0:T(2,128)}, bf16[1024,1024]{1,0:T(8,128)(2,1)}) conditional(s32[]{:T(128)} %convert_element_type.1160, (bf16[1024,1,1024]{2,0,1:T(8,128)(2,1)}, bf16[704,1024]{1,0:T(8,128)(2,1)}, bf16[1024,1,1024]{2,0,1:T(8,128)(2,1)}, ...), branch_computations={%region_153.154_spmd, %region_154.155_spmd} | conditional | flops 11838554112 | bytes 88473752 | solution.py:149
  1127.1 31.5 %reduce-scatter.73.cloned.1.call-done = bf16[256,1,1024]{2,0,1:T(8,128)(2,1)} async-done(((bf16[1024,1,1024]{2,0,1:T(8,128)(2,1)}), bf16[256,1,1024]{2,0,1:T(8,128)(2,1)}) %reduce-scatter.73.cloned.1.call-update) | async-done | bytes 524304 | tf_op jit(solution)/shard_map/reduce_scatter | solution.py:47
  1164.2 21.2 all-gather.70.cloned.1.call-done
  1185.5 64.1 %conditional.49 = (f32[704,1024]{1,0:T(8,128)}, bf16[1024,1,2,256]{0,3,2,1:T(8,128)(2,1)}, bf16[1024,1024]{1,0:T(8,128)(2,1)}, f32[1024,2,704]{0,2,1:T(8,128)}, f32[1024,2,256]{2,1,0:T(2,128)}) conditional(s32[]{:T(128)} %convert_element_type.1160, (s32[1,1024]{1,0:T(1,128)S(1)}, s32[1,1,1024]{2,1,0:T(1,128)S(1)}, ...), branch_computations={%region_157.164_spmd, %region_164.165_spmd} | conditional | flops 11838554112 | bytes 232227008 | solution.py:149
  1253.6 33.8 %reduce-scatter.75.cloned.1.call-done = bf16[256,1,1024]{2,0,1:T(8,128)(2,1)} async-done(((bf16[1024,1,1024]{2,0,1:T(8,128)(2,1)}), bf16[256,1,1024]{2,0,1:T(8,128)(2,1)}) %reduce-scatter.75.cloned.1.call-update) | async-done | bytes 524304 | tf_op jit(solution)/shard_map/reduce_scatter | solution.py:47
  1294.9 22.7 all-gather.74.cloned.1.call-done
  1319.5 38.3 %reduce-scatter.81.cloned.1.call-done = bf16[256,1,1024]{2,0,1:T(8,128)(2,1)} async-done(((bf16[1024,1,1024]{2,0,1:T(8,128)(2,1)}), bf16[256,1,1024]{2,0,1:T(8,128)(2,1)}) %reduce-scatter.81.cloned.1.call-update) | async-done | bytes 524304 | tf_op jit(solution)/shard_map/reduce_scatter | solution.py:37
  1366.2 21.4 collective-permute-done.5
  1391.1 39.2 %reduce-scatter.83.cloned.1.call-done = bf16[256,1,1024]{2,0,1:T(8,128)(2,1)} async-done(((bf16[1024,1,1024]{2,0,1:T(8,128)(2,1)}), bf16[256,1,1024]{2,0,1:T(8,128)(2,1)}) %reduce-scatter.83.cloned.1.call-update) | async-done | bytes 524304 | tf_op jit(solution)/shard_map/reduce_scatter | solution.py:47
  1435.3 22.7 all-gather.78.cloned.1.call-done
  1467.2 44.6 %reduce-scatter.85.cloned.1.call-done = bf16[256,1,1024]{2,0,1:T(8,128)(2,1)} async-done(((bf16[1024,1,1024]{2,0,1:T(8,128)(2,1)}), bf16[256,1,1024]{2,0,1:T(8,128)(2,1)}) %reduce-scatter.85.cloned.1.call-update) | async-done | bytes 524304 | tf_op jit(solution)/shard_map/reduce_scatter | solution.py:47
  1516.1 20.5 all-gather.72.cloned.1.call-done
  1536.6 66.3 %conditional.50 = (f32[256,1024]{1,0:T(8,128)}, bf16[1024,1024]{1,0:T(8,128)(2,1)}, f32[1024,3,256]{2,0,1:T(8,128)}) conditional(s32[]{:T(128)} %convert_element_type.1160, (bf16[1024,1,1024]{2,0,1:T(8,128)(2,1)}, bf16[1024,3,256]{2,0,1:T(8,128)(2,1)}, s32[1,1024]{1,0:T(1,128)S(1)}, pred[]{:T(512)}, bf16[1024,1,1024]{2,0,1:T(8,128)(2,1)}, ...), branch_computations={%region_167.174_spmd, %region_174.181_spmd} | conditional | flops 9210683392 | bytes 252940512 | solution.py:149
  1603.1 57.3 %conditional.44 = (bf16[1024,1,1024]{2,0,1:T(8,128)(2,1)S(1)}, f32[256,1024]{1,0:T(8,128)}, f32[1024,3,256]{2,0,1:T(8,128)}) conditional(s32[]{:T(128)} %convert_element_type.1160, (bf16[1024,1,1024]{2,0,1:T(8,128)(2,1)}, bf16[1024,3,256]{2,0,1:T(8,128)(2,1)}, s32[1,1024]{1,0:T(1,128)S(1)}, pred[]{:T(512)}, bf16[1024,1,1024]{2,0,1:T(8,128)(2,1)}, ...), branch_computations={%region_113.120_spmd, %region_120.121_spmd} | conditional | flops 9210683392 | bytes 377721280 | solution.py:152
  1661.8 67.5 %conditional.47 = (f32[256,1024]{1,0:T(8,128)}, bf16[1024,1024]{1,0:T(8,128)(2,1)}, f32[1024,3,256]{2,0,1:T(8,128)}) conditional(s32[]{:T(128)} %convert_element_type.1160, (bf16[1024,1,1024]{2,0,1:T(8,128)(2,1)}, bf16[1024,3,256]{2,0,1:T(8,128)(2,1)}, s32[1,1024]{1,0:T(1,128)}, pred[]{:T(512)}, bf16[1024,1,1024]{2,0,1:T(8,128)(2,1)}, ...), branch_computations={%region_137.144_spmd, %region_144.151_spmd} | conditional | flops 9210683392 | bytes 252940512 | solution.py:149
  1729.5 15.7 conditional.55
  1745.3 34.9 %conditional.37 = (bf16[1024,1,1024]{2,0,1:T(8,128)(2,1)}) conditional(s32[]{:T(128)} %convert_element_type.1160, (bf16[1024,1,1024]{2,0,1:T(8,128)(2,1)}, bf16[1024,3,256]{2,0,1:T(8,128)(2,1)}, s32[1,1024]{1,0:T(1,128)S(1)}, pred[]{:T(512)}, bf16[256,1024]{1,0:T(8,128)(2,1)}) %tuple.854, () %tuple.264), branch_computations={%region_64.69_spmd, %region_69.70_spmd} | conditional | flops 3252685312 | bytes 49336356 | solution.py:152
  1780.6 14.7 reduce-scatter.87.cloned.1.call-done
  1804.8 24.3 %reduce-scatter.51.cloned.1.call-done = bf16[256,1,1024]{2,0,1:T(8,128)(2,1)} async-done(((bf16[1024,1,1024]{2,0,1:T(8,128)(2,1)}), bf16[256,1,1024]{2,0,1:T(8,128)(2,1)}) %reduce-scatter.51.cloned.1.call-update) | async-done | bytes 524304 | tf_op jit(solution)/shard_map/reduce_scatter | solution.py:37
  1834.8 22.7 all-gather.48.cloned.1.call-done
  1857.5 32.0 %conditional.38 = (bf16[1024,1,1024]{2,0,1:T(8,128)(2,1)}) conditional(s32[]{:T(128)} %convert_element_type.1160, (s32[1,1024]{1,0:T(1,128)S(1)}, s32[1,1,1024]{2,1,0:T(1,128)S(1)}, bf16[1024,1,1024]{2,0,1:T(8,128)(2,1)}, bf16[1024,2,256]{2,0,1:T(8,128)(2,1)}, bf16[1024,1,2,256]{0,3,2,1:T(8,128)(2,1)}) %tuple.820, () %tuple.266), branch_computations={%region_72.77_spmd, %region_77.78_spmd} | conditional | flops 2175272960 | bytes 50380836 | solution.py:152
  1889.6 31.5 %reduce-scatter.53.cloned.1.call-done = bf16[256,1,1024]{2,0,1:T(8,128)(2,1)} async-done(((bf16[1024,1,1024]{2,0,1:T(8,128)(2,1)}), bf16[256,1,1024]{2,0,1:T(8,128)(2,1)}) %reduce-scatter.53.cloned.1.call-update) | async-done | bytes 524304 | tf_op jit(solution)/shard_map/reduce_scatter | solution.py:37
  1942.8 14.8 add_convert_fusion
  1986.4 29.4 %reduce-scatter.49.cloned.1.call-done = bf16[256,1,1024]{2,0,1:T(8,128)(2,1)} async-done(((bf16[1024,1,1024]{2,0,1:T(8,128)(2,1)}), bf16[256,1,1024]{2,0,1:T(8,128)(2,1)}) %reduce-scatter.49.cloned.1.call-update) | async-done | bytes 524304 | tf_op jit(solution)/shard_map/reduce_scatter | solution.py:37
  2020.8 49.2 %all-reduce.3.cloned.1.call-done = bf16[1024,2,256]{2,1,0:T(2,128)(2,1)} async-done(((bf16[1024,2,256]{2,1,0:T(2,128)(2,1)}), bf16[1024,2,256]{2,1,0:T(2,128)(2,1)}) %all-reduce.3.cloned.1.call-update) | async-done | bytes 1048592
  2071.9 33.7 %reduce-scatter.95.cloned.1.call-done = bf16[704,256]{1,0:T(8,128)(2,1)} async-done(((bf16[704,1024]{1,0:T(8,128)(2,1)}), bf16[704,256]{1,0:T(8,128)(2,1)}) %reduce-scatter.95.cloned.1.call-update) | async-done | bytes 360464 | tf_op jit(solution)/shard_map/reduce_scatter | solution.py:481
  2107.6 56.2 %reduce-scatter.93.cloned.1.call-done = bf16[256,2,704]{0,2,1:T(8,128)(2,1)} async-done(((bf16[1024,2,704]{0,2,1:T(8,128)(2,1)}), bf16[256,2,704]{0,2,1:T(8,128)(2,1)}) %reduce-scatter.93.cloned.1.call-update) | async-done | bytes 720912 | tf_op jit(solution)/shard_map/reduce_scatter | solution.py:478
  2166.1 22.2 reduce-scatter.91.cloned.1.call-done
  2189.9 34.3 %reduce-scatter.89.cloned.1.call-done = bf16[256,3,256]{2,0,1:T(8,128)(2,1)} async-done(((bf16[1024,3,256]{2,0,1:T(8,128)(2,1)}), bf16[256,3,256]{2,0,1:T(8,128)(2,1)}) %reduce-scatter.89.cloned.1.call-update) | async-done | bytes 393232 | tf_op jit(solution)/shard_map/reduce_scatter | solution.py:472
  2233.2 49.5 %reduce-scatter.97.cloned.1.call-done = f32[64,3]{1,0:T(8,128)} async-done(((f32[1024,3]{1,0:T(8,128)}), f32[64,3]{1,0:T(8,128)}) %reduce-scatter.97.cloned.1.call-update) | async-done | bytes 784
  2284.1 31.6 %reduce-scatter.55.cloned.1.call-done = bf16[256,1,1024]{2,0,1:T(8,128)(2,1)} async-done(((bf16[1024,1,1024]{2,0,1:T(8,128)(2,1)}), bf16[256,1,1024]{2,0,1:T(8,128)(2,1)}) %reduce-scatter.55.cloned.1.call-update) | async-done | bytes 524304 | tf_op jit(solution)/shard_map/reduce_scatter | solution.py:37
  (979 shorter events, 984.9 us)
Async XLA Ops:
  7.2 30.1 %all-gather.40.cloned.1.call-start = ((), (), s32[]{:S(2)}) async-start(), calls=%async_computation.43 | async-start | bytes 2621440 | tf_op jit(solution)/shard_map/all_gather | solution.py:33
  13.3 57.1 %all-gather.32.cloned.1.call-start = ((), (), s32[]{:S(2)}) async-start(), calls=%async_computation.36 | async-start | bytes 2621440 | tf_op jit(solution)/shard_map/all_gather | solution.py:33
  14.1 94.7 %all-gather.28.cloned.1.call-start = ((), (), s32[]{:S(2)}) async-start(), calls=%async_computation.32 | async-start | bytes 2621440 | tf_op jit(solution)/shard_map/all_gather | solution.py:33
  14.8 107.4 %all-gather.46.cloned.1.call-start = ((), (), s32[]{:S(2)}) async-start(), calls=%async_computation.49 | async-start | bytes 2621440 | tf_op jit(solution)/shard_map/all_gather | solution.py:33
  15.4 148.9 %reduce-scatter.45.cloned.1.call-start = ((), (), s32[]{:S(2)}) async-start(), calls=%async_computation.44 | async-start | bytes 2621440 | tf_op jit(solution)/shard_map/reduce_scatter | solution.py:37
  70.4 108.9 %reduce-scatter.39.cloned.1.call-start = ((), (), s32[]{:S(2)}) async-start(), calls=%async_computation.37 | async-start | bytes 2621440 | tf_op jit(solution)/shard_map/reduce_scatter | solution.py:37
  108.1 105.1 %reduce-scatter.79.cloned.1.call-start = ((), (), s32[]{:S(2)}) async-start(), calls=%async_computation.77 | async-start | bytes 2621440 | tf_op jit(solution)/shard_map/reduce_scatter | solution.py:37
  115.5 131.9 %reduce-scatter.35.cloned.1.call-start = ((), (), s32[]{:S(2)}) async-start(), calls=%async_computation.33 | async-start | bytes 2621440 | tf_op jit(solution)/shard_map/reduce_scatter | solution.py:37
  122.2 159.2 %reduce-scatter.57.cloned.1.call-start = ((), (), s32[]{:S(2)}) async-start(), calls=%async_computation.56 | async-start | bytes 2621440 | tf_op jit(solution)/shard_map/reduce_scatter | solution.py:37
  164.0 146.8 %all-gather.30.cloned.1.call-start = ((), (), s32[]{:S(2)}) async-start(), calls=%async_computation.34 | async-start | bytes 2621440 | tf_op jit(solution)/shard_map/all_gather | solution.py:33
  288.0 62.9 %reduce-scatter.37.cloned.1.call-start = ((), (), s32[]{:S(2)}) async-start(), calls=%async_computation.35 | async-start | bytes 2621440 | tf_op jit(solution)/shard_map/reduce_scatter | solution.py:37
  312.5 64.5 %all-gather.36.cloned.1.call-start = ((), (), s32[]{:S(2)}) async-start(), calls=%async_computation.39 | async-start | bytes 2621440 | tf_op jit(solution)/shard_map/all_gather | solution.py:33
  354.2 47.5 %all-gather.34.cloned.1.call-start = ((), (), s32[]{:S(2)}) async-start(), calls=%async_computation.38 | async-start | bytes 2621440 | tf_op jit(solution)/shard_map/all_gather | solution.py:33
  355.0 113.8 %reduce-scatter.41.cloned.1.call-start = ((), (), s32[]{:S(2)}) async-start(), calls=%async_computation.40 | async-start | bytes 2621440 | tf_op jit(solution)/shard_map/reduce_scatter | solution.py:37
  377.6 28.3 %collective-permute-start = (bf16[1024,1,2,256]{0,3,2,1:T(8,128)(2,1)S(1)}, bf16[1024,1,2,256]{0,3,2,1:T(8,128)(2,1)}, u32[]{:S(2)}, u32[]{:S(2)}) collective-permute-start(bf16[1024,1,2,256]{0,3,2,1:T(8,128)(2,1)S(1)} %copy.185), channel_id=1, source_target_pairs={{0,16},{1,17},{2,18},{3,19},{4,20},{5,21},{6,22},{7,23},{8,24},{9,... | collective-permute-start | bytes 3145736 | tf_op jit(solution)/shard_map/ppermute | solution.py:19
  437.2 57.6 %all-gather.38.cloned.1.call-start = ((), (), s32[]{:S(2)}) async-start(), calls=%async_computation.41 | async-start | bytes 2621440 | tf_op jit(solution)/shard_map/all_gather | solution.py:33
  472.1 47.4 %all-gather.42.cloned.1.call-start = ((), (), s32[]{:S(2)}) async-start(), calls=%async_computation.45 | async-start | bytes 2621440 | tf_op jit(solution)/shard_map/all_gather | solution.py:33
  472.6 123.7 %reduce-scatter.47.cloned.1.call-start = ((), (), s32[]{:S(2)}) async-start(), calls=%async_computation.46 | async-start | bytes 2621440 | tf_op jit(solution)/shard_map/reduce_scatter | solution.py:37
  506.6 27.3 %collective-permute-start.1 = (bf16[1024,1,2,256]{0,3,2,1:T(8,128)(2,1)S(1)}, bf16[1024,1,2,256]{0,3,2,1:T(8,128)(2,1)}, u32[]{:S(2)}, u32[]{:S(2)}) collective-permute-start(bf16[1024,1,2,256]{0,3,2,1:T(8,128)(2,1)S(1)} %copy.189), channel_id=1, source_target_pairs={{0,16},{1,17},{2,18},{3,19},{4,20},{5,21},{6,22},{7,23},{8,24},{9,... | collective-permute-start | bytes 3145736 | tf_op jit(solution)/shard_map/ppermute | solution.py:19
  564.8 57.5 %all-gather.44.cloned.1.call-start = ((), (), s32[]{:S(2)}) async-start(), calls=%async_computation.47 | async-start | bytes 2621440 | tf_op jit(solution)/shard_map/all_gather | solution.py:33
  599.6 47.5 %all-gather.54.cloned.1.call-start = ((), (), s32[]{:S(2)}) async-start(), calls=%async_computation.57 | async-start | bytes 2621440 | tf_op jit(solution)/shard_map/all_gather | solution.py:33
  600.3 122.4 %reduce-scatter.59.cloned.1.call-start = ((), (), s32[]{:S(2)}) async-start(), calls=%async_computation.58 | async-start | bytes 2621440 | tf_op jit(solution)/shard_map/reduce_scatter | solution.py:37
  633.7 27.3 %collective-permute-start.2 = (bf16[1024,1,2,256]{0,3,2,1:T(8,128)(2,1)S(1)}, bf16[1024,1,2,256]{0,3,2,1:T(8,128)(2,1)}, u32[]{:S(2)}, u32[]{:S(2)}) collective-permute-start(bf16[1024,1,2,256]{0,3,2,1:T(8,128)(2,1)S(1)} %copy.192), channel_id=1, source_target_pairs={{0,16},{1,17},{2,18},{3,19},{4,20},{5,21},{6,22},{7,23},{8,24},{9,... | collective-permute-start | bytes 3145736 | tf_op jit(solution)/shard_map/ppermute | solution.py:19
  691.1 56.4 %all-gather.52.cloned.1.call-start = ((), (), s32[]{:S(2)}) async-start(), calls=%async_computation.55 | async-start | bytes 2621440 | tf_op jit(solution)/shard_map/all_gather | solution.py:43
  696.0 76.4 %all-gather.56.cloned.1.call-start = ((), (), s32[]{:S(2)}) async-start(), calls=%async_computation.59 | async-start | bytes 2621440 | tf_op jit(solution)/shard_map/all_gather | solution.py:33
  726.0 101.3 %reduce-scatter.61.cloned.1.call-start = ((), (), s32[]{:S(2)}) async-start(), calls=%async_computation.60 | async-start | bytes 2621440 | tf_op jit(solution)/shard_map/reduce_scatter | solution.py:47
  795.8 59.6 %all-gather.58.cloned.1.call-start = ((), (), s32[]{:S(2)}) async-start(), calls=%async_computation.61 | async-start | bytes 2621440 | tf_op jit(solution)/shard_map/all_gather | solution.py:43
  832.6 77.3 %all-gather.62.cloned.1.call-start = ((), (), s32[]{:S(2)}) async-start(), calls=%async_computation.65 | async-start | bytes 2621440 | tf_op jit(solution)/shard_map/all_gather | solution.py:43
  833.4 157.0 %reduce-scatter.67.cloned.1.call-start = ((), (), s32[]{:S(2)}) async-start(), calls=%async_computation.66 | async-start | bytes 2621440 | tf_op jit(solution)/shard_map/reduce_scatter | solution.py:47
  958.9 58.4 %all-gather.64.cloned.1.call-start = ((), (), s32[]{:S(2)}) async-start(), calls=%async_computation.67 | async-start | bytes 2621440 | tf_op jit(solution)/shard_map/all_gather | solution.py:43
  994.5 83.3 %all-gather.68.cloned.1.call-start = ((), (), s32[]{:S(2)}) async-start(), calls=%async_computation.71 | async-start | bytes 2621440 | tf_op jit(solution)/shard_map/all_gather | solution.py:43
  995.3 163.4 %reduce-scatter.73.cloned.1.call-start = ((), (), s32[]{:S(2)}) async-start(), calls=%async_computation.72 | async-start | bytes 2621440 | tf_op jit(solution)/shard_map/reduce_scatter | solution.py:47
  1127.1 58.4 %all-gather.70.cloned.1.call-start = ((), (), s32[]{:S(2)}) async-start(), calls=%async_computation.73 | async-start | bytes 2621440 | tf_op jit(solution)/shard_map/all_gather | solution.py:43
  1162.7 87.1 %reduce-scatter.63.cloned.1.call-start = ((), (), s32[]{:S(2)}) async-start(), calls=%async_computation.62 | async-start | bytes 2621440 | tf_op jit(solution)/shard_map/reduce_scatter | solution.py:47
  1163.5 90.2 %reduce-scatter.69.cloned.1.call-start = ((), (), s32[]{:S(2)}) async-start(), calls=%async_computation.68 | async-start | bytes 2621440 | tf_op jit(solution)/shard_map/reduce_scatter | solution.py:47
  1164.2 123.2 %reduce-scatter.75.cloned.1.call-start = ((), (), s32[]{:S(2)}) async-start(), calls=%async_computation.74 | async-start | bytes 2621440 | tf_op jit(solution)/shard_map/reduce_scatter | solution.py:47
  1249.7 67.8 %all-gather.74.cloned.1.call-start = ((), (), s32[]{:S(2)}) async-start(), calls=%async_computation.78 | async-start | bytes 2621440 | tf_op jit(solution)/shard_map/all_gather | solution.py:33
  1294.8 63.0 %reduce-scatter.81.cloned.1.call-start = ((), (), s32[]{:S(2)}) async-start(), calls=%async_computation.79 | async-start | bytes 2621440 | tf_op jit(solution)/shard_map/reduce_scatter | solution.py:37
  1319.4 68.1 %all-gather.76.cloned.1.call-start = ((), (), s32[]{:S(2)}) async-start(), calls=%async_computation.80 | async-start | bytes 2621440 | tf_op jit(solution)/shard_map/all_gather | solution.py:33
  1361.1 69.2 %reduce-scatter.83.cloned.1.call-start = ((), (), s32[]{:S(2)}) async-start(), calls=%async_computation.81 | async-start | bytes 2621440 | tf_op jit(solution)/shard_map/reduce_scatter | solution.py:47
  1362.7 24.9 %collective-permute-start.5 = (bf16[1024,1,2,256]{3,0,2,1:T(8,128)(2,1)S(1)}, bf16[1024,1,2,256]{3,0,2,1:T(8,128)(2,1)}, u32[]{:S(2)}, u32[]{:S(2)}) collective-permute-start(bf16[1024,1,2,256]{3,0,2,1:T(8,128)(2,1)S(1)} %copy.198), channel_id=1, source_target_pairs={{16,0},{17,1},{18,2},{19,3},{20,4},{21,5},{22,6},{23,7},{24,8},{25... | collective-permute-start | bytes 3145736 | tf_op jit(solution)/shard_map/ppermute | solution.py:19
  1391.1 66.9 %all-gather.78.cloned.1.call-start = ((), (), s32[]{:S(2)}) async-start(), calls=%async_computation.82 | async-start | bytes 2621440 | tf_op jit(solution)/shard_map/all_gather | solution.py:43
  1435.3 76.6 %reduce-scatter.85.cloned.1.call-start = ((), (), s32[]{:S(2)}) async-start(), calls=%async_computation.83 | async-start | bytes 2621440 | tf_op jit(solution)/shard_map/reduce_scatter | solution.py:47
  1464.9 71.7 %all-gather.72.cloned.1.call-start = ((), (), s32[]{:S(2)}) async-start(), calls=%async_computation.75 | async-start | bytes 2621440 | tf_op jit(solution)/shard_map/all_gather | solution.py:43
  1465.7 137.4 %all-gather.60.cloned.1.call-start = ((), (), s32[]{:S(2)}) async-start(), calls=%async_computation.63 | async-start | bytes 2621440 | tf_op jit(solution)/shard_map/all_gather | solution.py:43
  1466.4 195.4 %all-gather.66.cloned.1.call-start = ((), (), s32[]{:S(2)}) async-start(), calls=%async_computation.69 | async-start | bytes 2621440 | tf_op jit(solution)/shard_map/all_gather | solution.py:43
  1467.2 262.3 %all-gather.80.cloned.1.call-start = ((), (), s32[]{:S(2)}) async-start(), calls=%async_computation.84 | async-start | bytes 2621440 | tf_op jit(solution)/shard_map/all_gather | solution.py:43
  1516.0 264.5 %reduce-scatter.77.cloned.1.call-start = ((), (), s32[]{:S(2)}) async-start(), calls=%async_computation.76 | async-start | bytes 2621440 | tf_op jit(solution)/shard_map/reduce_scatter | solution.py:47
  1603.0 177.5 %reduce-scatter.65.cloned.1.call-start = ((), (), s32[]{:S(2)}) async-start(), calls=%async_computation.64 | async-start | bytes 2621440 | tf_op jit(solution)/shard_map/reduce_scatter | solution.py:47
  1661.8 118.8 %reduce-scatter.71.cloned.1.call-start = ((), (), s32[]{:S(2)}) async-start(), calls=%async_computation.70 | async-start | bytes 2621440 | tf_op jit(solution)/shard_map/reduce_scatter | solution.py:47
  1729.4 65.8 %reduce-scatter.87.cloned.1.call-start = ((), (), s32[]{:S(2)}) async-start(), calls=%async_computation.85 | async-start | bytes 2621440 | tf_op jit(solution)/shard_map/reduce_scatter | solution.py:47
  1745.2 83.9 %reduce-scatter.51.cloned.1.call-start = ((), (), s32[]{:S(2)}) async-start(), calls=%async_computation.50 | async-start | bytes 2621440 | tf_op jit(solution)/shard_map/reduce_scatter | solution.py:37
  1780.2 77.3 %all-gather.48.cloned.1.call-start = ((), (), s32[]{:S(2)}) async-start(), calls=%async_computation.51 | async-start | bytes 2621440 | tf_op jit(solution)/shard_map/all_gather | solution.py:33
  1834.8 86.4 %reduce-scatter.53.cloned.1.call-start = ((), (), s32[]{:S(2)}) async-start(), calls=%async_computation.52 | async-start | bytes 2621440 | tf_op jit(solution)/shard_map/reduce_scatter | solution.py:37
  1889.6 79.8 %all-gather.50.cloned.1.call-start = ((), (), s32[]{:S(2)}) async-start(), calls=%async_computation.53 | async-start | bytes 2621440 | tf_op jit(solution)/shard_map/all_gather | solution.py:33
  1925.1 58.9 %reduce-scatter.43.cloned.1.call-start = ((), (), s32[]{:S(2)}) async-start(), calls=%async_computation.42 | async-start | bytes 2621440 | tf_op jit(solution)/shard_map/reduce_scatter | solution.py:37
  1925.8 90.0 %reduce-scatter.49.cloned.1.call-start = ((), (), s32[]{:S(2)}) async-start(), calls=%async_computation.48 | async-start | bytes 2621440 | tf_op jit(solution)/shard_map/reduce_scatter | solution.py:37
  1926.4 143.6 %all-reduce.3.cloned.1.call-start = ((), (), s32[]{:S(2)}) async-start(), calls=%async_computation.91 | async-start | bytes 2097152
  1933.3 172.3 %reduce-scatter.95.cloned.1.call-start = ((), (), s32[]{:S(2)}) async-start(), calls=%async_computation.89 | async-start | bytes 1802240 | tf_op jit(solution)/shard_map/reduce_scatter | solution.py:481
  1942.8 221.0 %reduce-scatter.93.cloned.1.call-start = ((), (), s32[]{:S(2)}) async-start(), calls=%async_computation.88 | async-start | bytes 3604480 | tf_op jit(solution)/shard_map/reduce_scatter | solution.py:478
  1957.7 230.6 %reduce-scatter.91.cloned.1.call-start = ((), (), s32[]{:S(2)}) async-start(), calls=%async_computation.87 | async-start | bytes 655360 | tf_op jit(solution)/shard_map/reduce_scatter | solution.py:475
  1961.4 262.7 %reduce-scatter.89.cloned.1.call-start = ((), (), s32[]{:S(2)}) async-start(), calls=%async_computation.86 | async-start | bytes 1966080 | tf_op jit(solution)/shard_map/reduce_scatter | solution.py:472
  1968.0 314.7 %reduce-scatter.97.cloned.1.call-start = ((), (), s32[]{:S(2)}) async-start(), calls=%async_computation.90 | async-start | bytes 557056
  1969.3 346.4 %reduce-scatter.55.cloned.1.call-start = ((), (), s32[]{:S(2)}) async-start(), calls=%async_computation.54 | async-start | bytes 2621440 | tf_op jit(solution)/shard_map/reduce_scatter | solution.py:37
  (218 other events, 5001.4 us)
Sparse Core Ops, SparseCore 0:
  13.5 23.8 all-gather.39
  39.4 22.5 all-gather.31
  64.2 22.5 all-gather.27
  88.8 22.5 all-gather.45
  113.8 31.4 reduce-scatter.44
  147.9 31.3 reduce-scatter.38
  181.8 31.4 reduce-scatter.78
  215.9 31.3 reduce-scatter.34
  249.9 31.4 reduce-scatter.56
  288.1 22.5 all-gather.29
  313.5 37.3 reduce-scatter.36
  354.3 22.5 all-gather.35
  379.1 22.5 all-gather.33
  437.4 31.4 reduce-scatter.40
  472.2 22.5 all-gather.37
  496.9 22.5 all-gather.41
  564.9 31.3 reduce-scatter.46
  599.7 22.5 all-gather.43
  624.5 22.5 all-gather.53
  691.2 31.4 reduce-scatter.58
  724.9 22.5 all-gather.51
  749.7 22.5 all-gather.55
  795.9 31.3 reduce-scatter.60
  832.8 22.5 all-gather.57
  857.5 22.5 all-gather.61
  959.0 31.4 reduce-scatter.66
  994.6 22.5 all-gather.63
  1019.5 22.5 all-gather.67
  1127.2 31.3 reduce-scatter.72
  1162.8 22.5 all-gather.69
  1188.0 31.4 reduce-scatter.62
  1222.2 31.3 reduce-scatter.68
  1256.0 31.4 reduce-scatter.74
  1294.9 22.5 all-gather.73
  1320.2 37.5 reduce-scatter.80
  1361.3 22.5 all-gather.75
  1391.2 39.0 reduce-scatter.82
  1435.4 22.5 all-gather.77
  1465.1 46.7 reduce-scatter.84
  1514.0 22.5 all-gather.71
  1538.7 22.5 all-gather.59
  1563.5 22.5 all-gather.65
  1587.6 22.5 all-gather.79
  1612.7 31.4 reduce-scatter.76
  1661.9 31.6 reduce-scatter.64
  1729.5 31.6 reduce-scatter.70
  1763.8 31.4 reduce-scatter.86
  1797.6 31.4 reduce-scatter.50
  1834.9 22.5 all-gather.47
  1889.7 31.3 reduce-scatter.52
  1925.2 22.5 all-gather.49
  1950.4 31.4 reduce-scatter.42
  1984.3 31.3 reduce-scatter.48
  2018.2 51.8 all-reduce.2
  2073.0 32.6 reduce-scatter.94
  2108.7 55.0 reduce-scatter.92
  2166.7 21.4 reduce-scatter.90
  2190.5 33.5 reduce-scatter.88
  2227.9 54.7 reduce-scatter.96
  2285.3 30.4 reduce-scatter.54
where the time goes:
time: 2340 us; the launch traced here: 2330 us
  waiting for transfers between devices  1340 us (57%)
  matrix products  567 us (24%)
  other arithmetic  209 us (9%)
  local copies, waits for them, and re-layouts  103 us (4%)
  loops' own time  72.9 us (3%)
    reduce_scatter x15, waiting for transfers between devices, summed_rows(): lax.psum_scatter(branch_term.astype(jnp.bfloat16), 'mp', scatter_dimensio...  400 us
    reduce_scatter x12, waiting for transfers between devices, summed_grads(): lax.psum_scatter(branch_term.astype(jnp.bfloat16), 'mp', scatter_dimensio...  231 us
    all_gather x16, waiting for transfers between devices, gathered_normed(): return (normed, lax.all_gather(normed, 'mp', axis=0, tiled=True))  227 us
    all_gather x11, waiting for transfers between devices, gathered_grad(): lax.all_gather(gradient.astype(jnp.bfloat16), 'mp', axis=0, tiled=True)  130 us
    sub x16, matrix products, attend(): exponent = jnp.exp(scores - row_max)  116 us
    dot_general x28, matrix products, attend(): jnp.einsum('rhqk,krhd->qrhd', weights_low, value_heads, preferred_element...  113 us
    unnamed x62, waiting for transfers between devices  109 us
    ppermute x6, waiting for transfers between devices, from_behind(): return lax.ppermute(block, axis, route)  99.8 us
  transfers between devices with their start and end apart: 66, of which 50 were waited for; matrix products, arithmetic and copies ran while one was open for 25% of the time, Pallas kernels for 0%

commit v1 on v0

v1 whole, which is shorter than its diff:
```python
import functools
import math

import jax
import jax.numpy as jnp
from jax import lax
from jax.experimental import pallas as pl
from jax.experimental.pallas import tpu as pltpu
from jax.sharding import PartitionSpec as P

DK = 64
EPS = 1e-06
BIG = -1e30
SCALE = DK**-0.5
LOG_SCALE = SCALE * math.log2(math.e)
BF, F32 = jnp.bfloat16, jnp.float32

DOC_LANES = 3
OFFSET_LANE = 3
BLOCK_LANE = 8

MESH = pl.DeviceIdType.MESH

NT = (((1,), (1,)), ((), ()))
NN = (((1,), (0,)), ((), ()))
TN = (((0,), (0,)), ((), ()))


def dot(a, b, dims=NN):
    return lax.dot_general(a, b, dims, preferred_element_type=F32)


def norm_scale(tensor, gain):
    return tensor * lax.rsqrt(jnp.mean(tensor * tensor, axis=-1, keepdims=True) + EPS) * gain


def norm_back(tensor, gain, gradient):
    _, pull_back = jax.vjp(norm_scale, tensor, gain)
    return pull_back(gradient)


def split_three(column):
    high = column.astype(BF)
    rest = column - high.astype(F32)
    middle = rest.astype(BF)
    low = (rest - middle.astype(F32)).astype(BF)
    return high, middle, low


def with_offsets(base, column):
    lane = lax.broadcasted_iota(jnp.int32, base.shape, 1)
    out = base.astype(F32)
    for i, piece in enumerate(split_three(column)):
        out = jnp.where(lane == OFFSET_LANE + i, piece.astype(F32), out)
    return out.astype(BF)


def attn_fwd_kernel(size, *refs):
    q_ref, k_ref, v_ref, qa_ref, ka_ref = refs[:5]
    tri_ref = refs[5] if len(refs) == 8 else None
    mix_ref, aug_ref = refs[-2:]
    key_aug = ka_ref[...]
    for head in range(2):
        lanes = slice(head * DK, (head + 1) * DK)
        keys = jnp.concatenate([k_ref[:, lanes], key_aug], axis=1)
        values = jnp.concatenate([v_ref[:, lanes], key_aug], axis=1)
        for c in range(q_ref.shape[0] // size):
            rows = slice(c * size, (c + 1) * size)
            base = qa_ref[rows, :]
            query = jnp.concatenate([q_ref[rows, lanes], base], axis=1)
            scores = []
            for j in range(k_ref.shape[0] // size):
                s = dot(query, keys[j * size : (j + 1) * size], NT)
                scores.append(s + tri_ref[...] if tri_ref is not None and j == c else s)
            top = functools.reduce(jnp.maximum, scores)
            top = jnp.max(top, axis=1, keepdims=True)
            total = None
            for j, s in enumerate(scores):
                p = jnp.exp2((s - top) * LOG_SCALE).astype(BF)
                o = dot(p, values[j * size : (j + 1) * size])
                total = o if total is None else total + o
            weight = total[:, DK + OFFSET_LANE : DK + OFFSET_LANE + 1]
            mix_ref[rows, lanes] = (total[:, :DK] / weight).astype(BF)
            log_raw = top + jnp.log2(weight) * (1.0 / LOG_SCALE)
            aug_ref[rows, lanes] = with_offsets(base, -log_raw)


def attn_bwd_kernel(size, places, hid, *refs):
    q_ref, k_ref, v_ref, do_ref, mix_ref, aug_ref, ka_ref = refs[:7]
    out_refs = [refs[at - len(places_used(places))] for at, _ in places]
    tri_ref = refs[7] if len(refs) == 8 + len(places_used(places)) else None
    length = k_ref.shape[0]
    key_aug = ka_ref[...]
    at_lane = pl.program_id(0) * (2 * DK)
    grads_q, grads_k, grads_v = [], [], []
    for head in range(2):
        lanes = slice(head * DK, (head + 1) * DK)
        key = k_ref[:, lanes]
        keys = jnp.concatenate([key, key_aug], axis=1)
        values = jnp.concatenate([v_ref[:, lanes], key_aug], axis=1)
        grad_k = jnp.zeros((length, DK), F32)
        grad_v = jnp.zeros((length, DK), F32)
        pieces_q = []
        for c in range(q_ref.shape[0] // size):
            rows = slice(c * size, (c + 1) * size)
            query = q_ref[rows, lanes]
            grad = do_ref[rows, lanes]
            delta = jnp.sum(
                grad.astype(F32) * mix_ref[rows, lanes].astype(F32), axis=1, keepdims=True
            )
            queries = jnp.concatenate([query, aug_ref[rows, lanes]], axis=1)
            grads = jnp.concatenate(
                [grad, with_offsets(jnp.zeros((size, DK), BF), -delta)], axis=1
            )
            weights, slopes = [], []
            for j in range(length // size):
                block = slice(j * size, (j + 1) * size)
                s = dot(keys[block], queries, NT)
                if tri_ref is not None and j == c:
                    s = s + tri_ref[...]
                p = jnp.exp2(s * LOG_SCALE)
                slope = p * dot(values[block], grads, NT)
                weights.append(p.astype(BF))
                slopes.append(slope.astype(BF))
            weights = jnp.concatenate(weights, axis=0)
            slopes = jnp.concatenate(slopes, axis=0)
            grad_v = grad_v + dot(weights, grad)
            grad_k = grad_k + dot(slopes, query)
            pieces_q.append((dot(slopes, key, TN) * SCALE).astype(BF))
        grads_q.append(jnp.concatenate(pieces_q, axis=0))
        grads_k.append((grad_k * SCALE).astype(BF))
        grads_v.append(grad_v.astype(BF))
    for ref, (_, lane), halves in zip(out_refs, places, (grads_q, grads_k, grads_v)):
        where = pl.ds(pl.multiple_of(at_lane + lane * hid, 2 * DK), 2 * DK)
        ref[:, where] = jnp.concatenate(halves, axis=1)


def places_used(places):
    return sorted({at for at, _ in places})


def lane_spec(length, first):
    return pl.BlockSpec((length, 2 * DK), lambda i: (0, first + i))


def whole_spec(shape):
    return pl.BlockSpec(shape, lambda i: (0,) * len(shape))


def attn_forward(size, pairs, q, k, v, query_aug, key_aug, tri=None):
    (q, q_at), (k, k_at), (v, v_at) = q, k, v
    rows, length = q.shape[0], k.shape[0]
    out = jax.ShapeDtypeStruct((rows, pairs * 2 * DK), BF)
    extra = [] if tri is None else [tri]
    return pl.pallas_call(
        functools.partial(attn_fwd_kernel, size),
        grid=(pairs,),
        in_specs=[
            lane_spec(rows, q_at),
            lane_spec(length, k_at),
            lane_spec(length, v_at),
            *(whole_spec(a.shape) for a in (query_aug, key_aug, *extra)),
        ],
        out_specs=[lane_spec(rows, 0)] * 2,
        out_shape=[out, out],
        compiler_params=pltpu.CompilerParams(vmem_limit_bytes=48 * 1024 * 1024),
        cost_estimate=pl.CostEstimate(
            flops=pairs * 2 * rows * length * DK * 4 * 4,
            bytes_accessed=pairs * length * 2 * DK * 2 * 5,
            transcendentals=pairs * 2 * rows * length,
        ),
        name="attn_fwd",
    )(q, k, v, query_aug, key_aug, *extra)


def attn_backward(size, pairs, q, k, v, grad, mix, aug, key_aug, tri=None, joined=False):
    (q, q_at), (k, k_at), (v, v_at) = q, k, v
    rows, length = q.shape[0], k.shape[0]
    hid = pairs * 2 * DK
    extra = [] if tri is None else [tri]
    if joined:
        places = ((0, 0), (0, 1), (0, 2))
        shapes = [(length, 3 * hid)]
    else:
        places = ((0, 0), (1, 0), (1, 1))
        shapes = [(rows, hid), (length, 2 * hid)]
    return pl.pallas_call(
        functools.partial(attn_bwd_kernel, size, places, hid),
        grid=(pairs,),
        in_specs=[
            lane_spec(rows, q_at),
            lane_spec(length, k_at),
            lane_spec(length, v_at),
            lane_spec(rows, 0),
            lane_spec(rows, 0),
            lane_spec(rows, 0),
            *(whole_spec(a.shape) for a in (key_aug, *extra)),
        ],
        out_specs=[whole_spec(shape) for shape in shapes],
        out_shape=[jax.ShapeDtypeStruct(shape, BF) for shape in shapes],
        compiler_params=pltpu.CompilerParams(vmem_limit_bytes=48 * 1024 * 1024),
        cost_estimate=pl.CostEstimate(
            flops=pairs * 2 * rows * length * DK * 10 * 4,
            bytes_accessed=pairs * length * 2 * DK * 2 * 9,
            transcendentals=pairs * 2 * rows * length,
        ),
        name="attn_bwd",
    )(q, k, v, grad, mix, aug, key_aug, *extra)


def low_bit(j):
    return j & -j


def flipped(index, bit):
    return index + bit - 2 * bit * lax.rem(index // bit, 2)


class Links:
    def __init__(self, n, own, got, out, back, sems):
        self.n, self.own, self.got, self.out, self.back = n, own, got, out, back
        self.gather_send, self.gather_recv, self.sum_send, self.sum_recv = sems
        self.idx = lax.axis_index("mp")
        self.slots = range(1, n)
        self.parents = sorted({j ^ low_bit(j) for j in self.slots} - {0}, key=int.bit_count)

    def greet(self):
        barrier = pltpu.get_barrier_semaphore()
        bits = [j for j in self.slots if j == low_bit(j)]
        for bit in bits:
            pl.semaphore_signal(
                barrier, inc=1, device_id={"mp": flipped(self.idx, bit)}, device_id_type=MESH
            )
        pl.semaphore_wait(barrier, len(bits))

    def block(self, r, j):
        return self.own.at[r] if j == 0 else self.got.at[r, j - 1]

    def gather_copy(self, r, j):
        return pltpu.make_async_remote_copy(
            src_ref=self.block(r, j ^ low_bit(j)),
            dst_ref=self.got.at[r, j - 1],
            send_sem=self.gather_send.at[r, j - 1],
            recv_sem=self.gather_recv.at[r, j - 1],
            device_id={"mp": flipped(self.idx, low_bit(j))},
            device_id_type=MESH,
        )

    def sum_copy(self, r, j):
        return pltpu.make_async_remote_copy(
            src_ref=self.out.at[r, j - 1],
            dst_ref=self.back.at[r, j - 1],
            send_sem=self.sum_send.at[r, j - 1],
            recv_sem=self.sum_recv.at[r, j - 1],
            device_id={"mp": flipped(self.idx, low_bit(j))},
            device_id_type=MESH,
        )

    def start_gather(self, r):
        for j in sorted(self.slots, reverse=True):
            if j == low_bit(j):
                self.gather_copy(r, j).start()

    def forward_gather(self, r):
        for parent in self.parents:
            self.gather_copy(r, parent).wait_recv()
            for j in self.slots:
                if j ^ low_bit(j) == parent:
                    self.gather_copy(r, j).start()

    def finish_gather(self, r):
        for j in self.slots:
            if j not in self.parents:
                self.gather_copy(r, j).wait_recv()

    def terms(self, j):
        limit = low_bit(j) if j else self.n
        return [j | 1 << b for b in range(self.n.bit_length()) if 1 << b < limit]

    def start_sum(self, r):
        for j in self.slots:
            if low_bit(j) == 1:
                self.sum_copy(r, j).start()

    def forward_sum(self, r):
        for j in sorted(self.slots, key=low_bit):
            if low_bit(j) == 1:
                continue
            total = self.out[r, j - 1].astype(F32)
            for k in self.terms(j):
                self.sum_copy(r, k).wait_recv()
                total = total + self.back[r, k - 1].astype(F32)
            self.out[r, j - 1] = total.astype(BF)
            self.sum_copy(r, j).start()

    def finish_sum(self, r, own):
        for k in self.terms(0):
            self.sum_copy(r, k).wait_recv()
            own = own + self.back[r, k - 1].astype(F32)
        return own

    def drain(self, rows):
        @pl.loop(0, rows)
        def _(r):
            for j in self.slots:
                self.gather_copy(r, j).wait_send()
                self.sum_copy(r, j).wait_send()


def attend_into(size, length, hid, qkv, query_aug, key_aug, tri, mix, aug):
    keys_aug = key_aug[...]
    blocks = length // size
    for head in range(hid // DK):
        lanes = slice(head * DK, (head + 1) * DK)
        k_lanes = slice(hid + head * DK, hid + (head + 1) * DK)
        v_lanes = slice(2 * hid + head * DK, 2 * hid + (head + 1) * DK)
        keys = jnp.concatenate([qkv[:, k_lanes], keys_aug], axis=1)
        values = jnp.concatenate([qkv[:, v_lanes], keys_aug], axis=1)
        for c in range(blocks):
            rows = slice(c * size, (c + 1) * size)
            base = query_aug[rows, :]
            query = jnp.concatenate([qkv[rows, lanes], base], axis=1)
            scores = []
            for j in range(blocks):
                s = dot(query, keys[j * size : (j + 1) * size], NT)
                scores.append(s + tri[...] if j == c else s)
            top = functools.reduce(jnp.maximum, scores)
            top = jnp.max(top, axis=1, keepdims=True)
            total = None
            for j, s in enumerate(scores):
                p = jnp.exp2((s - top) * LOG_SCALE).astype(BF)
                o = dot(p, values[j * size : (j + 1) * size])
                total = o if total is None else total + o
            weight = total[:, DK + OFFSET_LANE : DK + OFFSET_LANE + 1]
            mix[rows, lanes] = (total[:, :DK] / weight).astype(BF)
            log_raw = top + jnp.log2(weight) * (1.0 / LOG_SCALE)
            aug[rows, lanes] = with_offsets(base, -log_raw)


def self_stage_kernel(
    n,
    x,
    w_qkv,
    w_out,
    query_aug,
    key_aug,
    tri,
    total,
    full_out,
    qkv_out,
    mix_out,
    aug_out,
    got,
    out,
    back,
    qkv,
    mix,
    aug,
    *sems,
):
    rows, size = x.shape[:2]
    length, hid = n * size, w_out.shape[0]
    save = sems[-1]
    links = Links(n, x, got, out, back, sems[:4])
    links.greet()

    def saves(r, which):
        for i in which:
            if i < n:
                pair = (links.block(r, i), full_out.at[r, pl.ds(i * size, size)])
            else:
                ref, dst = ((qkv, qkv_out), (mix, mix_out), (aug, aug_out))[i - n]
                pair = (ref.at[r], dst.at[r])
            yield pltpu.make_async_copy(*pair, save.at[r, i])

    for r in range(rows):
        links.start_gather(r)
    links.forward_gather(0)

    @pl.loop(0, rows)
    def _(r):
        links.finish_gather(r)
        for j in range(n):
            qkv[r, j * size : (j + 1) * size, :] = dot(links.block(r, j)[...], w_qkv[...]).astype(
                BF
            )
        for copy in saves(r, range(n + 1)):
            copy.start()

        @pl.when(r > 0)
        def _():
            links.forward_sum(r - 1)

        attend_into(
            size,
            length,
            hid,
            qkv.at[r],
            query_aug.at[r],
            key_aug.at[r],
            tri,
            mix.at[r],
            aug.at[r],
        )
        for copy in saves(r, range(n + 1, n + 3)):
            copy.start()

        @pl.when(r + 1 < rows)
        def _():
            links.forward_gather(r + 1)

        for j in reversed(range(n)):
            part = dot(mix[r, j * size : (j + 1) * size, :], w_out[...])
            if j:
                out[r, j - 1] = part.astype(BF)
                if low_bit(j) == 1:
                    links.sum_copy(r, j).start()
            else:
                total[r] = part

        @pl.when(r > 0)
        def _():
            total[r - 1] = links.finish_sum(r - 1, total[r - 1])

    links.forward_sum(rows - 1)
    total[rows - 1] = links.finish_sum(rows - 1, total[rows - 1])
    links.drain(rows)

    @pl.loop(0, rows)
    def _(r):
        for copy in saves(r, range(n + 3)):
            copy.wait()


def self_stage(n, x, w_qkv, w_out, query_aug, key_aug, tri):
    rows, size, width = x.shape
    length, hid = n * size, w_out.shape[0]
    vmem = pl.BlockSpec(memory_space=pltpu.VMEM)
    hbm = pl.BlockSpec(memory_space=pl.ANY)
    slots = (rows, n - 1)
    return pl.pallas_call(
        functools.partial(self_stage_kernel, n),
        in_specs=[vmem] * 6,
        out_specs=[vmem] + [hbm] * 4,
        out_shape=[
            jax.ShapeDtypeStruct((rows, size, width), F32),
            jax.ShapeDtypeStruct((rows, length, width), BF),
            jax.ShapeDtypeStruct((rows, length, 3 * hid), BF),
            jax.ShapeDtypeStruct((rows, length, hid), BF),
            jax.ShapeDtypeStruct((rows, length, hid), BF),
        ],
        scratch_shapes=[
            pltpu.VMEM((*slots, size, width), BF),
            pltpu.VMEM((*slots, size, width), BF),
            pltpu.VMEM((*slots, size, width), BF),
            pltpu.VMEM((rows, length, 3 * hid), BF),
            pltpu.VMEM((rows, length, hid), BF),
            pltpu.VMEM((rows, length, hid), BF),
            *[pltpu.SemaphoreType.DMA(slots)] * 4,
            pltpu.SemaphoreType.DMA((rows, n + 3)),
        ],
        compiler_params=pltpu.CompilerParams(
            collective_id=1, has_side_effects=True, vmem_limit_bytes=56 * 1024 * 1024
        ),
        cost_estimate=pl.CostEstimate(
            flops=rows * length * width * hid * 8 + rows * length * length * hid * 16,
            bytes_accessed=rows * length * width * 16,
            transcendentals=rows * length * length * hid // DK,
        ),
        name="self_stage",
    )(x, w_qkv, w_out, query_aug, key_aug, tri)


def gelu(gate):
    return jax.nn.gelu(gate, approximate=True)


def body(
    block_input, cotangent, segments, attn_weight, attn_out, ffn_in, ffn_out, cross_weight, gains
):
    enc = lax.axis_index("section") == 0
    idx = lax.axis_index("mp")
    n = lax.axis_size("mp")
    dp_size = lax.axis_size("dp")
    bits = [1 << b for b in range(n.bit_length() - 1)]
    inner, outer = bits[:1], bits[1:]
    size, row_count, width = block_input.shape[1:]
    length = size * n
    hid = attn_weight.shape[3]
    ffd = ffn_in.shape[3]
    pairs = hid // (2 * DK)
    rows = range(row_count)

    def across(tensor, bit):
        return lax.ppermute(tensor, "mp", [(i, i ^ bit) for i in range(n)])

    def spread(tensor, over):
        have = {0: tensor}
        for bit in reversed(over):
            for j in list(have):
                have[j ^ bit] = across(have[j], bit)
        return [have[j] for j in sorted(have)]

    def gather(tensor, over):
        return jnp.concatenate(spread(tensor, over), axis=0)

    def collect(have, over):
        have = dict(have)
        for bit in over:
            for j in sorted((j for j in have if j & bit), reverse=True):
                came = across(have.pop(j), bit)
                total = have[j ^ bit].astype(F32) + came.astype(F32)
                have[j ^ bit] = total if len(have) == 1 else total.astype(BF)
        return have[0].astype(F32)

    def scatter_sum(parts):
        return collect(enumerate(parts), bits)

    def pair_sum(out):
        return out[:size] + across(out[size:].astype(BF), 1).astype(F32)

    def pieces(a, b, dims=NN):
        return tuple(dot(a[j * size : (j + 1) * size], b, dims).astype(BF) for j in range(n))

    def total_of(terms):
        terms = list(terms)
        return functools.reduce(jnp.add, terms)

    def on(side, fn):
        shapes = jax.eval_shape(fn)
        blank = lambda: jax.tree.map(lambda o: jnp.zeros(o.shape, o.dtype), shapes)
        return lax.cond(enc, *((fn, blank) if side == "enc" else (blank, fn)))

    w_qkv = attn_weight[0].reshape(width, 3 * hid)
    w_out = attn_out[0]
    gain = gains[0]
    rows_bf = [block_input[0, :, r] for r in rows]
    rows_in = [v.astype(F32) for v in rows_bf]
    rows_cot = [cotangent[0, :, r] for r in rows]

    order = jnp.arange(n, dtype=jnp.int32) ^ idx
    block_of = jnp.repeat(order, size)
    lane = jnp.arange(DK, dtype=jnp.int32)[None]

    def local_order(seg):
        return jnp.take(seg.reshape(n, size), order, axis=0).reshape(length)

    def query_features(seg, causal):
        doc = (lane < DOC_LANES) & (lane != seg[:, None])
        later = (lane >= BLOCK_LANE) & (lane < BLOCK_LANE + n)
        later = later & (lane - BLOCK_LANE > block_of[: seg.shape[0], None]) & causal
        return jnp.where(doc | later, BIG, 0.0).astype(BF)

    def key_features(seg):
        doc = (lane < DOC_LANES) & (lane == seg[:, None])
        ones = (lane >= OFFSET_LANE) & (lane < OFFSET_LANE + 3)
        place = lane - BLOCK_LANE == block_of[:, None]
        return jnp.where(doc | ones | place, 1.0, 0.0).astype(BF)

    above = jnp.arange(size)[None, :] > jnp.arange(size)[:, None]
    tri = jnp.where(above & ~enc, BIG, 0.0).astype(F32)
    feats = []
    for r in rows:
        seg_enc, seg_dec = local_order(segments[0, r]), local_order(segments[1, r])
        own = jnp.where(enc, seg_enc, seg_dec)
        feats.append(
            (
                query_features(own, ~enc),
                key_features(own),
                query_features(seg_dec[: 2 * size], False),
                key_features(seg_enc),
            )
        )

    normed1 = jnp.stack([norm_scale(v, gain[0]).astype(BF) for v in rows_in])
    total1, full1, qkv1, mix1, aug1 = self_stage(
        n,
        normed1,
        w_qkv,
        w_out,
        jnp.stack([f[0] for f in feats]),
        jnp.stack([f[1] for f in feats]),
        tri,
    )
    saved1 = [(qkv1[r], mix1[r], aug1[r]) for r in rows]
    mid1 = [rows_in[r] + total1[r] for r in rows]

    w_in = spread(ffn_in[0].reshape(width, 2 * ffd), outer)
    w_down = spread(ffn_out[0], outer)
    w_cross = spread(cross_weight[0].reshape(width, 2 * hid), outer)
    w_kv = [lax.ppermute(w, "section", [(0, 1)]) for w in w_cross]
    w_q = [w[:, :hid] for w in w_cross]
    w_o = [w[:, hid:] for w in w_cross]
    parts = range(len(w_in))

    def gate_up_of(full):
        return [dot(full, w) for w in w_in]

    def ffn_out_of(gate_up):
        hidden = [(gelu(g[:, :ffd]) * g[:, ffd:]).astype(BF) for g in gate_up]
        return total_of(dot(h, w) for h, w in zip(hidden, w_down))

    def ffn_back(grad_full, gate_up):
        kept, grad_normed = [], []
        for b in parts:
            gate, up = gate_up[b][:, :ffd].astype(F32), gate_up[b][:, ffd:].astype(F32)
            activated, pull = jax.vjp(gelu, gate)
            hidden = (activated * up).astype(BF)
            grad_hidden = dot(grad_full, w_down[b], NT)
            grad_gate = pull(grad_hidden * up)[0].astype(BF)
            grad_up = (grad_hidden * activated).astype(BF)
            grad_pair = jnp.concatenate([grad_gate, grad_up], axis=1)
            grad_normed.append(dot(grad_pair, w_in[b], NT))
            kept.append((hidden, grad_pair))
        return total_of(grad_normed), kept

    def cross_fwd(full, mem, r):
        outs, saved = [], []
        for b in parts:
            q = dot(full, w_q[b]).astype(BF)
            kv = dot(mem, w_kv[b]).astype(BF)
            mix, aug = attn_forward(
                size, pairs, (q, 0), (kv, 0), (kv, pairs), feats[r][2], feats[r][3]
            )
            outs.append(dot(mix, w_o[b], NT))
            saved.append((q, kv, mix, aug))
        return total_of(outs), saved

    def cross_back(grad_full, saved, r):
        kept, grad_normed, grad_mem = [], [], []
        for b in parts:
            q, kv, mix, aug = saved[b]
            grad_mix = dot(grad_full, w_o[b]).astype(BF)
            dq, dkv = attn_backward(
                size, pairs, (q, 0), (kv, 0), (kv, pairs), grad_mix, mix, aug, feats[r][3]
            )
            grad_normed.append(dot(dq, w_q[b], NT))
            grad_mem.append(dot(dkv, w_kv[b], NT))
            kept.append((dq, dkv))
        grad_mem = total_of(grad_mem).astype(BF)
        return total_of(grad_normed), tuple(
            grad_mem[j * size : (j + 1) * size] for j in range(n)
        ), kept

    full2, gate_up2, mid2_e, memory, mem_full = [], [], [], [], []
    for r in rows:
        full2.append(gather(norm_scale(mid1[r], gain[1]).astype(BF), inner))

        def enc_ffn(r=r):
            gate_up = gate_up_of(full2[r])
            return ffn_out_of(gate_up), [g.astype(BF) for g in gate_up]

        out, gate_up = on("enc", enc_ffn)
        gate_up2.append(gate_up)
        mid2_e.append(mid1[r] + pair_sum(out))
        memory.append(norm_scale(mid2_e[r], gain[2]).astype(BF))
        mem_full.append(gather(lax.ppermute(memory[r], "section", [(0, 1)]), bits))

    saved_x, mid2_d, full3, dec_out, kept3, grad_mid2_d = [], [], [], [], [], []
    grad_full3, grad_full2_d, kept_x, grad_mid1_d, grad_memory = [], [], [], [], []
    gain_sums = [[], [], []]
    for r in rows:
        out, saved = on("dec", lambda r=r: cross_fwd(full2[r], mem_full[r], r))
        saved_x.append(saved)
        mid2_d.append(mid1[r] + pair_sum(out))
    for r in rows:
        full3.append(gather(norm_scale(mid2_d[r], gain[2]).astype(BF), inner))
        grad_full3.append(gather(rows_cot[r], inner))

        def dec_ffn(r=r):
            gate_up = gate_up_of(full3[r])
            grad_normed, kept = ffn_back(grad_full3[r], gate_up)
            return ffn_out_of(gate_up), grad_normed, kept

        out, grad_normed, kept = on("dec", dec_ffn)
        kept3.append(kept)
        dec_out.append((mid2_d[r] + pair_sum(out)).astype(BF))
        part, gain_grad = norm_back(mid2_d[r], gain[2], pair_sum(grad_normed))
        gain_sums[2].append(jnp.where(enc, 0.0, gain_grad))
        grad_mid2_d.append(rows_cot[r].astype(F32) + part)
    for r in rows:
        grad_full2_d.append(gather(grad_mid2_d[r].astype(BF), inner))
        grad_normed, grad_mem, kept = on(
            "dec", lambda r=r: cross_back(grad_full2_d[r], saved_x[r], r)
        )
        kept_x.append(kept)
        arrived = lax.ppermute(scatter_sum(grad_mem).astype(BF), "section", [(1, 0)])
        grad_memory.append(arrived.astype(F32))
        part, gain_grad = norm_back(mid1[r], gain[1], pair_sum(grad_normed))
        gain_sums[1].append(jnp.where(enc, 0.0, gain_grad))
        grad_mid1_d.append(grad_mid2_d[r] + part)

    kept2, grad_full2_e, grad_mid1 = [], [], []
    for r in rows:
        part, gain_grad = norm_back(
            mid2_e[r], gain[2], rows_cot[r].astype(F32) + grad_memory[r]
        )
        gain_sums[2].append(jnp.where(enc, gain_grad, 0.0))
        grad_mid2 = part
        grad_full2_e.append(gather(grad_mid2.astype(BF), inner))
        grad_normed, kept = on("enc", lambda r=r: ffn_back(grad_full2_e[r], gate_up2[r]))
        kept2.append(kept)
        part, gain_grad = norm_back(mid1[r], gain[1], pair_sum(grad_normed))
        gain_sums[1].append(jnp.where(enc, gain_grad, 0.0))
        grad_mid1.append(jnp.where(enc, grad_mid2 + part, grad_mid1_d[r]))

    grad_full1, grad_qkv, input_grad = [], [], []
    for r in rows:
        qkv, mix, aug = saved1[r]
        grad_full1.append(gather(grad_mid1[r].astype(BF), bits))
        grad_mix = dot(grad_full1[r], w_out, NT).astype(BF)
        (dqkv,) = attn_backward(
            size,
            pairs,
            (qkv, 0),
            (qkv, pairs),
            (qkv, 2 * pairs),
            grad_mix,
            mix,
            aug,
            feats[r][1],
            tri.T,
            joined=True,
        )
        grad_qkv.append(dqkv)
        part, gain_grad = norm_back(
            rows_in[r], gain[0], scatter_sum(pieces(dqkv, w_qkv, NT))
        )
        gain_sums[0].append(gain_grad)
        input_grad.append(grad_mid1[r] + part)

    def contract(lefts, rights):
        return total_of(dot(a, b, TN) for a, b in zip(lefts, rights)).astype(BF)

    def ffn_weights(full, kept, grad_full):
        return (
            [contract(full, [kept[r][b][1] for r in rows]) for b in parts],
            [contract([kept[r][b][0] for r in rows], grad_full) for b in parts],
        )

    def cross_weights():
        q = [contract(full2, [kept_x[r][b][0] for r in rows]) for b in parts]
        o = [contract(grad_full2_d, [saved_x[r][b][2] for r in rows]) for b in parts]
        kv = [contract(mem_full, [kept_x[r][b][1] for r in rows]) for b in parts]
        return [jnp.concatenate(qo, axis=1) for qo in zip(q, o)], kv

    def over_outer(blocks):
        step = 2
        return collect({step * b: t for b, t in enumerate(blocks)}, outer).astype(BF)

    def over_rows(total, dim):
        return lax.psum_scatter(total, "dp", scatter_dimension=dim, tiled=True).astype(F32)

    sum_in, sum_down = lax.cond(
        enc,
        lambda: ffn_weights(full2, kept2, grad_full2_e),
        lambda: ffn_weights(full3, kept3, grad_full3),
    )
    sum_qo, sum_kv = on("dec", cross_weights)
    sum_qkv = contract([full1[r] for r in rows], grad_qkv)
    sum_out = contract([s[1] for s in saved1], grad_full1)

    quarter = width // dp_size
    out_in = over_rows(over_outer(sum_in), 0).reshape(quarter, 2, ffd)
    out_down = over_rows(over_outer(sum_down), 1)
    sum_kv = lax.ppermute(over_outer(sum_kv), "section", [(1, 0)])
    sum_cross = jnp.where(enc, sum_kv, over_outer(sum_qo))
    out_cross = over_rows(sum_cross, 0).reshape(quarter, 2, hid)
    out_qkv = over_rows(sum_qkv, 0).reshape(quarter, 3, hid)
    out_out = over_rows(sum_out, 1)
    gain_total = lax.psum_scatter(
        jnp.stack([total_of(items) for items in gain_sums]),
        ("dp", "mp"),
        scatter_dimension=1,
        tiled=True,
    )
    block_out = jnp.stack([jnp.where(enc, memory[r], dec_out[r]) for r in rows], axis=1)
    return (
        block_out[None],
        jnp.stack(input_grad, axis=1)[None],
        out_qkv[None],
        out_out[None],
        out_in[None],
        out_down[None],
        out_cross[None],
        gain_total[None],
    )


def solution(mesh):
    in_specs = (
        P("section", "mp", "dp", None),
        P("section", "mp", "dp", None),
        P(None, "dp", None),
        P("section", None, None, "mp"),
        P("section", "mp", None),
        P("section", None, None, "mp"),
        P("section", "mp", None),
        P("section", None, None, "mp"),
        P("section", None, None),
    )
    out_specs = (
        P("section", "mp", "dp", None),
        P("section", "mp", "dp", None),
        P("section", "dp", None, "mp"),
        P("section", "mp", "dp"),
        P("section", "dp", None, "mp"),
        P("section", "mp", "dp"),
        P("section", "dp", None, "mp"),
        P("section", None, ("dp", "mp")),
    )
    return jax.shard_map(body, mesh=mesh, in_specs=in_specs, out_specs=out_specs, check_vma=False)
```

time: 2340 us -> 1160 us (0.50)
  waiting for transfers between devices: 1340 us -> 295 us
  matrix products: 567 us -> 223 us
  Pallas kernels: 0 us -> 265 us
  starting transfers between devices: 13.1 us -> 85.2 us
  other arithmetic: 209 us -> 139 us
  loops' own time: 72.9 us -> 13.9 us
    reduce_scatter x31 -> x5, waiting for transfers between devices: 777 us -> 93.1 us  [over_rows(): lax.psum_scatter(total, 'dp', scatter_dimension=dim, tiled=True).astype(F32)]
    all_gather x27 -> x0, waiting for transfers between devices: 357 us -> none  [the longest x16 227 us: gathered_normed(): return (normed, lax.all_gather(normed, 'mp', axis=0, tiled=True))]
    pallas_call x0 -> x16, Pallas kernels: none -> 265 us  [the longest x1 150 us: self_stage(): pl.pallas_call(functools.partial(self_stage_kernel, n), in_specs=[vmem] *...]
    dot_general x155 -> x111, matrix products: 451 us -> 223 us  [dot(): return lax.dot_general(a, b, dims, preferred_element_type=F32)]
    sub x16 -> x0, matrix products: 116 us -> none  [attend(): exponent = jnp.exp(scores - row_max)]
    unnamed x62 -> x7, waiting for transfers between devices: 109 us -> 0.1 us
    ppermute x6 -> x85, waiting for transfers between devices: 99.8 us -> 202 us  [the longest x76 137 us: across(): return lax.ppermute(tensor, 'mp', [(i, i ^ bit) for i in range(n)])]
    ppermute x6 -> x85, starting transfers between devices: 10.1 us -> 84.8 us  [the longest x1 37.6 us: body(): sum_kv = lax.ppermute(over_outer(sum_kv), 'section', [(1, 0)])]
  transfers between devices with their start and end apart: 66 -> 91, of which waited for: 50 -> 20; matrix products, arithmetic and copies ran while one was open for 25% -> 36% of each run, Pallas kernels for 0% -> 23%
where the time goes in v1:
time: 1160 us; the launch traced here: 1150 us
  waiting for transfers between devices  295 us (25%)
  Pallas kernels  265 us (23%)
  matrix products  223 us (19%)
  other arithmetic  139 us (12%)
  local copies, waits for them, and re-layouts  111 us (10%)
  starting transfers between devices  85.2 us (7%)
  between operations  18.6 us (2%)
  loops' own time  13.9 us (1%)
    dot_general x111, matrix products, dot(): return lax.dot_general(a, b, dims, preferred_element_type=F32)  223 us
    pallas_call x1, Pallas kernels, self_stage(): pl.pallas_call(functools.partial(self_stage_kernel, n), in_specs=[vmem] *...  150 us
    ppermute x76, waiting for transfers between devices, across(): return lax.ppermute(tensor, 'mp', [(i, i ^ bit) for i in range(n)])  137 us
    reduce_scatter x5, waiting for transfers between devices, over_rows(): lax.psum_scatter(total, 'dp', scatter_dimension=dim, tiled=True).astype(F32)  93.1 us
    pallas_call x9, Pallas kernels, attn_backward(): pl.pallas_call(functools.partial(attn_bwd_kernel, size, places, hid), gri...  83.6 us
    ppermute x3, waiting for transfers between devices, body(): mem_full.append(gather(lax.ppermute(memory[r], 'section', [(0, 1)]), bits))  54.4 us
    unnamed x621, local copies, waits for them, and re-layouts  43.1 us
    ppermute x1, starting transfers between devices, body(): sum_kv = lax.ppermute(over_outer(sum_kv), 'section', [(1, 0)])  37.6 us
  transfers between devices with their start and end apart: 91, of which 20 were waited for; matrix products, arithmetic and copies ran while one was open for 36% of the time, Pallas kernels for 23%

profile of v1, /device:TPU:2, one launch (start us, length us, event | category | flops | bytes accessed | tf_op | source)
XLA Modules:
  0.0 1149.5 jit_solution(14743490547481690000)
XLA Ops:
  26.6 150.2 %self_stage.1 = (f32[3,256,1024]{2,1,0:T(8,128)}, bf16[3,1024,1024]{2,1,0:T(8,128)(2,1)}, bf16[3,1024,768]{2,1,0:T(8,128)(2,1)}, bf16[3,1024,256]{2,1,0:T(8,128)(2,1)}, bf16[3,1024,256]{2,1,0:T(8,128)(2,1)}) custom-call(bf16[3,256,1024]{2,1,0:T(8,128)(2,1)} %pad_maximum_fusion.16.x, bf16[1024,768]{1,0:T(8,128)(2,1)} %copy.127.w_qkv, ...), custom_call_target="tpu_custom_call" | custom-call | flops 19327352832 | bytes 50331648 | tf_op jit(solution)/shard_map/self_stage/pallas_call | solution.py:441
  205.9 29.7 %collective-permute-done.4 = bf16[256,1024]{1,0:T(8,128)(2,1)} collective-permute-done((bf16[256,1024]{1,0:T(8,128)(2,1)S(1)}, bf16[256,1024]{1,0:T(8,128)(2,1)}, u32[]{:S(2)}, u32[]{:S(2)}) %collective-permute-start.4) | collective-permute-done | bytes 524320 | tf_op jit(solution)/shard_map/ppermute | solution.py:657
  237.1 9.3 collective-permute-done.17
  254.2 6.2 collective-permute-done.19
  265.6 10.6 collective-permute-done.10
  276.2 20.8 %conditional.29 = (f32[512,1024]{1,0:T(8,128)S(1)}, bf16[512,256]{1,0:T(8,128)(2,1)S(1)}, bf16[1024,512]{1,0:T(8,128)(2,1)S(1)}, bf16[512,256]{1,0:T(8,128)(2,1)...) conditional(s32[]{:T(128)} %convert_element_type.905, ...), branch_computations={%region_16.18_spmd, %region_17.19_spmd} | conditional | flops 7518027776 | bytes 25165896 | solution.py:532
  285.8 5.1 attn_fwd.9
  290.9 5.1 attn_fwd.8
  313.4 18.3 %conditional.26 = (f32[512,1024]{1,0:T(8,128)S(1)}, bf16[512,256]{1,0:T(8,128)(2,1)S(1)}, bf16[1024,512]{1,0:T(8,128)(2,1)S(1)}, bf16[512,256]{1,0:T(8,128)(2,1)...) conditional(s32[]{:T(128)} %convert_element_type.905, ...), branch_computations={%region_7.9_spmd, %region_8.10_spmd} | conditional | flops 7518027776 | bytes 25165896 | solution.py:532
  320.6 5.1 attn_fwd.7
  325.7 5.1 attn_fwd.6
  341.4 19.6 %conditional.30 = (f32[512,1024]{1,0:T(8,128)S(1)}, f32[512,1024]{1,0:T(8,128)S(1)}, bf16[512,704]{1,0:T(8,128)(2,1)S(1)}, bf16[512,1408]{1,0:T(8,128)(2,1)S(1)}...) conditional(s32[]{:T(128)} %convert_element_type.905, (bf16[512,1024]{1,0:T(8,128)(2,1)}, ...), branch_computations={%region_19.21_spmd, %region_20.22_spmd} | conditional | flops 8883929088 | bytes 60031024 | solution.py:532
  341.5 4.0 fusion.415
  361.4 3.8 multiply_reduce_fusion.30
  370.4 15.4 %collective-permute-done.27 = bf16[256,1024]{1,0:T(8,128)(2,1)S(1)} collective-permute-done((bf16[256,1024]{1,0:T(8,128)(2,1)S(1)}, bf16[256,1024]{1,0:T(8,128)(2,1)S(1)}, u32[]{:S(2)}, u32[]{:S(2)}) %collective-permute-start.27) | collective-permute-done | bytes 524320 | tf_op jit(solution)/shard_map/ppermute | solution.py:657
  386.2 13.4 %collective-permute-done.29 = bf16[256,1024]{1,0:T(8,128)(2,1)S(1)} collective-permute-done((bf16[256,1024]{1,0:T(8,128)(2,1)S(1)}, bf16[256,1024]{1,0:T(8,128)(2,1)S(1)}, u32[]{:S(2)}, u32[]{:S(2)}) %collective-permute-start.29) | collective-permute-done | bytes 524320 | tf_op jit(solution)/shard_map/ppermute | solution.py:495
  403.6 18.4 %conditional.32 = (f32[512,1024]{1,0:T(8,128)S(1)}, bf16[512,256]{1,0:T(8,128)(2,1)S(1)}, bf16[1024,512]{1,0:T(8,128)(2,1)S(1)}, bf16[512,256]{1,0:T(8,128)(2,1)...) conditional(s32[]{:T(128)} %convert_element_type.905, ...), branch_computations={%region_25.27_spmd, %region_26.28_spmd} | conditional | flops 7518027776 | bytes 25165896 | solution.py:532
  410.7 5.2 attn_fwd.11
  415.9 5.1 attn_fwd.10
  422.8 4.3 pad_maximum_fusion.19
  429.6 22.4 %conditional.27 = (f32[512,1024]{1,0:T(8,128)S(1)}, f32[512,1024]{1,0:T(8,128)S(1)}, bf16[512,704]{1,0:T(8,128)(2,1)S(1)}, bf16[512,1408]{1,0:T(8,128)(2,1)S(1)}...) conditional(s32[]{:T(128)} %convert_element_type.905, (bf16[512,1024]{1,0:T(8,128)(2,1)}, ...), branch_computations={%region_10.12_spmd, %region_11.13_spmd} | conditional | flops 8883929088 | bytes 65798220 | solution.py:532
  430.0 4.0 fusion.410
  463.3 22.2 %conditional.33 = (f32[512,1024]{1,0:T(8,128)S(1)}, f32[512,1024]{1,0:T(8,128)S(1)}, bf16[512,704]{1,0:T(8,128)(2,1)S(1)}, bf16[512,1408]{1,0:T(8,128)(2,1)S(1)}...) conditional(s32[]{:T(128)} %convert_element_type.905, (bf16[512,1024]{1,0:T(8,128)(2,1)}, ...), branch_computations={%region_28.30_spmd, %region_29.31_spmd} | conditional | flops 8883929088 | bytes 60031024 | solution.py:532
  463.3 4.0 fusion.420
  490.4 4.2 fusion.392
  497.7 25.4 %conditional.38 = (f32[512,1024]{1,0:T(8,128)S(1)}, bf16[256,1024]{1,0:T(8,128)(2,1)}, bf16[256,1024]{1,0:T(8,128)(2,1)}, bf16[512,256]{1,0:T(8,128)(2,1)S(1)}, ...) conditional(s32[]{:T(128)} %convert_element_type.905, ...), branch_computations={%region_49.51_spmd, %region_50.52_spmd} | conditional | flops 13962051584 | bytes 40894536 | solution.py:532
  501.1 7.3 attn_bwd.14
  508.4 7.3 attn_bwd.13
  523.4 4.3 pad_maximum_fusion.28
  527.8 25.8 %conditional.36 = (f32[512,1024]{1,0:T(8,128)S(1)}, bf16[256,1024]{1,0:T(8,128)(2,1)}, bf16[256,1024]{1,0:T(8,128)(2,1)}, bf16[512,256]{1,0:T(8,128)(2,1)S(1)}, ...) conditional(s32[]{:T(128)} %convert_element_type.905, ...), branch_computations={%region_40.42_spmd, %region_41.43_spmd} | conditional | flops 13962051584 | bytes 50331804 | solution.py:532
  531.3 7.3 attn_bwd.12
  538.6 7.3 attn_bwd.11
  555.2 3.7 pad_maximum_fusion.26
  559.0 25.3 %conditional.34 = (f32[512,1024]{1,0:T(8,128)S(1)}, bf16[256,1024]{1,0:T(8,128)(2,1)}, bf16[256,1024]{1,0:T(8,128)(2,1)}, bf16[512,256]{1,0:T(8,128)(2,1)S(1)}, ...) conditional(s32[]{:T(128)} %convert_element_type.905, ...), branch_computations={%region_31.33_spmd, %region_32.34_spmd} | conditional | flops 13962051584 | bytes 50331804 | solution.py:532
  562.4 7.3 attn_bwd.10
  569.7 7.3 attn_bwd.9
  591.0 10.7 collective-permute-done.69
  605.9 7.0 collective-permute-done.54
  617.5 6.6 collective-permute-done.39
  626.6 40.0 %conditional.41 = (bf16[1024,512]{0,1:T(8,128)(2,1)}, bf16[1024,512]{1,0:T(8,128)(2,1)S(1)}, f32[1024,512]{1,0:T(8,128)S(1)}, f32[1024,512]{1,0:T(8,128)}) conditional(s32[]{:T(128)} %convert_element_type.905, (bf16[512,1024]{1,0:T(8,128)(2,1)S(1)}, bf16[512,256]{1,0:T(8,128)(2,1)S(1)}, bf16[512,1024]{1,0:T(8,128)(2,1)}, ...), branch_computations={%region_63.65_spmd, %region_64.66_spmd} | conditional | flops 9674686464 | bytes 112197864 | solution.py:532
  669.6 3.7 multiply_reduce_fusion
  687.5 5.9 conditional.39
  698.3 6.3 conditional.37
  708.9 6.0 conditional.35
  727.2 37.6 %collective-permute-start.83 = (bf16[1024,512]{1,0:T(8,128)(2,1)S(1)}, bf16[1024,512]{1,0:T(8,128)(2,1)S(1)}, u32[]{:S(2)}, u32[]{:S(2)}) collective-permute-start(bf16[1024,512]{1,0:T(8,128)(2,1)S(1)} %add_convert_fusion.13), channel_id=1, source_target_pairs={{16,0},{17,1},{18,2},{19,3},{20,4},{21,5},{22,6},{23,7},{24,8},{25... | collective-permute-start | bytes 3145736 | tf_op jit(solution)/shard_map/ppermute | solution.py:766
  765.0 4.7 multiply_reduce_fusion.8
  769.8 3.9 fusion.390
  775.2 3.9 fusion.388
  779.8 3.7 fusion.386
  784.9 3.9 collective-permute-done.75
  790.4 42.1 %conditional.40 = (bf16[1024,1408]{1,0:T(8,128)(2,1)S(1)}, bf16[704,1024]{1,0:T(8,128)(2,1)}, f32[1024,1408]{1,0:T(8,128)S(1)}, f32[704,1024]{1,0:T(8,128)S(1)}) conditional(s32[]{:T(128)} %convert_element_type.905, (bf16[512,1024]{1,0:T(8,128)(2,1)}, bf16[512,1408]{1,0:T(8,128)(2,1)}, bf16[512,1024]{1,0:T(8,128)(2,1)}, ...), branch_computations={%region_59.61_spmd, %region_60.62_spmd} | conditional | flops 13302693888 | bytes 160956800
  835.2 4.5 convolution_convert_fusion.18.refs_3_
  839.8 13.1 %attn_bwd.17 = bf16[1024,768]{1,0:T(8,128)(2,1)S(1)} custom-call(bf16[1024,768]{1,0:T(8,128)(2,1)S(1)} %copy-done, bf16[1024,768]{1,0:T(8,128)(2,1)S(1)} %copy-done, bf16[1024,768]{1,0:T(8,128)(2,1)S(1)} %copy-done, bf16[1024,256]{1,0:T(8,128)(2,1)S(1)} %convolution_convert_fusion.18.refs_3_, bf16[1024,256]{1,0:T(8,128)(2,1)S(1)} %copy-done.6, ...), custom_call_target="tpu_custom_call" | custom-call | flops 10737418240 | bytes 4718592 | tf_op jit(solution)/shard_map/attn_bwd/pallas_call | solution.py:187
  858.3 13.6 %attn_bwd.16 = bf16[1024,768]{1,0:T(8,128)(2,1)S(1)} custom-call(bf16[1024,768]{1,0:T(8,128)(2,1)S(1)} %get-tuple-element.1235.refs_0_.refs_1_.refs_2_, bf16[1024,768]{1,0:T(8,128)(2,1)S(1)} %get-tuple-element.1235.refs_0_.refs_1_.refs_2_, bf16[1024,768]{1,0:T(8,128)(2,1)S(1)} %get-tuple-element.1235.refs_0_.refs_1_.refs_2_, ...), custom_call_target="tpu_custom_call" | custom-call | flops 10737418240 | bytes 4718592 | tf_op jit(solution)/shard_map/attn_bwd/pallas_call | solution.py:187
  886.4 13.3 %attn_bwd.15 = bf16[1024,768]{1,0:T(8,128)(2,1)S(1)} custom-call(bf16[1024,768]{1,0:T(8,128)(2,1)S(1)} %get-tuple-element.1233.refs_0_.refs_1_.refs_2_, bf16[1024,768]{1,0:T(8,128)(2,1)S(1)} %get-tuple-element.1233.refs_0_.refs_1_.refs_2_, bf16[1024,768]{1,0:T(8,128)(2,1)S(1)} %get-tuple-element.1233.refs_0_.refs_1_.refs_2_, ...), custom_call_target="tpu_custom_call" | custom-call | flops 10737418240 | bytes 4718592 | tf_op jit(solution)/shard_map/attn_bwd/pallas_call | solution.py:187
  911.6 8.3 collective-permute-done.79
  919.9 11.2 collective-permute-done.64
  931.1 10.8 collective-permute-done.49
  941.9 3.9 fusion.273
  947.0 3.8 add_convert_fusion.11
  963.1 54.2 %collective-permute-done.80 = bf16[1024,1408]{1,0:T(8,128)(2,1)} collective-permute-done((bf16[1024,1408]{1,0:T(8,128)(2,1)}, bf16[1024,1408]{1,0:T(8,128)(2,1)}, u32[]{:S(2)}, u32[]{:S(2)}) %collective-permute-start.80) | collective-permute-done | bytes 2883616 | tf_op jit(solution)/shard_map/ppermute | solution.py:495
  1017.3 6.0 add_convert_fusion.9
  1048.1 34.5 %reduce-scatter.9.cloned.1.call-done = bf16[256,768]{1,0:T(8,128)(2,1)} async-done(((bf16[1024,768]{1,0:T(8,128)(2,1)}), bf16[256,768]{1,0:T(8,128)(2,1)}) %reduce-scatter.9.cloned.1.call-update) | async-done | bytes 393232 | tf_op jit(solution)/shard_map/reduce_scatter | solution.py:752
  1084.9 55.0 %reduce-scatter.13.cloned.1.call-done = bf16[256,1408]{1,0:T(8,128)(2,1)} async-done(((bf16[1024,1408]{1,0:T(8,128)(2,1)}), bf16[256,1408]{1,0:T(8,128)(2,1)}) %reduce-scatter.13.cloned.1.call-update) | async-done | bytes 720912 | tf_op jit(solution)/shard_map/reduce_scatter | solution.py:752
  (1126 shorter events, 459.5 us)
Async XLA Ops:
  7.2 1024.8 %reduce-scatter.17.cloned.1.call-start = ((), (), s32[]{:S(2)}) async-start(), calls=%async_computation.10 | async-start | bytes 1310720 | tf_op jit(solution)/shard_map/reduce_scatter | solution.py:752
  7.2 179.8 %collective-permute-start.2 = (bf16[704,1024]{1,0:T(8,128)(2,1)}, bf16[704,1024]{1,0:T(8,128)(2,1)S(1)}, u32[]{:S(2)}, u32[]{:S(2)}) collective-permute-start(bf16[704,1024]{1,0:T(8,128)(2,1)} %bitcast.592), channel_id=1, source_target_pairs={{0,2},{1,3},{2,0},{3,1},{4,6},{5,7},{6,4},{7,5},{8,10},{9,11},{10,... | collective-permute-start | bytes 4325384 | tf_op jit(solution)/shard_map/ppermute | solution.py:495
  8.8 178.3 %collective-permute-start.1 = (bf16[1024,1408]{0,1:T(8,128)(2,1)}, bf16[1024,1408]{0,1:T(8,128)(2,1)}, u32[]{:S(2)}, u32[]{:S(2)}) collective-permute-start(bf16[1024,1408]{0,1:T(8,128)(2,1)} %bitcast.582), channel_id=1, source_target_pairs={{0,2},{1,3},{2,0},{3,1},{4,6},{5,7},{6,4},{7,5},{8,10},{9,11},{10,... | collective-permute-start | bytes 8650760 | tf_op jit(solution)/shard_map/ppermute | solution.py:495
  183.0 82.6 %collective-permute-start.8 = (bf16[1024,512]{1,0:T(8,128)(2,1)}, bf16[1024,512]{1,0:T(8,128)(2,1)}, u32[]{:S(2)}, u32[]{:S(2)}) collective-permute-start(bf16[1024,512]{1,0:T(8,128)(2,1)} %bitcast.67), channel_id=1, source_target_pairs={{0,16},{1,17},{2,18},{3,19},{4,20},{5,21},{6,22},{7,23},{8,24},{9,... | collective-permute-start | bytes 3145736 | tf_op jit(solution)/shard_map/ppermute | solution.py:591
  184.2 65.0 %collective-permute-start.9 = (bf16[1024,512]{1,0:T(8,128)(2,1)}, bf16[1024,512]{1,0:T(8,128)(2,1)}, u32[]{:S(2)}, u32[]{:S(2)}) collective-permute-start(bf16[1024,512]{1,0:T(8,128)(2,1)} %bitcast.67), channel_id=1, source_target_pairs={{0,2},{1,3},{2,0},{3,1},{4,6},{5,7},{6,4},{7,5},{8,10},{9,11},{10,... | collective-permute-start | bytes 3145736 | tf_op jit(solution)/shard_map/ppermute | solution.py:495
  191.2 60.3 %collective-permute-start.23 = (bf16[256,1024]{1,0:T(8,128)(2,1)S(1)}, bf16[256,1024]{1,0:T(8,128)(2,1)}, u32[]{:S(2)}, u32[]{:S(2)}) collective-permute-start(bf16[256,1024]{1,0:T(8,128)(2,1)S(1)} %get-tuple-element.1261), channel_id=1, source_target_pairs={{0,1},{1,0},{2,3},{3,2},{4,5},{5,4},{6,7},{7,6},{8,9},{9,8},{10,11... | collective-permute-start | bytes 1572872 | tf_op jit(solution)/shard_map/ppermute | solution.py:495
  200.9 34.7 %collective-permute-start.4 = (bf16[256,1024]{1,0:T(8,128)(2,1)S(1)}, bf16[256,1024]{1,0:T(8,128)(2,1)}, u32[]{:S(2)}, u32[]{:S(2)}) collective-permute-start(bf16[256,1024]{1,0:T(8,128)(2,1)S(1)} %get-tuple-element.1296), channel_id=1, source_target_pairs={{0,16},{1,17},{2,18},{3,19},{4,20},{5,21},{6,22},{7,23},{8,24},{9,... | collective-permute-start | bytes 1572872 | tf_op jit(solution)/shard_map/ppermute | solution.py:657
  202.2 44.2 %collective-permute-start.17 = (bf16[256,1024]{1,0:T(8,128)(2,1)S(1)}, bf16[256,1024]{1,0:T(8,128)(2,1)S(1)}, u32[]{:S(2)}, u32[]{:S(2)}) collective-permute-start(bf16[256,1024]{1,0:T(8,128)(2,1)S(1)} %get-tuple-element.1297), channel_id=1, source_target_pairs={{0,16},{1,17},{2,18},{3,19},{4,20},{5,21},{6,22},{7,23},{8,24},{9,... | collective-permute-start | bytes 1572872 | tf_op jit(solution)/shard_map/ppermute | solution.py:657
  235.6 18.0 %collective-permute-start.6 = (bf16[256,1024]{1,0:T(8,128)(2,1)}, bf16[256,1024]{1,0:T(8,128)(2,1)}, u32[]{:S(2)}, u32[]{:S(2)}) collective-permute-start(bf16[256,1024]{1,0:T(8,128)(2,1)} %collective-permute-done.4), channel_id=1, source_target_pairs={{0,2},{1,3},{2,0},{3,1},{4,6},{5,7},{6,4},{7,5},{8,10},{9,11},{10,... | collective-permute-start | bytes 1572872 | tf_op jit(solution)/shard_map/ppermute | solution.py:495
  249.3 26.9 %collective-permute-start.10 = (bf16[1024,512]{1,0:T(8,128)(2,1)}, bf16[1024,512]{1,0:T(8,128)(2,1)}, u32[]{:S(2)}, u32[]{:S(2)}) collective-permute-start(bf16[1024,512]{1,0:T(8,128)(2,1)} %collective-permute-done.9), channel_id=1, source_target_pairs={{0,16},{1,17},{2,18},{3,19},{4,20},{5,21},{6,22},{7,23},{8,24},{9,... | collective-permute-start | bytes 3145736 | tf_op jit(solution)/shard_map/ppermute | solution.py:591
  253.6 46.7 %collective-permute-start.25 = (bf16[256,1024]{1,0:T(8,128)(2,1)}, bf16[256,1024]{1,0:T(8,128)(2,1)}, u32[]{:S(2)}, u32[]{:S(2)}) collective-permute-start(bf16[256,1024]{1,0:T(8,128)(2,1)} %get-tuple-element.1300), channel_id=1, source_target_pairs={{0,1},{1,0},{2,3},{3,2},{4,5},{5,4},{6,7},{7,6},{8,9},{9,8},{10,11... | collective-permute-start | bytes 1572872 | tf_op jit(solution)/shard_map/ppermute | solution.py:495
  262.6 45.0 %collective-permute-start.5 = (bf16[256,1024]{1,0:T(8,128)(2,1)}, bf16[256,1024]{1,0:T(8,128)(2,1)}, u32[]{:S(2)}, u32[]{:S(2)}) collective-permute-start(bf16[256,1024]{1,0:T(8,128)(2,1)} %collective-permute-done.4), channel_id=1, source_target_pairs={{0,1},{1,0},{2,3},{3,2},{4,5},{5,4},{6,7},{7,6},{8,9},{9,8},{10,11... | collective-permute-start | bytes 1572872 | tf_op jit(solution)/shard_map/ppermute | solution.py:495
  264.8 46.8 %collective-permute-start.7 = (bf16[256,1024]{1,0:T(8,128)(2,1)}, bf16[256,1024]{1,0:T(8,128)(2,1)}, u32[]{:S(2)}, u32[]{:S(2)}) collective-permute-start(bf16[256,1024]{1,0:T(8,128)(2,1)} %collective-permute-done.6), channel_id=1, source_target_pairs={{0,1},{1,0},{2,3},{3,2},{4,5},{5,4},{6,7},{7,6},{8,9},{9,8},{10,11... | collective-permute-start | bytes 1572872 | tf_op jit(solution)/shard_map/ppermute | solution.py:495
  300.3 33.0 %collective-permute-start.21 = (bf16[256,1024]{1,0:T(8,128)(2,1)}, bf16[256,1024]{1,0:T(8,128)(2,1)}, u32[]{:S(2)}, u32[]{:S(2)}) collective-permute-start(bf16[256,1024]{1,0:T(8,128)(2,1)} %slice.1019), channel_id=1, source_target_pairs={{0,1},{1,0},{2,3},{3,2},{4,5},{5,4},{6,7},{7,6},{8,9},{9,8},{10,11... | collective-permute-start | bytes 1572872 | tf_op jit(solution)/shard_map/ppermute | solution.py:495
  305.2 30.8 %collective-permute-start.26 = (bf16[256,1024]{1,0:T(8,128)(2,1)}, bf16[256,1024]{1,0:T(8,128)(2,1)}, u32[]{:S(2)}, u32[]{:S(2)}) collective-permute-start(bf16[256,1024]{1,0:T(8,128)(2,1)} %slice.1017), channel_id=1, source_target_pairs={{0,1},{1,0},{2,3},{3,2},{4,5},{5,4},{6,7},{7,6},{8,9},{9,8},{10,11... | collective-permute-start | bytes 1572872 | tf_op jit(solution)/shard_map/ppermute | solution.py:495
  332.9 28.5 %collective-permute-start.11 = (bf16[256,1024]{1,0:T(8,128)(2,1)}, bf16[256,1024]{1,0:T(8,128)(2,1)}, u32[]{:S(2)}, u32[]{:S(2)}) collective-permute-start(bf16[256,1024]{1,0:T(8,128)(2,1)} %slice.1022), channel_id=1, source_target_pairs={{0,1},{1,0},{2,3},{3,2},{4,5},{5,4},{6,7},{7,6},{8,9},{9,8},{10,11... | collective-permute-start | bytes 1572872 | tf_op jit(solution)/shard_map/ppermute | solution.py:495
  399.7 23.1 %collective-permute-start.13 = (bf16[256,1024]{1,0:T(8,128)(2,1)}, bf16[256,1024]{1,0:T(8,128)(2,1)}, u32[]{:S(2)}, u32[]{:S(2)}) collective-permute-start(bf16[256,1024]{1,0:T(8,128)(2,1)} %get-tuple-element.1259), channel_id=1, source_target_pairs={{0,1},{1,0},{2,3},{3,2},{4,5},{5,4},{6,7},{7,6},{8,9},{9,8},{10,11... | collective-permute-start | bytes 1572872 | tf_op jit(solution)/shard_map/ppermute | solution.py:495
  400.2 27.0 %collective-permute-start.12 = (bf16[256,1024]{1,0:T(8,128)(2,1)}, bf16[256,1024]{1,0:T(8,128)(2,1)}, u32[]{:S(2)}, u32[]{:S(2)}) collective-permute-start(bf16[256,1024]{1,0:T(8,128)(2,1)} %get-tuple-element.1293), channel_id=1, source_target_pairs={{0,1},{1,0},{2,3},{3,2},{4,5},{5,4},{6,7},{7,6},{8,9},{9,8},{10,11... | collective-permute-start | bytes 1572872 | tf_op jit(solution)/shard_map/ppermute | solution.py:495
  422.2 31.2 %collective-permute-start.31 = (bf16[256,1024]{1,0:T(8,128)(2,1)S(1)}, bf16[256,1024]{1,0:T(8,128)(2,1)}, u32[]{:S(2)}, u32[]{:S(2)}) collective-permute-start(bf16[256,1024]{1,0:T(8,128)(2,1)S(1)} %slice.1016), channel_id=1, source_target_pairs={{0,1},{1,0},{2,3},{3,2},{4,5},{5,4},{6,7},{7,6},{8,9},{9,8},{10,11... | collective-permute-start | bytes 1572872 | tf_op jit(solution)/shard_map/ppermute | solution.py:495
  422.7 36.5 %collective-permute-start.33 = (bf16[256,1024]{1,0:T(8,128)(2,1)}, bf16[256,1024]{1,0:T(8,128)(2,1)}, u32[]{:S(2)}, u32[]{:S(2)}) collective-permute-start(bf16[256,1024]{1,0:T(8,128)(2,1)} %get-tuple-element.1260), channel_id=1, source_target_pairs={{0,1},{1,0},{2,3},{3,2},{4,5},{5,4},{6,7},{7,6},{8,9},{9,8},{10,11... | collective-permute-start | bytes 1572872 | tf_op jit(solution)/shard_map/ppermute | solution.py:495
  494.7 28.8 %collective-permute-start.51 = (bf16[256,1024]{1,0:T(8,128)(2,1)}, bf16[256,1024]{1,0:T(8,128)(2,1)}, u32[]{:S(2)}, u32[]{:S(2)}) collective-permute-start(bf16[256,1024]{1,0:T(8,128)(2,1)} %get-tuple-element.1137), channel_id=1, source_target_pairs={{0,1},{1,0},{2,3},{3,2},{4,5},{5,4},{6,7},{7,6},{8,9},{9,8},{10,11... | collective-permute-start | bytes 1572872 | tf_op jit(solution)/shard_map/ppermute | solution.py:495
  495.2 60.0 %collective-permute-start.36 = (bf16[256,1024]{1,0:T(8,128)(2,1)}, bf16[256,1024]{1,0:T(8,128)(2,1)}, u32[]{:S(2)}, u32[]{:S(2)}) collective-permute-start(bf16[256,1024]{1,0:T(8,128)(2,1)} %get-tuple-element.1246), channel_id=1, source_target_pairs={{0,1},{1,0},{2,3},{3,2},{4,5},{5,4},{6,7},{7,6},{8,9},{9,8},{10,11... | collective-permute-start | bytes 1572872 | tf_op jit(solution)/shard_map/ppermute | solution.py:495
  523.2 61.9 %collective-permute-start.68 = (bf16[256,1024]{1,0:T(8,128)(2,1)}, bf16[256,1024]{1,0:T(8,128)(2,1)}, u32[]{:S(2)}, u32[]{:S(2)}) collective-permute-start(bf16[256,1024]{1,0:T(8,128)(2,1)} %get-tuple-element.802), channel_id=1, source_target_pairs={{0,1},{1,0},{2,3},{3,2},{4,5},{5,4},{6,7},{7,6},{8,9},{9,8},{10,11... | collective-permute-start | bytes 1572872 | tf_op jit(solution)/shard_map/ppermute | solution.py:495
  553.7 33.1 %collective-permute-start.53 = (bf16[256,1024]{1,0:T(8,128)(2,1)}, bf16[256,1024]{1,0:T(8,128)(2,1)}, u32[]{:S(2)}, u32[]{:S(2)}) collective-permute-start(bf16[256,1024]{1,0:T(8,128)(2,1)} %get-tuple-element.785), channel_id=1, source_target_pairs={{0,1},{1,0},{2,3},{3,2},{4,5},{5,4},{6,7},{7,6},{8,9},{9,8},{10,11... | collective-permute-start | bytes 1572872 | tf_op jit(solution)/shard_map/ppermute | solution.py:495
  554.6 35.8 %collective-permute-start.67 = (bf16[256,1024]{1,0:T(8,128)(2,1)}, bf16[256,1024]{1,0:T(8,128)(2,1)}, u32[]{:S(2)}, u32[]{:S(2)}) collective-permute-start(bf16[256,1024]{1,0:T(8,128)(2,1)} %get-tuple-element.800), channel_id=1, source_target_pairs={{0,1},{1,0},{2,3},{3,2},{4,5},{5,4},{6,7},{7,6},{8,9},{9,8},{10,11... | collective-permute-start | bytes 1572872 | tf_op jit(solution)/shard_map/ppermute | solution.py:495
  554.7 51.2 %collective-permute-start.52 = (bf16[256,1024]{1,0:T(8,128)(2,1)}, bf16[256,1024]{1,0:T(8,128)(2,1)}, u32[]{:S(2)}, u32[]{:S(2)}) collective-permute-start(bf16[256,1024]{1,0:T(8,128)(2,1)} %get-tuple-element.783), channel_id=1, source_target_pairs={{0,1},{1,0},{2,3},{3,2},{4,5},{5,4},{6,7},{7,6},{8,9},{9,8},{10,11... | collective-permute-start | bytes 1572872 | tf_op jit(solution)/shard_map/ppermute | solution.py:495
  584.3 33.2 %collective-permute-start.37 = (bf16[256,1024]{1,0:T(8,128)(2,1)}, bf16[256,1024]{1,0:T(8,128)(2,1)S(1)}, u32[]{:S(2)}, u32[]{:S(2)}) collective-permute-start(bf16[256,1024]{1,0:T(8,128)(2,1)} %get-tuple-element.763), channel_id=1, source_target_pairs={{0,1},{1,0},{2,3},{3,2},{4,5},{5,4},{6,7},{7,6},{8,9},{9,8},{10,11... | collective-permute-start | bytes 1572872 | tf_op jit(solution)/shard_map/ppermute | solution.py:495
  588.6 24.3 %collective-permute-start.54 = (bf16[256,1024]{1,0:T(8,128)(2,1)S(1)}, bf16[256,1024]{1,0:T(8,128)(2,1)S(1)}, u32[]{:S(2)}, u32[]{:S(2)}) collective-permute-start(bf16[256,1024]{1,0:T(8,128)(2,1)S(1)} %add_convert_fusion.22), channel_id=1, source_target_pairs={{0,2},{1,3},{2,0},{3,1},{4,6},{5,7},{6,4},{7,5},{8,10},{9,11},{10,... | collective-permute-start | bytes 1572872 | tf_op jit(solution)/shard_map/ppermute | solution.py:495
  590.4 33.7 %collective-permute-start.39 = (bf16[256,1024]{1,0:T(8,128)(2,1)S(1)}, bf16[256,1024]{1,0:T(8,128)(2,1)S(1)}, u32[]{:S(2)}, u32[]{:S(2)}) collective-permute-start(bf16[256,1024]{1,0:T(8,128)(2,1)S(1)} %add_convert_fusion.27), channel_id=1, source_target_pairs={{0,2},{1,3},{2,0},{3,1},{4,6},{5,7},{6,4},{7,5},{8,10},{9,11},{10,... | collective-permute-start | bytes 1572872 | tf_op jit(solution)/shard_map/ppermute | solution.py:495
  603.8 65.7 %collective-permute-start.70 = (bf16[256,1024]{1,0:T(8,128)(2,1)}, bf16[256,1024]{1,0:T(8,128)(2,1)}, u32[]{:S(2)}, u32[]{:S(2)}) collective-permute-start(bf16[256,1024]{1,0:T(8,128)(2,1)} %add_convert_fusion.16), channel_id=1, source_target_pairs={{16,0},{17,1},{18,2},{19,3},{20,4},{21,5},{22,6},{23,7},{24,8},{25... | collective-permute-start | bytes 1572872 | tf_op jit(solution)/shard_map/ppermute | solution.py:687
  615.3 54.2 %collective-permute-start.55 = (bf16[256,1024]{1,0:T(8,128)(2,1)}, bf16[256,1024]{1,0:T(8,128)(2,1)}, u32[]{:S(2)}, u32[]{:S(2)}) collective-permute-start(bf16[256,1024]{1,0:T(8,128)(2,1)} %add_convert_fusion.21), channel_id=1, source_target_pairs={{16,0},{17,1},{18,2},{19,3},{20,4},{21,5},{22,6},{23,7},{24,8},{25... | collective-permute-start | bytes 1572872 | tf_op jit(solution)/shard_map/ppermute | solution.py:687
  625.1 44.4 %collective-permute-start.40 = (bf16[256,1024]{1,0:T(8,128)(2,1)}, bf16[256,1024]{1,0:T(8,128)(2,1)S(1)}, u32[]{:S(2)}, u32[]{:S(2)}) collective-permute-start(bf16[256,1024]{1,0:T(8,128)(2,1)} %add_convert_fusion.26), channel_id=1, source_target_pairs={{16,0},{17,1},{18,2},{19,3},{20,4},{21,5},{22,6},{23,7},{24,8},{25... | collective-permute-start | bytes 1572872 | tf_op jit(solution)/shard_map/ppermute | solution.py:687
  668.9 48.5 %collective-permute-start.82 = (bf16[1024,512]{1,0:T(8,128)(2,1)}, bf16[1024,512]{1,0:T(8,128)(2,1)}, u32[]{:S(2)}, u32[]{:S(2)}) collective-permute-start(bf16[1024,512]{1,0:T(8,128)(2,1)} %copy-done.292), channel_id=1, source_target_pairs={{0,2},{1,3},{2,0},{3,1},{4,6},{5,7},{6,4},{7,5},{8,10},{9,11},{10,... | collective-permute-start | bytes 3145736 | tf_op jit(solution)/shard_map/ppermute | solution.py:495
  676.4 19.1 %collective-permute-start.56 = (bf16[256,1024]{1,0:T(8,128)(2,1)}, bf16[256,1024]{1,0:T(8,128)(2,1)}, u32[]{:S(2)}, u32[]{:S(2)}) collective-permute-start(bf16[256,1024]{1,0:T(8,128)(2,1)} %get-tuple-element.1244), channel_id=1, source_target_pairs={{0,1},{1,0},{2,3},{3,2},{4,5},{5,4},{6,7},{7,6},{8,9},{9,8},{10,11... | collective-permute-start | bytes 1572872 | tf_op jit(solution)/shard_map/ppermute | solution.py:495
  680.5 36.5 %collective-permute-start.73 = (bf16[256,1024]{1,0:T(8,128)(2,1)}, bf16[256,1024]{1,0:T(8,128)(2,1)}, u32[]{:S(2)}, u32[]{:S(2)}) collective-permute-start(bf16[256,1024]{1,0:T(8,128)(2,1)} %slice.1006), channel_id=1, source_target_pairs={{0,1},{1,0},{2,3},{3,2},{4,5},{5,4},{6,7},{7,6},{8,9},{9,8},{10,11... | collective-permute-start | bytes 1572872 | tf_op jit(solution)/shard_map/ppermute | solution.py:495
  680.5 26.1 %collective-permute-start.41 = (bf16[256,1024]{1,0:T(8,128)(2,1)}, bf16[256,1024]{1,0:T(8,128)(2,1)}, u32[]{:S(2)}, u32[]{:S(2)}) collective-permute-start(bf16[256,1024]{1,0:T(8,128)(2,1)} %get-tuple-element.1243), channel_id=1, source_target_pairs={{0,1},{1,0},{2,3},{3,2},{4,5},{5,4},{6,7},{7,6},{8,9},{9,8},{10,11... | collective-permute-start | bytes 1572872 | tf_op jit(solution)/shard_map/ppermute | solution.py:495
  686.5 39.2 %collective-permute-start.43 = (bf16[256,1024]{1,0:T(8,128)(2,1)}, bf16[256,1024]{1,0:T(8,128)(2,1)}, u32[]{:S(2)}, u32[]{:S(2)}) collective-permute-start(bf16[256,1024]{1,0:T(8,128)(2,1)} %slice.1012), channel_id=1, source_target_pairs={{0,1},{1,0},{2,3},{3,2},{4,5},{5,4},{6,7},{7,6},{8,9},{9,8},{10,11... | collective-permute-start | bytes 1572872 | tf_op jit(solution)/shard_map/ppermute | solution.py:495
  695.5 31.7 %collective-permute-start.58 = (bf16[256,1024]{1,0:T(8,128)(2,1)}, bf16[256,1024]{1,0:T(8,128)(2,1)}, u32[]{:S(2)}, u32[]{:S(2)}) collective-permute-start(bf16[256,1024]{1,0:T(8,128)(2,1)} %slice.1009), channel_id=1, source_target_pairs={{0,1},{1,0},{2,3},{3,2},{4,5},{5,4},{6,7},{7,6},{8,9},{9,8},{10,11... | collective-permute-start | bytes 1572872 | tf_op jit(solution)/shard_map/ppermute | solution.py:495
  706.6 58.2 %collective-permute-start.72 = (bf16[256,1024]{1,0:T(8,128)(2,1)}, bf16[256,1024]{1,0:T(8,128)(2,1)}, u32[]{:S(2)}, u32[]{:S(2)}) collective-permute-start(bf16[256,1024]{1,0:T(8,128)(2,1)} %slice.1007), channel_id=1, source_target_pairs={{0,1},{1,0},{2,3},{3,2},{4,5},{5,4},{6,7},{7,6},{8,9},{9,8},{10,11... | collective-permute-start | bytes 1572872 | tf_op jit(solution)/shard_map/ppermute | solution.py:495
  717.0 47.9 %collective-permute-start.42 = (bf16[256,1024]{1,0:T(8,128)(2,1)}, bf16[256,1024]{1,0:T(8,128)(2,1)}, u32[]{:S(2)}, u32[]{:S(2)}) collective-permute-start(bf16[256,1024]{1,0:T(8,128)(2,1)} %slice.1013), channel_id=1, source_target_pairs={{0,1},{1,0},{2,3},{3,2},{4,5},{5,4},{6,7},{7,6},{8,9},{9,8},{10,11... | collective-permute-start | bytes 1572872 | tf_op jit(solution)/shard_map/ppermute | solution.py:495
  717.5 47.4 %collective-permute-start.57 = (bf16[256,1024]{1,0:T(8,128)(2,1)}, bf16[256,1024]{1,0:T(8,128)(2,1)}, u32[]{:S(2)}, u32[]{:S(2)}) collective-permute-start(bf16[256,1024]{1,0:T(8,128)(2,1)} %slice.1010), channel_id=1, source_target_pairs={{0,1},{1,0},{2,3},{3,2},{4,5},{5,4},{6,7},{7,6},{8,9},{9,8},{10,11... | collective-permute-start | bytes 1572872 | tf_op jit(solution)/shard_map/ppermute | solution.py:495
  725.6 57.9 %collective-permute-start.84 = (bf16[1024,512]{1,0:T(8,128)(2,1)S(1)}, bf16[1024,512]{1,0:T(8,128)(2,1)S(1)}, u32[]{:S(2)}, u32[]{:S(2)}) collective-permute-start(bf16[1024,512]{1,0:T(8,128)(2,1)S(1)} %copy-done.172), channel_id=1, source_target_pairs={{0,2},{1,3},{2,0},{3,1},{4,6},{5,7},{6,4},{7,5},{8,10},{9,11},{10,... | collective-permute-start | bytes 3145736 | tf_op jit(solution)/shard_map/ppermute | solution.py:495
  727.2 61.6 %collective-permute-start.83 = (bf16[1024,512]{1,0:T(8,128)(2,1)S(1)}, bf16[1024,512]{1,0:T(8,128)(2,1)S(1)}, u32[]{:S(2)}, u32[]{:S(2)}) collective-permute-start(bf16[1024,512]{1,0:T(8,128)(2,1)S(1)} %add_convert_fusion.13), channel_id=1, source_target_pairs={{16,0},{17,1},{18,2},{19,3},{20,4},{21,5},{22,6},{23,7},{24,8},{25... | collective-permute-start | bytes 3145736 | tf_op jit(solution)/shard_map/ppermute | solution.py:766
  775.1 59.0 %collective-permute-start.74 = (bf16[256,1024]{1,0:T(8,128)(2,1)}, bf16[256,1024]{1,0:T(8,128)(2,1)}, u32[]{:S(2)}, u32[]{:S(2)}) collective-permute-start(bf16[256,1024]{1,0:T(8,128)(2,1)} %get-tuple-element.1133), channel_id=1, source_target_pairs={{0,1},{1,0},{2,3},{3,2},{4,5},{5,4},{6,7},{7,6},{8,9},{9,8},{10,11... | collective-permute-start | bytes 1572872 | tf_op jit(solution)/shard_map/ppermute | solution.py:495
  779.1 55.2 %collective-permute-start.60 = (bf16[256,1024]{1,0:T(8,128)(2,1)}, bf16[256,1024]{1,0:T(8,128)(2,1)}, u32[]{:S(2)}, u32[]{:S(2)}) collective-permute-start(bf16[256,1024]{1,0:T(8,128)(2,1)} %get-tuple-element.1129), channel_id=1, source_target_pairs={{0,2},{1,3},{2,0},{3,1},{4,6},{5,7},{6,4},{7,5},{8,10},{9,11},{10,... | collective-permute-start | bytes 1572872 | tf_op jit(solution)/shard_map/ppermute | solution.py:495
  783.6 51.1 %collective-permute-start.45 = (bf16[256,1024]{1,0:T(8,128)(2,1)}, bf16[256,1024]{1,0:T(8,128)(2,1)}, u32[]{:S(2)}, u32[]{:S(2)}) collective-permute-start(bf16[256,1024]{1,0:T(8,128)(2,1)} %get-tuple-element.1125), channel_id=1, source_target_pairs={{0,2},{1,3},{2,0},{3,1},{4,6},{5,7},{6,4},{7,5},{8,10},{9,11},{10,... | collective-permute-start | bytes 1572872 | tf_op jit(solution)/shard_map/ppermute | solution.py:495
  788.8 46.1 %collective-permute-start.76 = (bf16[256,1024]{1,0:T(8,128)(2,1)}, bf16[256,1024]{1,0:T(8,128)(2,1)}, u32[]{:S(2)}, u32[]{:S(2)}) collective-permute-start(bf16[256,1024]{1,0:T(8,128)(2,1)} %collective-permute-done.75), channel_id=1, source_target_pairs={{0,1},{1,0},{2,3},{3,2},{4,5},{5,4},{6,7},{7,6},{8,9},{9,8},{10,11... | collective-permute-start | bytes 1572872 | tf_op jit(solution)/shard_map/ppermute | solution.py:495
  790.2 249.4 %reduce-scatter.11.cloned.1.call-start = ((), (), s32[]{:S(2)}) async-start(), calls=%async_computation.7 | async-start | bytes 655360 | tf_op jit(solution)/shard_map/reduce_scatter | solution.py:752
  832.5 114.6 %collective-permute-start.81 = (bf16[704,1024]{1,0:T(8,128)(2,1)}, bf16[704,1024]{1,0:T(8,128)(2,1)}, u32[]{:S(2)}, u32[]{:S(2)}) collective-permute-start(bf16[704,1024]{1,0:T(8,128)(2,1)} %get-tuple-element.835), channel_id=1, source_target_pairs={{0,2},{1,3},{2,0},{3,1},{4,6},{5,7},{6,4},{7,5},{8,10},{9,11},{10,... | collective-permute-start | bytes 4325384 | tf_op jit(solution)/shard_map/ppermute | solution.py:495
  834.1 21.6 %collective-permute-start.59 = (bf16[256,1024]{1,0:T(8,128)(2,1)}, bf16[256,1024]{1,0:T(8,128)(2,1)S(1)}, u32[]{:S(2)}, u32[]{:S(2)}) collective-permute-start(bf16[256,1024]{1,0:T(8,128)(2,1)} %get-tuple-element.1129), channel_id=1, source_target_pairs={{0,1},{1,0},{2,3},{3,2},{4,5},{5,4},{6,7},{7,6},{8,9},{9,8},{10,11... | collective-permute-start | bytes 1572872 | tf_op jit(solution)/shard_map/ppermute | solution.py:495
  834.3 45.3 %collective-permute-start.44 = (bf16[256,1024]{1,0:T(8,128)(2,1)}, bf16[256,1024]{1,0:T(8,128)(2,1)S(1)}, u32[]{:S(2)}, u32[]{:S(2)}) collective-permute-start(bf16[256,1024]{1,0:T(8,128)(2,1)} %get-tuple-element.1125), channel_id=1, source_target_pairs={{0,1},{1,0},{2,3},{3,2},{4,5},{5,4},{6,7},{7,6},{8,9},{9,8},{10,11... | collective-permute-start | bytes 1572872 | tf_op jit(solution)/shard_map/ppermute | solution.py:495
  834.6 21.6 %collective-permute-start.61 = (bf16[256,1024]{1,0:T(8,128)(2,1)}, bf16[256,1024]{1,0:T(8,128)(2,1)S(1)}, u32[]{:S(2)}, u32[]{:S(2)}) collective-permute-start(bf16[256,1024]{1,0:T(8,128)(2,1)} %collective-permute-done.60), channel_id=1, source_target_pairs={{0,1},{1,0},{2,3},{3,2},{4,5},{5,4},{6,7},{7,6},{8,9},{9,8},{10,11... | collective-permute-start | bytes 1572872 | tf_op jit(solution)/shard_map/ppermute | solution.py:495
  834.9 45.3 %collective-permute-start.46 = (bf16[256,1024]{1,0:T(8,128)(2,1)}, bf16[256,1024]{1,0:T(8,128)(2,1)S(1)}, u32[]{:S(2)}, u32[]{:S(2)}) collective-permute-start(bf16[256,1024]{1,0:T(8,128)(2,1)} %collective-permute-done.45), channel_id=1, source_target_pairs={{0,1},{1,0},{2,3},{3,2},{4,5},{5,4},{6,7},{7,6},{8,9},{9,8},{10,11... | collective-permute-start | bytes 1572872 | tf_op jit(solution)/shard_map/ppermute | solution.py:495
  855.7 55.9 %collective-permute-start.77 = (bf16[256,1024]{1,0:T(8,128)(2,1)}, bf16[256,1024]{1,0:T(8,128)(2,1)}, u32[]{:S(2)}, u32[]{:S(2)}) collective-permute-start(bf16[256,1024]{1,0:T(8,128)(2,1)} %convolution_convert_fusion.23), channel_id=1, source_target_pairs={{0,1},{1,0},{2,3},{3,2},{4,5},{5,4},{6,7},{7,6},{8,9},{9,8},{10,11... | collective-permute-start | bytes 1572872 | tf_op jit(solution)/shard_map/ppermute | solution.py:495
  856.3 44.6 %collective-permute-start.78 = (bf16[256,1024]{1,0:T(8,128)(2,1)}, bf16[256,1024]{1,0:T(8,128)(2,1)}, u32[]{:S(2)}, u32[]{:S(2)}) collective-permute-start(bf16[256,1024]{1,0:T(8,128)(2,1)} %convolution_convert_fusion.21), channel_id=1, source_target_pairs={{0,1},{1,0},{2,3},{3,2},{4,5},{5,4},{6,7},{7,6},{8,9},{9,8},{10,11... | collective-permute-start | bytes 1572872 | tf_op jit(solution)/shard_map/ppermute | solution.py:495
  879.7 27.5 %collective-permute-start.62 = (bf16[256,1024]{1,0:T(8,128)(2,1)}, bf16[256,1024]{1,0:T(8,128)(2,1)}, u32[]{:S(2)}, u32[]{:S(2)}) collective-permute-start(bf16[256,1024]{1,0:T(8,128)(2,1)} %convolution_convert_fusion.27), channel_id=1, source_target_pairs={{0,1},{1,0},{2,3},{3,2},{4,5},{5,4},{6,7},{7,6},{8,9},{9,8},{10,11... | collective-permute-start | bytes 1572872 | tf_op jit(solution)/shard_map/ppermute | solution.py:495
  880.2 23.1 %collective-permute-start.63 = (bf16[256,1024]{1,0:T(8,128)(2,1)}, bf16[256,1024]{1,0:T(8,128)(2,1)}, u32[]{:S(2)}, u32[]{:S(2)}) collective-permute-start(bf16[256,1024]{1,0:T(8,128)(2,1)} %convolution_convert_fusion.25), channel_id=1, source_target_pairs={{0,1},{1,0},{2,3},{3,2},{4,5},{5,4},{6,7},{7,6},{8,9},{9,8},{10,11... | collective-permute-start | bytes 1572872 | tf_op jit(solution)/shard_map/ppermute | solution.py:495
  883.8 157.5 %reduce-scatter.19.cloned.1.call-start = ((), (), s32[]{:S(2)}) async-start(), calls=%async_computation.11 | async-start | bytes 557056
  907.2 23.9 %collective-permute-start.64 = (bf16[256,1024]{1,0:T(8,128)(2,1)S(1)}, bf16[256,1024]{1,0:T(8,128)(2,1)S(1)}, u32[]{:S(2)}, u32[]{:S(2)}) collective-permute-start(bf16[256,1024]{1,0:T(8,128)(2,1)S(1)} %add_convert_fusion.19), channel_id=1, source_target_pairs={{0,2},{1,3},{2,0},{3,1},{4,6},{5,7},{6,4},{7,5},{8,10},{9,11},{10,... | collective-permute-start | bytes 1572872 | tf_op jit(solution)/shard_map/ppermute | solution.py:495
  907.8 34.0 %collective-permute-start.49 = (bf16[256,1024]{1,0:T(8,128)(2,1)S(1)}, bf16[256,1024]{1,0:T(8,128)(2,1)S(1)}, u32[]{:S(2)}, u32[]{:S(2)}) collective-permute-start(bf16[256,1024]{1,0:T(8,128)(2,1)S(1)} %add_convert_fusion.24), channel_id=1, source_target_pairs={{0,2},{1,3},{2,0},{3,1},{4,6},{5,7},{6,4},{7,5},{8,10},{9,11},{10,... | collective-permute-start | bytes 1572872 | tf_op jit(solution)/shard_map/ppermute | solution.py:495
  947.0 99.3 %reduce-scatter.15.cloned.1.call-start = ((), (), s32[]{:S(2)}) async-start(), calls=%async_computation.9 | async-start | bytes 1802240 | tf_op jit(solution)/shard_map/reduce_scatter | solution.py:752
  950.9 131.7 %reduce-scatter.9.cloned.1.call-start = ((), (), s32[]{:S(2)}) async-start(), calls=%async_computation.6 | async-start | bytes 1966080 | tf_op jit(solution)/shard_map/reduce_scatter | solution.py:752
  951.2 66.2 %collective-permute-start.80 = (bf16[1024,1408]{1,0:T(8,128)(2,1)}, bf16[1024,1408]{1,0:T(8,128)(2,1)}, u32[]{:S(2)}, u32[]{:S(2)}) collective-permute-start(bf16[1024,1408]{1,0:T(8,128)(2,1)} %copy-done.151), channel_id=1, source_target_pairs={{0,2},{1,3},{2,0},{3,1},{4,6},{5,7},{6,4},{7,5},{8,10},{9,11},{10,... | collective-permute-start | bytes 8650760 | tf_op jit(solution)/shard_map/ppermute | solution.py:495
  963.1 176.8 %reduce-scatter.13.cloned.1.call-start = ((), (), s32[]{:S(2)}) async-start(), calls=%async_computation.8 | async-start | bytes 3604480 | tf_op jit(solution)/shard_map/reduce_scatter | solution.py:752
  (349 other events, 3558.7 us)
Sparse Core Ops, SparseCore 0:
  790.4 36.3 reduce-scatter.16
  883.8 28.7 reduce-scatter.10
  947.1 64.0 reduce-scatter.18
  1013.9 32.2 reduce-scatter.14
  1048.4 34.1 reduce-scatter.8
  1084.7 55.1 reduce-scatter.12

commit v2 on v1

v2 whole, which is shorter than its diff:
```python
import functools
import math

import jax
import jax.numpy as jnp
from jax import lax
from jax.experimental import pallas as pl
from jax.experimental.pallas import tpu as pltpu
from jax.sharding import PartitionSpec as P

DK = 64
EPS = 1e-06
BIG = -1e30
SCALE = DK**-0.5
LOG_SCALE = SCALE * math.log2(math.e)
BF, F32 = jnp.bfloat16, jnp.float32

DOC_LANES = 3
OFFSET_LANE = 3
BLOCK_LANE = 8

MESH = pl.DeviceIdType.MESH

NT = (((1,), (1,)), ((), ()))
NN = (((1,), (0,)), ((), ()))
TN = (((0,), (0,)), ((), ()))


def dot(a, b, dims=NN):
    return lax.dot_general(a, b, dims, preferred_element_type=F32)


def norm_scale(tensor, gain):
    return tensor * lax.rsqrt(jnp.mean(tensor * tensor, axis=-1, keepdims=True) + EPS) * gain


def norm_back(tensor, gain, gradient):
    _, pull_back = jax.vjp(norm_scale, tensor, gain)
    return pull_back(gradient)


def split_three(column):
    high = column.astype(BF)
    rest = column - high.astype(F32)
    middle = rest.astype(BF)
    low = (rest - middle.astype(F32)).astype(BF)
    return high, middle, low


def with_offsets(base, column):
    lane = lax.broadcasted_iota(jnp.int32, base.shape, 1)
    out = base.astype(F32)
    for i, piece in enumerate(split_three(column)):
        out = jnp.where(lane == OFFSET_LANE + i, piece.astype(F32), out)
    return out.astype(BF)


def low_bit(j):
    return j & -j


def flipped(index, bit):
    return index + bit - 2 * bit * lax.rem(index // bit, 2)


def greet(n, section=False):
    barrier = pltpu.get_barrier_semaphore()
    idx = lax.axis_index("mp")
    bits = [j for j in range(1, n) if j == low_bit(j)]
    for bit in bits:
        pl.semaphore_signal(
            barrier, inc=1, device_id={"mp": flipped(idx, bit)}, device_id_type=MESH
        )
    if section:
        other = 1 - lax.axis_index("section")
        pl.semaphore_signal(barrier, inc=1, device_id={"section": other}, device_id_type=MESH)
    pl.semaphore_wait(barrier, len(bits) + (1 if section else 0))


class Gather:
    def __init__(self, n, own, got, send, recv):
        self.n, self.own, self.got, self.send, self.recv = n, own, got, send, recv
        self.idx = lax.axis_index("mp")
        self.slots = range(1, n)
        self.parents = sorted({j ^ low_bit(j) for j in self.slots} - {0}, key=int.bit_count)

    def block(self, r, j):
        return self.own.at[r] if j == 0 else self.got.at[r, j - 1]

    def copy(self, r, j):
        return pltpu.make_async_remote_copy(
            src_ref=self.block(r, j ^ low_bit(j)),
            dst_ref=self.got.at[r, j - 1],
            send_sem=self.send.at[r, j - 1],
            recv_sem=self.recv.at[r, j - 1],
            device_id={"mp": flipped(self.idx, low_bit(j))},
            device_id_type=MESH,
        )

    def start(self, r):
        for j in sorted(self.slots, reverse=True):
            if j == low_bit(j):
                self.copy(r, j).start()

    def forward(self, r):
        for parent in self.parents:
            self.copy(r, parent).wait_recv()
            for j in self.slots:
                if j ^ low_bit(j) == parent:
                    self.copy(r, j).start()

    def finish(self, r):
        for j in self.slots:
            if j not in self.parents:
                self.copy(r, j).wait_recv()

    def drain(self, r):
        for j in self.slots:
            self.copy(r, j).wait_send()


class Sums:
    def __init__(self, n, out, back, send, recv):
        self.n, self.out, self.back, self.send, self.recv = n, out, back, send, recv
        self.idx = lax.axis_index("mp")
        self.slots = range(1, n)

    def copy(self, r, j):
        return pltpu.make_async_remote_copy(
            src_ref=self.out.at[r, j - 1],
            dst_ref=self.back.at[r, j - 1],
            send_sem=self.send.at[r, j - 1],
            recv_sem=self.recv.at[r, j - 1],
            device_id={"mp": flipped(self.idx, low_bit(j))},
            device_id_type=MESH,
        )

    def terms(self, j):
        limit = low_bit(j) if j else self.n
        return [j | 1 << b for b in range(self.n.bit_length()) if 1 << b < limit]

    def put(self, r, j, part):
        self.out[r, j - 1] = part.astype(BF)
        if low_bit(j) == 1:
            self.copy(r, j).start()

    def forward(self, r):
        for j in sorted(self.slots, key=low_bit):
            if low_bit(j) == 1:
                continue
            total = self.out[r, j - 1].astype(F32)
            for k in self.terms(j):
                self.copy(r, k).wait_recv()
                total = total + self.back[r, k - 1].astype(F32)
            self.out[r, j - 1] = total.astype(BF)
            self.copy(r, j).start()

    def total(self, r, own):
        for k in self.terms(0):
            self.copy(r, k).wait_recv()
            own = own + self.back[r, k - 1].astype(F32)
        return own

    def drain(self, r):
        for j in self.slots:
            self.copy(r, j).wait_send()


def attend_into(size, heads, q, k, v, query_aug, key_aug, tri, mix, aug):
    keys_aug = key_aug[...]
    blocks = mix.shape[0] // size
    lanes_of = lambda at, head: slice(at + head * DK, at + (head + 1) * DK)
    for head in range(heads):
        lanes = lanes_of(0, head)
        keys = jnp.concatenate([k[0][:, lanes_of(k[1], head)], keys_aug], axis=1)
        values = jnp.concatenate([v[0][:, lanes_of(v[1], head)], keys_aug], axis=1)
        for c in range(blocks):
            rows = slice(c * size, (c + 1) * size)
            base = query_aug[rows, :]
            query = jnp.concatenate([q[0][rows, lanes_of(q[1], head)], base], axis=1)
            scores = []
            for j in range(blocks):
                s = dot(query, keys[j * size : (j + 1) * size], NT)
                scores.append(s + tri[...] if tri is not None and j == c else s)
            top = functools.reduce(jnp.maximum, scores)
            top = jnp.max(top, axis=1, keepdims=True)
            total = None
            for j, s in enumerate(scores):
                p = jnp.exp2((s - top) * LOG_SCALE).astype(BF)
                o = dot(p, values[j * size : (j + 1) * size])
                total = o if total is None else total + o
            weight = total[:, DK + OFFSET_LANE : DK + OFFSET_LANE + 1]
            mix[rows, lanes] = (total[:, :DK] / weight).astype(BF)
            log_raw = top + jnp.log2(weight) * (1.0 / LOG_SCALE)
            aug[rows, lanes] = with_offsets(base, -log_raw)


def attend_back_into(size, heads, q, k, v, grad, mix, aug, key_aug, tri, dq, dk, dv):
    keys_aug = key_aug[...]
    length = k[0].shape[0]
    at = lambda ref, head: slice(ref[1] + head * DK, ref[1] + (head + 1) * DK)
    for head in range(heads):
        key = k[0][:, at(k, head)]
        keys = jnp.concatenate([key, keys_aug], axis=1)
        values = jnp.concatenate([v[0][:, at(v, head)], keys_aug], axis=1)
        grad_k = jnp.zeros((length, DK), F32)
        grad_v = jnp.zeros((length, DK), F32)
        for c in range(length // size):
            rows = slice(c * size, (c + 1) * size)
            query = q[0][rows, at(q, head)]
            slope_in = grad[0][rows, at(grad, head)]
            delta = jnp.sum(
                slope_in.astype(F32) * mix[0][rows, at(mix, head)].astype(F32),
                axis=1,
                keepdims=True,
            )
            queries = jnp.concatenate([query, aug[0][rows, at(aug, head)]], axis=1)
            grads = jnp.concatenate(
                [slope_in, with_offsets(jnp.zeros((size, DK), BF), -delta)], axis=1
            )
            weights, slopes = [], []
            for j in range(length // size):
                block = slice(j * size, (j + 1) * size)
                s = dot(keys[block], queries, NT)
                if tri is not None and j == c:
                    s = s + tri[...]
                p = jnp.exp2(s * LOG_SCALE)
                slope = p * dot(values[block], grads, NT)
                weights.append(p.astype(BF))
                slopes.append(slope.astype(BF))
            weights = jnp.concatenate(weights, axis=0)
            slopes = jnp.concatenate(slopes, axis=0)
            grad_v = grad_v + dot(weights, slope_in)
            grad_k = grad_k + dot(slopes, query)
            dq[0][rows, at(dq, head)] = (dot(slopes, key, TN) * SCALE).astype(BF)
        dk[0][:, at(dk, head)] = (grad_k * SCALE).astype(BF)
        dv[0][:, at(dv, head)] = grad_v.astype(BF)


GELU_A, GELU_B = math.sqrt(2.0 / math.pi), 0.044715


def gelu_and_slope(x):
    square = x * x
    t = jnp.tanh(GELU_A * x * (1.0 + GELU_B * square))
    half = 0.5 * (1.0 + t)
    slope = half + 0.5 * x * (1.0 - t * t) * (GELU_A * (1.0 + 3.0 * GELU_B * square))
    return x * half, slope


def norm_parts(stream):
    return lax.rsqrt(jnp.mean(stream * stream, axis=-1, keepdims=True) + EPS)


def norm_back_parts(stream, gain, gradient):
    root = norm_parts(stream)
    unit = stream * root
    scaled = gradient * gain
    inner = jnp.mean(scaled * unit, axis=-1, keepdims=True)
    return root * (scaled - unit * inner), gradient * unit


def gain_terms(terms):
    return jnp.sum(terms.reshape(terms.shape[0] // 8, 8, terms.shape[1]), axis=0)


VMEM_LIMIT = 60 * 1024 * 1024


def call_stage(kernel, name, number, inputs, outputs, scratch, flops):
    vmem = pl.BlockSpec(memory_space=pltpu.VMEM)
    hbm = pl.BlockSpec(memory_space=pl.ANY)
    return pl.pallas_call(
        kernel,
        in_specs=[vmem if near else hbm for _, near in inputs],
        out_specs=[vmem if near else hbm for _, _, near in outputs],
        out_shape=[jax.ShapeDtypeStruct(shape, kind) for shape, kind, _ in outputs],
        scratch_shapes=scratch,
        compiler_params=pltpu.CompilerParams(
            collective_id=number, has_side_effects=True, vmem_limit_bytes=VMEM_LIMIT
        ),
        cost_estimate=pl.CostEstimate(
            flops=flops, bytes_accessed=1 << 25, transcendentals=1 << 24
        ),
        name=name,
    )(*(array for array, _ in inputs))


def self_stage_kernel(n, *refs):
    (x, w_qkv, w_out, query_aug, key_aug, tri) = refs[:6]
    (total, full_out, qkv_out, mix_out, aug_out) = refs[6:11]
    (got, out, back, qkv, mix, aug) = refs[11:17]
    sems = refs[17:]
    rows, size = x.shape[:2]
    hid = w_out.shape[0]
    gather = Gather(n, x, got, *sems[:2])
    sums = Sums(n, out, back, *sems[2:4])
    save = sems[4]
    greet(n)

    def saves(r, which):
        for i in which:
            if i < n:
                pair = (gather.block(r, i), full_out.at[r, pl.ds(i * size, size)])
            else:
                ref, dst = ((qkv, qkv_out), (mix, mix_out), (aug, aug_out))[i - n]
                pair = (ref.at[r], dst.at[r])
            yield pltpu.make_async_copy(*pair, save.at[r, i])

    for r in range(rows):
        gather.start(r)
    gather.forward(0)

    @pl.loop(0, rows)
    def _(r):
        gather.finish(r)
        for j in range(n):
            qkv[r, j * size : (j + 1) * size, :] = dot(
                gather.block(r, j)[...], w_qkv[...]
            ).astype(BF)
        for copy in saves(r, range(n + 1)):
            copy.start()

        @pl.when(r > 0)
        def _():
            sums.forward(r - 1)

        row = qkv.at[r]
        attend_into(
            size,
            hid // DK,
            (row, 0),
            (row, hid),
            (row, 2 * hid),
            query_aug.at[r],
            key_aug.at[r],
            tri,
            mix.at[r],
            aug.at[r],
        )
        for copy in saves(r, range(n + 1, n + 3)):
            copy.start()

        @pl.when(r + 1 < rows)
        def _():
            gather.forward(r + 1)

        for j in reversed(range(n)):
            part = dot(mix[r, j * size : (j + 1) * size, :], w_out[...])
            if j:
                sums.put(r, j, part)
            else:
                total[r] = part

        @pl.when(r > 0)
        def _():
            total[r - 1] = sums.total(r - 1, total[r - 1])

    sums.forward(rows - 1)
    total[rows - 1] = sums.total(rows - 1, total[rows - 1])

    @pl.loop(0, rows)
    def _(r):
        gather.drain(r)
        sums.drain(r)
        for copy in saves(r, range(n + 3)):
            copy.wait()


def self_stage(n, x, w_qkv, w_out, query_aug, key_aug, tri):
    rows, size, width = x.shape
    length, hid = n * size, w_out.shape[0]
    slots = (rows, n - 1)
    return call_stage(
        functools.partial(self_stage_kernel, n),
        "self_stage",
        1,
        [(a, True) for a in (x, w_qkv, w_out, query_aug, key_aug, tri)],
        [
            ((rows, size, width), F32, True),
            ((rows, length, width), BF, False),
            ((rows, length, 3 * hid), BF, False),
            ((rows, length, hid), BF, False),
            ((rows, length, hid), BF, False),
        ],
        [
            *[pltpu.VMEM((*slots, size, width), BF)] * 3,
            pltpu.VMEM((rows, length, 3 * hid), BF),
            pltpu.VMEM((rows, length, hid), BF),
            pltpu.VMEM((rows, length, hid), BF),
            *[pltpu.SemaphoreType.DMA(slots)] * 4,
            pltpu.SemaphoreType.DMA((rows, n + 3)),
        ],
        rows * length * width * hid * 8 + rows * length * length * hid * 16,
    )


def self_back_kernel(n, *refs):
    (x, w_qkv, w_out, key_aug, tri_t, qkv_in, mix_in, aug_in) = refs[:8]
    (total, full_out, dqkv_out) = refs[8:11]
    (got, out, back, qkv, mix, aug, grad, dqkv) = refs[11:19]
    sems = refs[19:]
    rows, size = x.shape[:2]
    hid = w_out.shape[0]
    gather = Gather(n, x, got, *sems[:2])
    sums = Sums(n, out, back, *sems[2:4])
    save, load = sems[4:]
    greet(n)

    def loads(r):
        for i, (src, dst) in enumerate(((qkv_in, qkv), (mix_in, mix), (aug_in, aug))):
            yield pltpu.make_async_copy(src.at[r], dst.at[r], load.at[r, i])

    def saves(r, which):
        for i in which:
            if i < n:
                pair = (gather.block(r, i), full_out.at[r, pl.ds(i * size, size)])
            else:
                pair = (dqkv.at[r], dqkv_out.at[r])
            yield pltpu.make_async_copy(*pair, save.at[r, i])

    for r in range(rows):
        gather.start(r)
        for copy in loads(r):
            copy.start()
    gather.forward(0)

    @pl.loop(0, rows)
    def _(r):
        gather.finish(r)
        for j in range(n):
            grad[j * size : (j + 1) * size, :] = dot(
                gather.block(r, j)[...], w_out[...], NT
            ).astype(BF)
        for copy in saves(r, range(n)):
            copy.start()
        for copy in loads(r):
            copy.wait()

        @pl.when(r > 0)
        def _():
            sums.forward(r - 1)

        row, slope = qkv.at[r], dqkv.at[r]
        attend_back_into(
            size,
            hid // DK,
            (row, 0),
            (row, hid),
            (row, 2 * hid),
            (grad, 0),
            (mix.at[r], 0),
            (aug.at[r], 0),
            key_aug.at[r],
            tri_t,
            (slope, 0),
            (slope, hid),
            (slope, 2 * hid),
        )
        for copy in saves(r, range(n, n + 1)):
            copy.start()

        @pl.when(r + 1 < rows)
        def _():
            gather.forward(r + 1)

        for j in reversed(range(n)):
            part = dot(dqkv[r, j * size : (j + 1) * size, :], w_qkv[...], NT)
            if j:
                sums.put(r, j, part)
            else:
                total[r] = part

        @pl.when(r > 0)
        def _():
            total[r - 1] = sums.total(r - 1, total[r - 1])

    sums.forward(rows - 1)
    total[rows - 1] = sums.total(rows - 1, total[rows - 1])

    @pl.loop(0, rows)
    def _(r):
        gather.drain(r)
        sums.drain(r)
        for copy in saves(r, range(n + 1)):
            copy.wait()


def self_back_stage(n, x, w_qkv, w_out, key_aug, tri_t, qkv, mix, aug):
    rows, size, width = x.shape
    length, hid = n * size, w_out.shape[0]
    slots = (rows, n - 1)
    return call_stage(
        functools.partial(self_back_kernel, n),
        "self_back_stage",
        2,
        [(a, True) for a in (x, w_qkv, w_out, key_aug, tri_t)]
        + [(a, False) for a in (qkv, mix, aug)],
        [
            ((rows, size, width), F32, True),
            ((rows, length, width), BF, False),
            ((rows, length, 3 * hid), BF, False),
        ],
        [
            *[pltpu.VMEM((*slots, size, width), BF)] * 3,
            pltpu.VMEM((rows, length, 3 * hid), BF),
            pltpu.VMEM((rows, length, hid), BF),
            pltpu.VMEM((rows, length, hid), BF),
            pltpu.VMEM((length, hid), BF),
            pltpu.VMEM((rows, length, 3 * hid), BF),
            *[pltpu.SemaphoreType.DMA(slots)] * 4,
            pltpu.SemaphoreType.DMA((rows, n + 1)),
            pltpu.SemaphoreType.DMA((rows, 3)),
        ],
        rows * length * width * hid * 8 + rows * length * length * hid * 40,
    )


def middle_kernel(n, *refs):
    (x, cot, mid1, gain, w_gate, w_up, w_down, w_cross, query_aug, key_aug) = refs[:10]
    (mid2, third, full_a, full_b, full_cot, kv_out, q_out, mix_out, aug_out) = refs[10:19]
    (got_a, got_b, got_c, out, back, kv, q, mix, aug) = refs[19:28]
    sems = refs[28:]
    rows, size = x.shape[:2]
    hid = q.shape[2]
    enc = lax.axis_index("section") == 0
    gather_a = Gather(n, x, got_a, *sems[0:2])
    gather_b = Gather(n, third, got_b, *sems[2:4])
    gather_c = Gather(n, cot, got_c, *sems[4:6])
    sums = Sums(n, out, back, *sems[6:8])
    pair_send, pair_recv, save_a, save_b, save_c, save_x = sems[8:]
    greet(n, True)

    def block_saves(gather, dst, sem, r):
        for j in range(n):
            yield pltpu.make_async_copy(
                gather.block(r, j), dst.at[r, pl.ds(j * size, size)], sem.at[r, j]
            )

    def cross_saves(r):
        for i, (src, dst) in enumerate(
            ((kv, kv_out), (q, q_out), (mix, mix_out), (aug, aug_out))
        ):
            yield pltpu.make_async_copy(src.at[r], dst.at[r], save_x.at[r, i])

    def pair_copy(r):
        return pltpu.make_async_remote_copy(
            src_ref=kv.at[r],
            dst_ref=kv.at[r],
            send_sem=pair_send.at[r],
            recv_sem=pair_recv.at[r],
            device_id={"section": 1 - lax.axis_index("section")},
            device_id_type=MESH,
        )

    def finish(r):
        stream = mid1[r] + sums.total(r, mid2[r])
        mid2[r] = stream
        third[r] = (stream * norm_parts(stream) * gain[...]).astype(BF)

    for r in range(rows):
        gather_a.start(r)
    gather_a.forward(0)

    @pl.when(enc)
    def _():
        @pl.loop(0, rows)
        def _(r):
            gather_a.finish(r)
            for copy in block_saves(gather_a, full_a, save_a, r):
                copy.start()

            @pl.when(r > 0)
            def _():
                sums.forward(r - 1)

            for j in reversed(range(n)):
                block = gather_a.block(r, j)[...]
                gate = dot(block, w_gate[...])
                up = dot(block, w_up[...])
                hidden = (gelu_and_slope(gate)[0] * up).astype(BF)
                part = dot(hidden, w_down[...])
                if j:
                    sums.put(r, j, part)
                else:
                    mid2[r] = part

            @pl.when(r + 1 < rows)
            def _():
                gather_a.forward(r + 1)

            @pl.when(r > 0)
            def _():
                finish(r - 1)
                gather_b.start(r - 1)

        sums.forward(rows - 1)
        gather_b.forward(0)
        finish(rows - 1)
        gather_b.start(rows - 1)

        @pl.loop(0, rows)
        def _(r):
            gather_b.finish(r)
            for j in range(n):
                kv[r, j * size : (j + 1) * size, :] = dot(
                    gather_b.block(r, j)[...], w_cross[...]
                ).astype(BF)
            pair_copy(r).start()
            for copy in block_saves(gather_b, full_b, save_b, r):
                copy.start()

            @pl.when(r + 1 < rows)
            def _():
                gather_b.forward(r + 1)

        @pl.loop(0, rows)
        def _(r):
            gather_b.drain(r)
            pair_copy(r).wait_send()
            for copy in block_saves(gather_b, full_b, save_b, r):
                copy.wait()

    @pl.when(jnp.logical_not(enc))
    def _():
        for r in range(rows):
            gather_c.start(r)

        @pl.loop(0, rows)
        def _(r):
            gather_a.finish(r)
            for copy in block_saves(gather_a, full_a, save_a, r):
                copy.start()
            for j in range(n):
                q[r, j * size : (j + 1) * size, :] = dot(
                    gather_a.block(r, j)[...], w_cross[:, :hid]
                ).astype(BF)

            @pl.when(r + 1 < rows)
            def _():
                gather_a.forward(r + 1)

        @pl.loop(0, rows)
        def _(r):
            gather_c.forward(r)
            gather_c.finish(r)
            for copy in block_saves(gather_c, full_cot, save_c, r):
                copy.start()

        @pl.loop(0, rows)
        def _(r):
            pair_copy(r).wait_recv()

            @pl.when(r > 0)
            def _():
                sums.forward(r - 1)

            row = kv.at[r]
            attend_into(
                size,
                hid // DK,
                (q.at[r], 0),
                (row, 0),
                (row, hid),
                query_aug.at[r],
                key_aug.at[r],
                None,
                mix.at[r],
                aug.at[r],
            )
            for copy in cross_saves(r):
                copy.start()
            for j in reversed(range(n)):
                part = dot(mix[r, j * size : (j + 1) * size, :], w_cross[:, hid:], NT)
                if j:
                    sums.put(r, j, part)
                else:
                    mid2[r] = part

            @pl.when(r > 0)
            def _():
                finish(r - 1)

        sums.forward(rows - 1)
        finish(rows - 1)

        @pl.loop(0, rows)
        def _(r):
            gather_c.drain(r)
            for copy in block_saves(gather_c, full_cot, save_c, r):
                copy.wait()
            for copy in cross_saves(r):
                copy.wait()

    @pl.loop(0, rows)
    def _(r):
        gather_a.drain(r)
        sums.drain(r)
        for copy in block_saves(gather_a, full_a, save_a, r):
            copy.wait()


def middle_stage(n, x, cot, mid1, gain, w_gate, w_up, w_down, w_cross, query_aug, key_aug):
    rows, size, width = x.shape
    length, hid, ffd = n * size, w_cross.shape[1] // 2, w_gate.shape[1]
    slots = (rows, n - 1)
    full = ((rows, length, width), BF, False)
    head = ((rows, length, hid), BF, False)
    near = (x, cot, mid1, gain, w_gate, w_up, w_down, w_cross, query_aug, key_aug)
    return call_stage(
        functools.partial(middle_kernel, n),
        "middle_stage",
        3,
        [(a, True) for a in near],
        [
            ((rows, size, width), F32, True),
            ((rows, size, width), BF, True),
            full,
            full,
            full,
            ((rows, length, 2 * hid), BF, False),
            head,
            head,
            head,
        ],
        [
            *[pltpu.VMEM((*slots, size, width), BF)] * 5,
            pltpu.VMEM((rows, length, 2 * hid), BF),
            *[pltpu.VMEM((rows, length, hid), BF)] * 3,
            *[pltpu.SemaphoreType.DMA(slots)] * 8,
            *[pltpu.SemaphoreType.DMA((rows,))] * 2,
            *[pltpu.SemaphoreType.DMA((rows, n))] * 3,
            pltpu.SemaphoreType.DMA((rows, 4)),
        ],
        rows * length * width * ffd * 6 + rows * length * length * hid * 16,
    )


def middle_back_kernel(n, *refs):
    (third, cot, gain2, gain1, w_gate, w_up, w_down, w_cross, key_aug) = refs[:9]
    (mid1_in, mid2_in, fwd_in, cot_in, kv_in, q_in, mix_in, aug_in) = refs[9:17]
    (grad, gain_out, parts_out, full_3, full_g) = refs[17:22]
    (hidden_out, dgate_out, dup_out, dkv_out, dq_out) = refs[22:27]
    (own, got, out, back, rest, dkv) = refs[27:33]
    (mid, full, kv, q, mix, aug, dq, hidden_s, dgate_s, dup_s, part_s) = refs[33:44]
    sems = refs[44:]
    rows, size = third.shape[:2]
    hid = q.shape[1]
    enc = lax.axis_index("section") == 0
    gather_3 = Gather(n, third, got, *sems[0:2])
    gather_g = Gather(n, own, got, *sems[2:4])
    sums_a = Sums(n, out, back, *sems[4:6])
    sums_b = Sums(n, out, back, *sems[6:8])
    pair_send, pair_recv, save_3, save_g, save_f, save_p, save_d, load_m, load_f, load_x = sems[8:]
    greet(n, True)
    gain_out[...] = jnp.zeros_like(gain_out)

    def block_saves(gather, dst, sem, r):
        for j in range(n):
            yield pltpu.make_async_copy(
                gather.block(r, j), dst.at[r, pl.ds(j * size, size)], sem.at[r, j]
            )

    def pair_copy(r):
        return pltpu.make_async_remote_copy(
            src_ref=dkv.at[r],
            dst_ref=dkv.at[r],
            send_sem=pair_send.at[r],
            recv_sem=pair_recv.at[r],
            device_id={"section": 1 - lax.axis_index("section")},
            device_id_type=MESH,
        )

    def mid_load(i, source, r):
        return pltpu.make_async_copy(source.at[r], mid.at[i], load_m.at[i])

    def full_load(source, r):
        return pltpu.make_async_copy(source.at[r], full, load_f.at[0])

    def cross_loads(r):
        for i, (src, dst) in enumerate(((kv_in, kv), (q_in, q), (mix_in, mix), (aug_in, aug))):
            yield pltpu.make_async_copy(src.at[r], dst, load_x.at[i])

    def ffn_saves(r):
        for i, (src, dst) in enumerate(
            ((hidden_s, hidden_out), (dgate_s, dgate_out), (dup_s, dup_out))
        ):
            yield pltpu.make_async_copy(src, dst.at[r], save_f.at[r, i])

    def part_save(r, j):
        return pltpu.make_async_copy(
            part_s.at[j], parts_out.at[r, pl.ds(j * size, size)], save_p.at[j]
        )

    def feed_forward(r, normed_of, grad_of, sums, with_out):
        @pl.when(r > 0)
        def _():
            for copy in ffn_saves(r - 1):
                copy.wait()

        for j in reversed(range(n)):
            at = slice(j * size, (j + 1) * size)
            normed, slope_in = normed_of(j), grad_of(j)
            gate = dot(normed, w_gate[...])
            up = dot(normed, w_up[...])
            active, slope = gelu_and_slope(gate)
            hidden = (active * up).astype(BF)
            hidden_s[at, :] = hidden
            back_hidden = dot(slope_in, w_down[...], NT)
            dgate = (back_hidden * up * slope).astype(BF)
            dup = (back_hidden * active).astype(BF)
            dgate_s[at, :] = dgate
            dup_s[at, :] = dup
            part = dot(dgate, w_gate[...], NT) + dot(dup, w_up[...], NT)
            if j:
                sums.put(r, j, part)
            else:
                rest[r] = part
            if with_out:
                part = dot(hidden, w_down[...]).astype(BF)

                @pl.when(r > 0)
                def _():
                    part_save(r - 1, j).wait()

                part_s[j] = part
                part_save(r, j).start()
        for copy in ffn_saves(r):
            copy.start()

    def finish_third(r, sums, add_cot):
        mid_load(0, mid2_in, r).wait()
        arriving = sums.total(r, rest[r])
        if add_cot:
            arriving = arriving + cot[r].astype(F32)
        part, terms = norm_back_parts(mid[0], gain2[...], arriving)
        gain_out[0] += gain_terms(terms)
        if not add_cot:
            part = part + cot[r].astype(F32)
        grad[r] = part
        own[r] = part.astype(BF)

    def finish_second(r, sums):
        mid_load(1, mid1_in, r).wait()
        part, terms = norm_back_parts(mid[1], gain1[...], sums.total(r, rest[r]))
        gain_out[1] += gain_terms(terms)
        grad[r] = grad[r] + part

    last = rows - 1

    @pl.when(jnp.logical_not(enc))
    def _():
        for r in range(rows):
            gather_3.start(r)
        full_load(cot_in, 0).start()
        gather_3.forward(0)

        @pl.loop(0, rows)
        def _(r):
            gather_3.finish(r)
            for copy in block_saves(gather_3, full_3, save_3, r):
                copy.start()
            full_load(cot_in, r).wait()

            @pl.when(r > 0)
            def _():
                gather_3.drain(r - 1)
                sums_a.forward(r - 1)
                mid_load(0, mid2_in, r - 1).start()

            for copy in block_saves(gather_3, full_3, save_3, r):
                copy.wait()
            feed_forward(
                r,
                lambda j: gather_3.block(r, j)[...],
                lambda j: full[j * size : (j + 1) * size, :],
                sums_a,
                True,
            )

            @pl.when(r + 1 < rows)
            def _():
                full_load(cot_in, r + 1).start()
                gather_3.forward(r + 1)

            @pl.when(r > 0)
            def _():
                finish_third(r - 1, sums_a, False)
                gather_g.start(r - 1)

        gather_3.drain(last)
        sums_a.forward(last)
        mid_load(0, mid2_in, last).start()
        for copy in cross_loads(0):
            copy.start()
        gather_g.forward(0)
        finish_third(last, sums_a, False)
        gather_g.start(last)

        @pl.loop(0, rows)
        def _(r):
            gather_g.finish(r)
            for copy in block_saves(gather_g, full_g, save_g, r):
                copy.start()
            for j in range(n):
                at = slice(j * size, (j + 1) * size)
                full[at, :hid] = dot(gather_g.block(r, j)[...], w_cross[:, hid:]).astype(BF)
            for copy in cross_loads(r):
                copy.wait()

            @pl.when(r > 0)
            def _():
                pltpu.make_async_copy(dq, dq_out.at[r - 1], save_d.at[0]).wait()
                sums_b.forward(r - 1)
                mid_load(1, mid1_in, r - 1).start()

            attend_back_into(
                size,
                hid // DK,
                (q, 0),
                (kv, 0),
                (kv, hid),
                (full, 0),
                (mix, 0),
                (aug, 0),
                key_aug.at[r],
                None,
                (dq, 0),
                (dkv.at[r], 0),
                (dkv.at[r], hid),
            )
            pair_copy(r).start()
            pltpu.make_async_copy(dq, dq_out.at[r], save_d.at[0]).start()

            @pl.when(r + 1 < rows)
            def _():
                for copy in cross_loads(r + 1):
                    copy.start()
                gather_g.forward(r + 1)

            sums_a.drain(r)
            for j in reversed(range(n)):
                part = dot(dq[j * size : (j + 1) * size, :], w_cross[:, :hid], NT)
                if j:
                    sums_b.put(r, j, part)
                else:
                    rest[r] = part

            @pl.when(r > 0)
            def _():
                finish_second(r - 1, sums_b)

        sums_b.forward(last)
        mid_load(1, mid1_in, last).start()
        finish_second(last, sums_b)

        @pl.loop(0, rows)
        def _(r):
            pair_copy(r).wait_send()

        for j in range(n):
            part_save(last, j).wait()
        pltpu.make_async_copy(dq, dq_out.at[last], save_d.at[0]).wait()

    @pl.when(enc)
    def _():
        full_load(fwd_in, 0).start()

        @pl.loop(0, rows + 1)
        def _(t):
            @pl.when(t < rows)
            def _():
                mid_load(0, mid2_in, t).start()
                pair_copy(t).wait_recv()
                pltpu.make_async_copy(dkv.at[t], dkv_out.at[t], save_d.at[1 + t]).start()
                for j in reversed(range(n)):
                    at = slice(j * size, (j + 1) * size)
                    part = dot(dkv[t, at, :], w_cross[...], NT)
                    if j:
                        sums_a.put(t, j, part)
                    else:
                        rest[t] = part
                sums_a.forward(t)

            @pl.when(t > 0)
            def _():
                r = t - 1
                mid_load(1, mid1_in, r).start()
                gather_g.forward(r)
                gather_g.finish(r)
                for copy in block_saves(gather_g, full_g, save_g, r):
                    copy.start()
                full_load(fwd_in, r).wait()
                sums_a.drain(r)
                feed_forward(
                    r,
                    lambda j: full[j * size : (j + 1) * size, :],
                    lambda j: gather_g.block(r, j)[...],
                    sums_b,
                    False,
                )

                @pl.when(r + 1 < rows)
                def _():
                    full_load(fwd_in, r + 1).start()

            @pl.when(t < rows)
            def _():
                finish_third(t, sums_a, True)
                gather_g.start(t)

            @pl.when(t > 0)
            def _():
                sums_b.forward(t - 1)
                finish_second(t - 1, sums_b)

        @pl.loop(0, rows)
        def _(r):
            pltpu.make_async_copy(dkv.at[r], dkv_out.at[r], save_d.at[1 + r]).wait()

    for copy in ffn_saves(last):
        copy.wait()

    @pl.loop(0, rows)
    def _(r):
        gather_g.drain(r)
        sums_b.drain(r)
        for copy in block_saves(gather_g, full_g, save_g, r):
            copy.wait()


def middle_back_stage(
    n,
    third,
    cot,
    gain2,
    gain1,
    w_gate,
    w_up,
    w_down,
    w_cross,
    key_aug,
    mid1,
    mid2,
    fwd,
    full_cot,
    kv,
    q,
    mix,
    aug,
):
    rows, size, width = third.shape
    length, hid, ffd = n * size, w_cross.shape[1] // 2, w_gate.shape[1]
    slots = (rows, n - 1)
    full = ((rows, length, width), BF, False)
    unit = ((rows, length, ffd), BF, False)
    near = (third, cot, gain2, gain1, w_gate, w_up, w_down, w_cross, key_aug)
    return call_stage(
        functools.partial(middle_back_kernel, n),
        "middle_back_stage",
        4,
        [(a, True) for a in near]
        + [(a, False) for a in (mid1, mid2, fwd, full_cot, kv, q, mix, aug)],
        [
            ((rows, size, width), F32, True),
            ((2, 8, width), F32, True),
            full,
            full,
            full,
            unit,
            unit,
            unit,
            ((rows, length, 2 * hid), BF, False),
            ((rows, length, hid), BF, False),
        ],
        [
            pltpu.VMEM((rows, size, width), BF),
            *[pltpu.VMEM((*slots, size, width), BF)] * 3,
            pltpu.VMEM((rows, size, width), F32),
            pltpu.VMEM((rows, length, 2 * hid), BF),
            pltpu.VMEM((2, size, width), F32),
            pltpu.VMEM((length, width), BF),
            pltpu.VMEM((length, 2 * hid), BF),
            *[pltpu.VMEM((length, hid), BF)] * 4,
            *[pltpu.VMEM((length, ffd), BF)] * 3,
            pltpu.VMEM((n, size, width), BF),
            *[pltpu.SemaphoreType.DMA(slots)] * 8,
            *[pltpu.SemaphoreType.DMA((rows,))] * 2,
            *[pltpu.SemaphoreType.DMA((rows, n))] * 2,
            pltpu.SemaphoreType.DMA((rows, 3)),
            pltpu.SemaphoreType.DMA((n,)),
            pltpu.SemaphoreType.DMA((rows + 1,)),
            pltpu.SemaphoreType.DMA((2,)),
            pltpu.SemaphoreType.DMA((1,)),
            pltpu.SemaphoreType.DMA((4,)),
        ],
        rows * length * width * ffd * 16 + rows * length * length * hid * 40,
    )


def body(
    block_input, cotangent, segments, attn_weight, attn_out, ffn_in, ffn_out, cross_weight, gains
):
    enc = lax.axis_index("section") == 0
    idx = lax.axis_index("mp")
    n = lax.axis_size("mp")
    dp_size = lax.axis_size("dp")
    bits = [1 << b for b in range(n.bit_length() - 1)]
    size, row_count, width = block_input.shape[1:]
    length = size * n
    hid = attn_weight.shape[3]
    ffd = ffn_in.shape[3]
    rows = range(row_count)

    w_qkv = attn_weight[0].reshape(width, 3 * hid)
    w_out = attn_out[0]
    w_gate, w_up = ffn_in[0, :, 0], ffn_in[0, :, 1]
    w_down = ffn_out[0]
    w_cross = cross_weight[0].reshape(width, 2 * hid)
    gain = gains[0]
    x_low = jnp.swapaxes(block_input[0], 0, 1)
    x = x_low.astype(F32)
    cot = jnp.swapaxes(cotangent[0], 0, 1)

    order = jnp.arange(n, dtype=jnp.int32) ^ idx
    block_of = jnp.repeat(order, size)[:, None]
    lane = jnp.arange(DK, dtype=jnp.int32)
    local = jnp.concatenate(
        [lax.dynamic_slice_in_dim(segments, (idx ^ j) * size, size, axis=2) for j in range(n)],
        axis=2,
    )[..., None]
    own = jnp.where(enc, local[0], local[1])

    def query_features(seg, causal):
        doc = (lane < DOC_LANES) & (lane != seg)
        later = (lane >= BLOCK_LANE) & (lane < BLOCK_LANE + n)
        later = later & (lane - BLOCK_LANE > block_of) & causal
        return jnp.where(doc | later, BIG, 0.0).astype(BF)

    def key_features(seg):
        doc = (lane < DOC_LANES) & (lane == seg)
        ones = (lane >= OFFSET_LANE) & (lane < OFFSET_LANE + 3)
        place = lane - BLOCK_LANE == block_of
        return jnp.where(doc | ones | place, 1.0, 0.0).astype(BF)

    above = jnp.arange(size)[None, :] > jnp.arange(size)[:, None]
    tri = jnp.where(above & ~enc, BIG, 0.0).astype(F32)
    key_own, key_enc = key_features(own), key_features(local[0])

    sum1, full1, qkv1, mix1, aug1 = self_stage(
        n,
        norm_scale(x, gain[0]).astype(BF),
        w_qkv,
        w_out,
        query_features(own, ~enc),
        key_own,
        tri,
    )
    mid1 = x + sum1
    mid2, third, full_a, full_b, full_cot, kv, q, mix, aug = middle_stage(
        n,
        norm_scale(mid1, gain[1]).astype(BF),
        cot,
        mid1,
        gain[2:3],
        w_gate,
        w_up,
        w_down,
        w_cross,
        query_features(local[1], False),
        key_enc,
    )

    grad1, gain_parts, parts, full_3, full_g, hidden, dgate, dup, dkv, dq = middle_back_stage(
        n,
        third,
        cot,
        gain[2:3],
        gain[1:2],
        w_gate,
        w_up,
        w_down,
        w_cross,
        key_enc,
        mid1,
        mid2,
        full_a,
        full_cot,
        kv,
        q,
        mix,
        aug,
    )

    def contract(left, right):
        return lax.dot_general(
            left, right, (((0, 1), (0, 1)), ((), ())), preferred_element_type=F32
        ).astype(BF)

    def over_rows(total):
        return lax.psum_scatter(total, "dp", scatter_dimension=0, tiled=True).astype(F32)

    sum_ffn = lax.cond(
        enc,
        lambda: jnp.concatenate(
            [contract(full_a, dgate), contract(full_a, dup), contract(full_g, hidden)], axis=1
        ),
        lambda: jnp.concatenate(
            [contract(full_3, dgate), contract(full_3, dup), contract(full_cot, hidden)], axis=1
        ),
    )
    sum_cross = lax.cond(
        enc,
        lambda: contract(full_b, dkv),
        lambda: jnp.concatenate([contract(full_a, dq), contract(full_g, mix)], axis=1),
    )
    sum2, full_s, dqkv = self_back_stage(
        n, grad1.astype(BF), w_qkv, w_out, key_own, tri.T, qkv1, mix1, aug1
    )
    part, gain_first = norm_back(x, gain[0], sum2)
    input_grad = grad1 + part

    def across(tensor, bit):
        return lax.ppermute(tensor, "mp", [(i, i ^ bit) for i in range(n)])

    have = {j: parts[:, j * size : (j + 1) * size] for j in range(n)}
    for bit in bits:
        for j in sorted((j for j in have if j & bit), reverse=True):
            came = across(have.pop(j), bit)
            total = have[j ^ bit].astype(F32) + came.astype(F32)
            have[j ^ bit] = total if len(have) == 1 else total.astype(BF)
    block_out = jnp.where(enc, third, (mid2 + have[0].astype(F32)).astype(BF))

    sum_attn = jnp.concatenate([contract(full1, dqkv), contract(full_s, mix1), sum_cross], axis=1)
    quarter = width // dp_size
    got_ffn = over_rows(sum_ffn)
    got_attn = over_rows(sum_attn)
    out_in = jnp.stack([got_ffn[:, :ffd], got_ffn[:, ffd : 2 * ffd]], axis=1)
    out_down = got_ffn[:, 2 * ffd :].T
    out_qkv = got_attn[:, : 3 * hid].reshape(quarter, 3, hid)
    out_out = got_attn[:, 3 * hid : 4 * hid].T
    out_cross = got_attn[:, 4 * hid :].reshape(quarter, 2, hid)
    gain_parts = jnp.sum(gain_parts, axis=1)
    gain_total = lax.psum_scatter(
        jnp.stack([gain_first, gain_parts[1], gain_parts[0]]),
        ("dp", "mp"),
        scatter_dimension=1,
        tiled=True,
    )
    return (
        jnp.swapaxes(block_out, 0, 1)[None],
        jnp.swapaxes(input_grad, 0, 1)[None],
        out_qkv[None],
        out_out[None],
        out_in[None],
        out_down[None],
        out_cross[None],
        gain_total[None],
    )


def solution(mesh):
    in_specs = (
        P("section", "mp", "dp", None),
        P("section", "mp", "dp", None),
        P(None, "dp", None),
        P("section", None, None, "mp"),
        P("section", "mp", None),
        P("section", None, None, "mp"),
        P("section", "mp", None),
        P("section", None, None, "mp"),
        P("section", None, None),
    )
    out_specs = (
        P("section", "mp", "dp", None),
        P("section", "mp", "dp", None),
        P("section", "dp", None, "mp"),
        P("section", "mp", "dp"),
        P("section", "dp", None, "mp"),
        P("section", "mp", "dp"),
        P("section", "dp", None, "mp"),
        P("section", None, ("dp", "mp")),
    )
    return jax.shard_map(body, mesh=mesh, in_specs=in_specs, out_specs=out_specs, check_vma=False)
```

time: 1160 us -> 894 us (0.77)
  Pallas kernels: 265 us -> 542 us
  matrix products: 223 us -> 40.1 us
  other arithmetic: 139 us -> 43.2 us
  local copies, waits for them, and re-layouts: 111 us -> 24.1 us
  starting transfers between devices: 85.2 us -> 0.9 us
  waiting for transfers between devices: 295 us -> 220 us
    pallas_call x16 -> x4, Pallas kernels: 265 us -> 542 us  [call_stage(): pl.pallas_call(kernel, in_specs=[vmem if near else hbm for _, near in inp...]
    dot_general x111 -> x7, matrix products: 223 us -> 40.1 us  [contract(): lax.dot_general(left, right, (((0, 1), (0, 1)), ((), ())), preferred_elem...]
    ppermute x76 -> x3, waiting for transfers between devices: 137 us -> 4.36 us  [across(): return lax.ppermute(tensor, 'mp', [(i, i ^ bit) for i in range(n)])]
    unnamed x7 -> x4, waiting for transfers between devices: 0.1 us -> 84.2 us
    ppermute x9 -> x0, waiting for transfers between devices: 65 us -> none  [the longest x3 54.4 us: body(): mem_full.append(gather(lax.ppermute(memory[r], 'section', [(0, 1)]), bits))]
    ppermute x9 -> x0, starting transfers between devices: 49.7 us -> none  [the longest x1 37.6 us: body(): sum_kv = lax.ppermute(over_outer(sum_kv), 'section', [(1, 0)])]
    reduce_scatter x5 -> x2, waiting for transfers between devices: 93.1 us -> 132 us  [over_rows(): lax.psum_scatter(total, 'dp', scatter_dimension=0, tiled=True).astype(F32)]
    convert_element_type x23 -> x6, other arithmetic: 47.6 us -> 13 us  [the longest x1 3.36 us: body(): norm_scale(mid1, gain[1]).astype(BF)]
  transfers between devices with their start and end apart: 91 -> 6, of which waited for: 20 -> 4; matrix products, arithmetic and copies ran while one was open for 36% -> 7% of each run, Pallas kernels for 23% -> 0%
where the time goes in v2:
time: 894 us; the launch traced here: 889 us
  Pallas kernels  542 us (61%)
  waiting for transfers between devices  220 us (25%)
  other arithmetic  43.2 us (5%)
  matrix products  40.1 us (4%)
  local copies, waits for them, and re-layouts  24.1 us (3%)
  between operations  14.4 us (2%)
    pallas_call x4, Pallas kernels, call_stage(): pl.pallas_call(kernel, in_specs=[vmem if near else hbm for _, near in inp...  542 us
    reduce_scatter x2, waiting for transfers between devices, over_rows(): lax.psum_scatter(total, 'dp', scatter_dimension=0, tiled=True).astype(F32)  132 us
    unnamed x4, waiting for transfers between devices  84.2 us
    dot_general x7, matrix products, contract(): lax.dot_general(left, right, (((0, 1), (0, 1)), ((), ())), preferred_elem...  40.1 us
  transfers between devices with their start and end apart: 6, of which 4 were waited for; matrix products, arithmetic and copies ran while one was open for 7% of the time, Pallas kernels for 0%

profile of v2, /device:TPU:2, one launch (start us, length us, event | category | flops | bytes accessed | tf_op | source)
XLA Modules:
  0.0 889.2 jit_solution(16739827538148754911)
XLA Ops:
  7.2 0.0 reduce-scatter.10.cloned.1.call-start
  7.3 0.8 constant_dynamic-slice_fusion
  8.1 0.7 fusion.28.refs_5_
  8.9 0.7 fusion.30.refs_4_
  9.6 1.3 slice_bitcast_fusion.7
  10.9 1.8 fusion.13
  12.7 0.6 copy-done.10
  13.3 1.8 copy.59
  15.1 1.6 copy.64.refs_1_
  16.7 0.1 broadcast_bitcast_fusion
  16.8 1.6 fusion.11.refs_0_
  18.4 0.2 broadcast_compare_fusion
  18.6 4.3 select_convert_fusion
  23.0 79.5 %self_stage.1 = (f32[3,256,1024]{2,1,0:T(8,128)}, bf16[3,1024,1024]{2,1,0:T(8,128)(2,1)}, bf16[3,1024,768]{2,1,0:T(8,128)(2,1)}, bf16[3,1024,256]{2,1,0:T(8,128)(2,1)}, bf16[3,1024,256]{2,1,0:T(8,128)(2,1)}) custom-call(bf16[3,256,1024]{2,1,0:T(8,128)(2,1)} %fusion.11.refs_0_, bf16[1024,768]{1,0:T(8,128)(2,1)} %copy.64.refs_1_, bf16[256,1024]{1,0:T(8,128)(2,1)} %bitcast.165, ...), custom_call_target="tpu_custom_call" | custom-call | flops 19327352832 | bytes 33554432 | tf_op jit(solution)/shard_map/self_stage/pallas_call | solution.py:273
  102.5 4.1 multiply_reduce_fusion
  106.6 1.4 fusion.34
  108.0 2.6 copy.99
  110.5 1.6 copy.100
  112.1 2.4 copy.102
  114.5 3.4 multiply_convert_fusion.refs_0_
  117.9 195.3 %middle_stage.1 = (f32[3,256,1024]{2,1,0:T(8,128)}, bf16[3,256,1024]{2,1,0:T(8,128)(2,1)}, bf16[3,1024,1024]{2,1,0:T(8,128)(2,1)}, bf16[3,1024,1024]{2,1,0:T(8,1...) custom-call(bf16[3,256,1024]{2,1,0:T(8,128)(2,1)} %multiply_convert_, ...), custom_call_target="tpu_custom_call" | custom-call | flops 26172456960 | bytes 33554432 | tf_op jit(solution)/shard_map/middle_stage/pallas_call | solution.py:273
  313.2 186.2 %middle_back_stage.1 = (f32[3,256,1024]{2,1,0:T(8,128)}, f32[2,8,1024]{2,1,0:T(8,128)}, bf16[3,1024,1024]{2,1,0:T(8,128)(2,1)}, bf16[3,1024,1024]{2,1,0:T(8,128)...) custom-call(bf16[3,256,1024]{2,1,0:T(8,128)(2,1)} %get-tuple-element, ...), custom_call_target="tpu_custom_call" | custom-call | flops 67645734912 | bytes 33554432 | tf_op jit(solution)/shard_map/middle_back_stage/pallas_call | solution.py:273
  499.4 3.3 convert_element_type.118.refs_0_
  502.7 80.8 %self_back_stage.1 = (f32[3,256,1024]{2,1,0:T(8,128)}, bf16[3,1024,1024]{2,1,0:T(8,128)(2,1)}, bf16[3,1024,768]{2,1,0:T(8,128)(2,1)}) custom-call(bf16[3,256,1024]{2,1,0:T(8,128)(2,1)} %convert_element_type.118.refs_0_, bf16[1024,768]{1,0:T(8,128)(2,1)} %copy.64.refs_1_, bf16[256,1024]{1,0:T(8,128)(2,1)} %bitcast.166, ...), custom_call_target="tpu_custom_call" | custom-call | flops 38654705664 | bytes 33554432 | tf_op jit(solution)/shard_map/self_back_stage/pallas_call | solution.py:273
  583.5 3.1 fusion.12
  586.6 1.0 copy.93
  587.6 0.0 reduce-scatter.10.cloned.1.call-update
  587.7 0.0 reduce-scatter.6.cloned.1.call-start
  587.7 5.2 fusion.26
  593.0 9.5 %bitcast_convert_fusion.7 = bf16[1024,768]{0,1:T(8,128)(2,1)} fusion(bf16[3,1024,1024]{2,1,0:T(8,128)(2,1)} %get-tuple-element.104, bf16[3,1024,768]{2,1,0:T(8,128)(2,1)} %get-tuple-element.105), kind=kOutput, calls=%fused_computation.18 | convolution fusion | flops 4832624640 | bytes 12582912 | tf_op jit(solution)/shard_map/dot_general | solution.py:1196
  602.5 7.1 conditional.2
  602.5 4.8 fusion.1
  607.3 1.9 fusion
  609.1 0.1 pad_maximum_fusion
  609.6 3.0 pad_maximum_fusion.3
  612.6 0.0 reduce-scatter.6.cloned.1.call-update
  612.6 0.0 reduce-scatter.8.cloned.1.call-start
  612.7 25.5 %conditional.3 = (bf16[1024,2112]{0,1:T(8,128)(2,1)}) conditional(s32[]{:T(128)} %convert_element_type.121, (bf16[3,1024,1024]{2,1,0:T(8,128)(2,1)}, bf16[3,1024,704]{2,1,0:T(8,128)(2,1)}, bf16[3,1024,704]{2,1,0:T(8,128)(2,1)}, bf16[3,1024,1024]{2,1,0:T(8,128)(2,1)}, bf16[3,1024,704]{2,1,0:T(8,128)(2,1)}) %tuple.22, ...), branch_computations={%region_6.7_spmd, %region_7.8_spmd} | conditional | flops 13302693888 | bytes 101449840 | solution.py:1203
  612.7 9.0 %bitcast_convert_fusion.1 = bf16[1024,704]{0,1:T(8,128)(2,1)S(1)} fusion(bf16[3,1024,1024]{2,1,0:T(8,128)(2,1)} %get-tuple-element.47, bf16[3,1024,704]{2,1,0:T(8,128)(2,1)} %get-tuple-element.174), kind=kOutput, calls=%fused_computation.7 | convolution fusion | flops 4429905920 | bytes 12058624 | tf_op jit(solution)/shard_map/cond/branch_0_fun/dot_general | solution.py:1196
  621.7 4.9 bitcast_convert_fusion.2
  626.7 4.9 bitcast_convert_fusion.3
  631.6 2.4 pad_maximum_fusion.1
  638.2 0.0 reduce-scatter.8.cloned.1.call-update
  638.2 2.4 fusion.33
  640.7 0.1 collective-permute-start.1
  640.8 0.5 collective-permute-start
  641.3 4.4 collective-permute-done.1
  645.6 3.2 add_convert_fusion.1
  648.9 0.2 collective-permute-start.2
  649.1 2.5 fusion.3
  651.6 84.2 %reduce-scatter.10.cloned.1.call-done = f32[64,3]{1,0:T(8,128)} async-done(((f32[1024,3]{1,0:T(8,128)}), f32[64,3]{1,0:T(8,128)}) %reduce-scatter.10.cloned.1.call-update) | async-done | bytes 784
  735.7 0.8 copy.94
  736.6 0.6 copy.81
  737.2 6.0 fusion.16
  743.2 54.3 %reduce-scatter.6.cloned.1.call-done = bf16[256,1536]{0,1:T(8,128)(2,1)} async-done(((bf16[1024,1536]{0,1:T(8,128)(2,1)}), bf16[256,1536]{0,1:T(8,128)(2,1)}) %reduce-scatter.6.cloned.1.call-update) | async-done | bytes 786448 | tf_op jit(solution)/shard_map/reduce_scatter | solution.py:1201
  797.5 1.1 slice.94
  798.6 1.1 copy.79
  799.8 1.0 copy.80
  800.8 0.1 convert_element_type.122
  800.9 0.7 slice_bitcast_fusion.3
  801.6 77.2 %reduce-scatter.8.cloned.1.call-done = bf16[256,2112]{0,1:T(8,128)(2,1)} async-done(((bf16[1024,2112]{0,1:T(8,128)(2,1)}), bf16[256,2112]{0,1:T(8,128)(2,1)}) %reduce-scatter.8.cloned.1.call-update) | async-done | bytes 1081360 | tf_op jit(solution)/shard_map/reduce_scatter | solution.py:1201
  878.8 1.4 convert_element_type.123
  880.2 1.0 slice_bitcast_fusion
  881.2 1.2 maximum_bitcast_fusion
  (60 shorter events, 0.3 us)
Async XLA Ops:
  7.2 728.6 %reduce-scatter.10.cloned.1.call-start = ((), (), s32[]{:S(2)}) async-start(), calls=%async_computation.5 | async-start | bytes 557056
  10.9 5.9 copy-start.5
  12.7 0.6 copy-start.10
  13.3 3.5 copy-start.7
  13.3 3.5 copy-start
  102.4 4.1 copy-start.4
  313.2 186.2 %copy-start.14 = (bf16[3,1024,256]{2,1,0:T(8,128)(2,1)}, bf16[3,1024,256]{2,1,0:T(8,128)(2,1)S(1)}, u32[]{:S(2)}) copy-start(bf16[3,1024,256]{2,1,0:T(8,128)(2,1)S(1)} %get-tuple-element.96.refs_15_) | copy-start | bytes 4718596
  502.7 80.8 %copy-start.6 = (f32[1,1,1024]{2,0,1:T(1,128)S(1)}, f32[1,1,1024]{2,0,1:T(1,128)}, u32[]{:S(2)}) copy-start(f32[1,1,1024]{2,0,1:T(1,128)} %copy-done.5) | copy-start | bytes 12292
  502.7 80.8 %copy-start.8 = (f32[3,256]{1,0:T(4,128)S(1)}, f32[3,256]{1,0:T(4,128)}, u32[]{:S(2)}) copy-start(f32[3,256]{1,0:T(4,128)} %copy-done.7) | copy-start | bytes 9220
  583.4 3.1 copy-start.9
  587.7 209.8 %reduce-scatter.6.cloned.1.call-start = ((), (), s32[]{:S(2)}) async-start(), calls=%async_computation.3 | async-start | bytes 3932160 | tf_op jit(solution)/shard_map/reduce_scatter | solution.py:1201
  587.7 5.2 copy-start.15
  587.7 5.2 copy-start.16
  602.5 4.8 copy-start.12
  612.6 266.2 %reduce-scatter.8.cloned.1.call-start = ((), (), s32[]{:S(2)}) async-start(), calls=%async_computation.4 | async-start | bytes 5406720 | tf_op jit(solution)/shard_map/reduce_scatter | solution.py:1201
  612.7 9.0 %copy-start.17 = (bf16[3,1024,1024]{2,1,0:T(8,128)(2,1)S(1)}, bf16[3,1024,1024]{2,1,0:T(8,128)(2,1)}, u32[]{:S(2)}) copy-start(bf16[3,1024,1024]{2,1,0:T(8,128)(2,1)} %get-tuple-element.44) | copy-start | bytes 18874372 | tf_op jit(solution)/shard_map/cond
  612.7 9.0 %copy-start.18 = (bf16[3,1024,704]{2,1,0:T(8,128)(2,1)S(1)}, bf16[3,1024,704]{2,1,0:T(8,128)(2,1)}, u32[]{:S(2)}) copy-start(bf16[3,1024,704]{2,1,0:T(8,128)(2,1)} %get-tuple-element.172) | copy-start | bytes 12976132 | tf_op jit(solution)/shard_map/cond
  612.7 13.9 %slice-start = ((s8[4718592]{0:T(1024)(128)(4,1)}), s8[4194304]{0:T(1024)(128)(4,1)S(1)}, s32[]{:S(2)}) async-start(s8[4718592]{0:T(1024)(128)(4,1)} %bitcast.167), calls=%async_computation.6 | async-start | bytes 8388608 | tf_op jit(solution)/shard_map/cond
  621.7 4.9 slice-start.1
  638.2 10.9 %copy-start.2 = (f32[3,256,1024]{2,1,0:T(8,128)S(1)}, f32[3,256,1024]{2,1,0:T(8,128)}, u32[]{:S(2)}) copy-start(f32[3,256,1024]{2,1,0:T(8,128)} %get-tuple-element.103) | copy-start | bytes 9437188
  640.7 8.4 copy-start.11
  640.7 8.4 copy-start.1
  640.7 4.9 collective-permute-start.1
  640.8 96.4 %collective-permute-start = (bf16[3,256,1024]{2,1,0:T(8,128)(2,1)S(1)}, bf16[3,256,1024]{2,1,0:T(8,128)(2,1)}, u32[]{:S(2)}, u32[]{:S(2)}) collective-permute-start(bf16[3,256,1024]{2,1,0:T(8,128)(2,1)S(1)} %get-tuple-element.192), channel_id=1, source_target_pairs={{0,1},{1,0},{2,3},{3,2},{4,5},{5,4},{6,7},{7,6},{8,9},{9,8},{10,11... | collective-permute-start | bytes 4718600 | tf_op jit(solution)/shard_map/ppermute | solution.py:1224
  648.9 88.3 %collective-permute-start.2 = (bf16[3,256,1024]{2,1,0:T(8,128)(2,1)}, bf16[3,256,1024]{2,1,0:T(8,128)(2,1)}, u32[]{:S(2)}, u32[]{:S(2)}) collective-permute-start(bf16[3,256,1024]{2,1,0:T(8,128)(2,1)} %add_convert_fusion.1), channel_id=1, source_target_pairs={{0,2},{1,3},{2,0},{3,1},{4,6},{5,7},{6,4},{7,5},{8,10},{9,11},{10,... | collective-permute-start | bytes 4718600 | tf_op jit(solution)/shard_map/ppermute | solution.py:1224
  797.5 2.3 copy-start.3
Sparse Core Ops, SparseCore 0:
  587.8 147.9 reduce-scatter.9
  738.2 59.2 reduce-scatter.5
  799.9 78.8 reduce-scatter.7

commit v3 on v2

--- a/solution.py
+++ b/solution.py
@@ -1098,6 +1098,62 @@
     )
 
 
+def weight_kernel(places, stacked, *refs):
+    out, acc = refs[-2:]
+    at = pl.program_id(0)
+
+    @pl.when(at == 0)
+    def _():
+        acc[...] = jnp.zeros_like(acc)
+
+    for i, j, start, count in places:
+        where = pl.ds(start, count)
+        part = dot(refs[i][...], refs[j][...], TN)
+        if stacked:
+            acc[where, :] += part
+        else:
+            acc[:, where] += part
+
+    @pl.when(at == pl.num_programs(0) - 1)
+    def _():
+        out[...] = acc[...].astype(BF)
+
+
+def weight_sums(pairs, stacked):
+    arrays, places, start = [], [], 0
+
+    def index(array):
+        for i, known in enumerate(arrays):
+            if known is array:
+                return i
+        arrays.append(array)
+        return len(arrays) - 1
+
+    for a, b in pairs:
+        count = (a if stacked else b).shape[-1]
+        places.append((index(a), index(b), start, count))
+        start += count
+    flat = [a.reshape(-1, a.shape[-1]) for a in arrays]
+    other = pairs[0][1 if stacked else 0].shape[-1]
+    shape = (start, other) if stacked else (other, start)
+    tokens, step = flat[0].shape[0], 512
+    return pl.pallas_call(
+        functools.partial(weight_kernel, places, stacked),
+        grid=(tokens // step,),
+        in_specs=[pl.BlockSpec((step, a.shape[1]), lambda i: (i, 0)) for a in flat],
+        out_specs=pl.BlockSpec(shape, lambda i: (0, 0)),
+        out_shape=jax.ShapeDtypeStruct(shape, BF),
+        scratch_shapes=[pltpu.VMEM(shape, F32)],
+        compiler_params=pltpu.CompilerParams(vmem_limit_bytes=VMEM_LIMIT),
+        cost_estimate=pl.CostEstimate(
+            flops=2 * tokens * start * other,
+            bytes_accessed=sum(a.size for a in flat) * 2,
+            transcendentals=0,
+        ),
+        name="weight_sums",
+    )(*flat)
+
+
 def body(
     block_input, cotangent, segments, attn_weight, attn_out, ffn_in, ffn_out, cross_weight, gains
 ):
@@ -1192,61 +1248,63 @@
         aug,
     )
 
-    def contract(left, right):
-        return lax.dot_general(
-            left, right, (((0, 1), (0, 1)), ((), ())), preferred_element_type=F32
-        ).astype(BF)
-
-    def over_rows(total):
-        return lax.psum_scatter(total, "dp", scatter_dimension=0, tiled=True).astype(F32)
-
-    sum_ffn = lax.cond(
+    def over_rows(total, dim):
+        return lax.psum_scatter(total, "dp", scatter_dimension=dim, tiled=True)
+
+    early = lax.cond(
         enc,
-        lambda: jnp.concatenate(
-            [contract(full_a, dgate), contract(full_a, dup), contract(full_g, hidden)], axis=1
+        lambda: weight_sums(
+            [(dgate, full_a), (dup, full_a), (hidden, full_g), (dkv, full_b)], True
         ),
-        lambda: jnp.concatenate(
-            [contract(full_3, dgate), contract(full_3, dup), contract(full_cot, hidden)], axis=1
+        lambda: weight_sums(
+            [(dgate, full_3), (dup, full_3), (hidden, full_cot), (dq, full_a), (mix, full_g)],
+            True,
         ),
     )
-    sum_cross = lax.cond(
-        enc,
-        lambda: contract(full_b, dkv),
-        lambda: jnp.concatenate([contract(full_a, dq), contract(full_g, mix)], axis=1),
-    )
-    sum2, full_s, dqkv = self_back_stage(
-        n, grad1.astype(BF), w_qkv, w_out, key_own, tri.T, qkv1, mix1, aug1
-    )
-    part, gain_first = norm_back(x, gain[0], sum2)
-    input_grad = grad1 + part
+    got_early = over_rows(early, 1)
 
     def across(tensor, bit):
-        return lax.ppermute(tensor, "mp", [(i, i ^ bit) for i in range(n)])
+        decoder = [(n + i, n + (i ^ bit)) for i in range(n)]
+        return lax.ppermute(tensor, ("section", "mp"), decoder)
 
     have = {j: parts[:, j * size : (j + 1) * size] for j in range(n)}
+    first = None
     for bit in bits:
         for j in sorted((j for j in have if j & bit), reverse=True):
             came = across(have.pop(j), bit)
             total = have[j ^ bit].astype(F32) + came.astype(F32)
             have[j ^ bit] = total if len(have) == 1 else total.astype(BF)
-    block_out = jnp.where(enc, third, (mid2 + have[0].astype(F32)).astype(BF))
-
-    sum_attn = jnp.concatenate([contract(full1, dqkv), contract(full_s, mix1), sum_cross], axis=1)
+        if bit == 1:
+            first = have[max(have)]
+    dec_out = mid2 + have[0].astype(F32)
+    block_out = jnp.where(enc, third, dec_out.astype(BF))
+
+    grad1_low, _, _ = lax.optimization_barrier((grad1.astype(BF), early, first))
+    sum2, full_s, dqkv = self_back_stage(
+        n, grad1_low, w_qkv, w_out, key_own, tri.T, qkv1, mix1, aug1
+    )
+    part, gain_first = norm_back(x, gain[0], sum2)
+    input_grad = grad1 + part
+
+    late = weight_sums([(full1, dqkv), (full_s, mix1)], False)
+    late, got_early = lax.optimization_barrier((late, got_early))
+    got_late = over_rows(late, 0).astype(F32)
+    got_early = got_early.astype(F32)
     quarter = width // dp_size
-    got_ffn = over_rows(sum_ffn)
-    got_attn = over_rows(sum_attn)
-    out_in = jnp.stack([got_ffn[:, :ffd], got_ffn[:, ffd : 2 * ffd]], axis=1)
-    out_down = got_ffn[:, 2 * ffd :].T
-    out_qkv = got_attn[:, : 3 * hid].reshape(quarter, 3, hid)
-    out_out = got_attn[:, 3 * hid : 4 * hid].T
-    out_cross = got_attn[:, 4 * hid :].reshape(quarter, 2, hid)
+    out_in = jnp.stack([got_early[:ffd].T, got_early[ffd : 2 * ffd].T], axis=1)
+    out_down = got_early[2 * ffd : 3 * ffd]
+    out_cross = got_early[3 * ffd :].T.reshape(quarter, 2, hid)
+    out_qkv = got_late[:, : 3 * hid].reshape(quarter, 3, hid)
+    out_out = got_late[:, 3 * hid :].T
     gain_parts = jnp.sum(gain_parts, axis=1)
-    gain_total = lax.psum_scatter(
-        jnp.stack([gain_first, gain_parts[1], gain_parts[0]]),
-        ("dp", "mp"),
-        scatter_dimension=1,
-        tiled=True,
-    )
+    gain_total = jnp.stack([gain_first, gain_parts[1], gain_parts[0]])
+    for axis, count in (("mp", n), ("dp", dp_size)):
+        for bit in (1 << b for b in range(count.bit_length() - 1)):
+            other = lax.ppermute(gain_total, axis, [(i, i ^ bit) for i in range(count)])
+            gain_total = gain_total + other
+    share = width // (n * dp_size)
+    place = (lax.axis_index("dp") * n + idx) * share
+    gain_total = lax.dynamic_slice_in_dim(gain_total, place, share, axis=1)
     return (
         jnp.swapaxes(block_out, 0, 1)[None],
         jnp.swapaxes(input_grad, 0, 1)[None],

time: 894 us -> 791 us (0.88)
  waiting for transfers between devices: 220 us -> 113 us
  Pallas kernels: 542 us -> 585 us
  matrix products: 40.1 us -> 0 us
  starting transfers between devices: 0.9 us -> 11.6 us
    unnamed x4 -> x2, waiting for transfers between devices: 84.2 us -> 0.03 us
    reduce_scatter x2, waiting for transfers between devices: 132 us -> 76.3 us  [over_rows(): return lax.psum_scatter(total, 'dp', scatter_dimension=dim, tiled=True)]
    dot_general x7 -> x0, matrix products: 40.1 us -> none  [contract(): lax.dot_general(left, right, (((0, 1), (0, 1)), ((), ())), preferred_elem...]
    pallas_call x0 -> x2, Pallas kernels: none -> 37.8 us  [weight_sums(): pl.pallas_call(functools.partial(weight_kernel, places, stacked), grid=(t...]
    ppermute x3 -> x7, waiting for transfers between devices: 4.36 us -> 37 us  [the longest x4 35.8 us: body(): other = lax.ppermute(gain_total, axis, [(i, i ^ bit) for i in range(count)])]
    ppermute x3 -> x7, starting transfers between devices: 0.78 us -> 11.5 us  [the longest x3 7.21 us: across(): return lax.ppermute(tensor, ('section', 'mp'), decoder)]
  transfers between devices with their start and end apart: 6 -> 9, of which waited for: 4 -> 5; matrix products, arithmetic and copies ran while one was open for 7% -> 3% of each run, Pallas kernels for 0% -> 12%
where the time goes in v3:
time: 791 us; the launch traced here: 782 us
  Pallas kernels  585 us (74%)
  waiting for transfers between devices  113 us (14%)
  other arithmetic  34.9 us (4%)
  local copies, waits for them, and re-layouts  22.8 us (3%)
  between operations  14.6 us (2%)
  starting transfers between devices  11.6 us (1%)
    pallas_call x4, Pallas kernels, call_stage(): pl.pallas_call(kernel, in_specs=[vmem if near else hbm for _, near in inp...  547 us
    reduce_scatter x2, waiting for transfers between devices, over_rows(): return lax.psum_scatter(total, 'dp', scatter_dimension=dim, tiled=True)  76.3 us
    pallas_call x2, Pallas kernels, weight_sums(): pl.pallas_call(functools.partial(weight_kernel, places, stacked), grid=(t...  37.8 us
    ppermute x4, waiting for transfers between devices, body(): other = lax.ppermute(gain_total, axis, [(i, i ^ bit) for i in range(count)])  35.8 us
  transfers between devices with their start and end apart: 9, of which 5 were waited for; matrix products, arithmetic and copies ran while one was open for 3% of the time, Pallas kernels for 12%

profile of v3, /device:TPU:2, one launch (start us, length us, event | category | flops | bytes accessed | tf_op | source)
XLA Modules:
  0.0 782.1 jit_solution(3320321069857873670)
XLA Ops:
  7.2 0.0 reduce-scatter.3.cloned.1.call-start
  7.3 0.8 constant_dynamic-slice_fusion
  8.1 0.1 broadcast_bitcast_fusion
  8.2 1.3 slice_bitcast_fusion.7
  9.5 1.8 fusion.11
  11.3 0.6 copy-done.14
  11.9 0.7 fusion.25.refs_5_
  12.6 1.8 copy.24
  14.5 1.6 copy.29.refs_1_
  16.1 0.0 copy-done
  16.1 1.6 fusion.9.refs_0_
  17.7 0.2 broadcast_compare_fusion
  17.9 4.3 select_convert_fusion
  22.2 79.5 %self_stage.1 = (f32[3,256,1024]{2,1,0:T(8,128)}, bf16[3,1024,1024]{2,1,0:T(8,128)(2,1)}, bf16[3,1024,768]{2,1,0:T(8,128)(2,1)}, bf16[3,1024,256]{2,1,0:T(8,128)(2,1)}, bf16[3,1024,256]{2,1,0:T(8,128)(2,1)}) custom-call(bf16[3,256,1024]{2,1,0:T(8,128)(2,1)} %fusion.9.refs_0_, bf16[1024,768]{1,0:T(8,128)(2,1)} %copy.29.refs_1_, bf16[256,1024]{1,0:T(8,128)(2,1)} %bitcast.135, ...), custom_call_target="tpu_custom_call" | custom-call | flops 19327352832 | bytes 33554432 | tf_op jit(solution)/shard_map/self_stage/pallas_call | solution.py:273
  101.7 0.0 copy-start.6
  101.7 4.1 multiply_reduce_fusion
  105.8 1.4 fusion.32
  107.2 1.6 copy.42
  108.8 2.7 copy.43
  111.5 2.4 copy.45
  113.9 1.5 multiply_convert_fusion.refs_0_
  115.4 194.5 %middle_stage.1 = (f32[3,256,1024]{2,1,0:T(8,128)}, bf16[3,256,1024]{2,1,0:T(8,128)(2,1)}, bf16[3,1024,1024]{2,1,0:T(8,128)(2,1)}, bf16[3,1024,1024]{2,1,0:T(8,1...) custom-call(bf16[3,256,1024]{2,1,0:T(8,128)(2,1)} %multiply_convert_, ...), custom_call_target="tpu_custom_call" | custom-call | flops 26172456960 | bytes 33554432 | tf_op jit(solution)/shard_map/middle_stage/pallas_call | solution.py:273
  310.0 192.4 %middle_back_stage.1 = (f32[3,256,1024]{2,1,0:T(8,128)}, f32[2,8,1024]{2,1,0:T(8,128)}, bf16[3,1024,1024]{2,1,0:T(8,128)(2,1)}, bf16[3,1024,1024]{2,1,0:T(8,128)...) custom-call(bf16[3,256,1024]{2,1,0:T(8,128)(2,1)} %get-tuple-element, ...), custom_call_target="tpu_custom_call" | custom-call | flops 67645734912 | bytes 33554432 | tf_op jit(solution)/shard_map/middle_back_stage/pallas_call | solution.py:273
  502.3 24.7 %conditional.1 = (bf16[2624,1024]{1,0:T(8,128)(2,1)}) conditional(s32[]{:T(128)} %convert_element_type.85, (bf16[3,1024,704]{2,1,0:T(8,128)(2,1)}, bf16[3,1024,1024]{2,1,0:T(8,128)(2,1)}, bf16[3,1024,704]{2,1,0:T(8,128)(2,1)}, bf16[3,1024,704]{2,1,0:T(8,128)(2,1)}, bf16[3,1024,1024]{2,1,0:T(8,128)(2,1)}, /*index=5*/bf16[3,1024,256]{2,1,0:T(8,128)(2,1)}, ...), branch_computations={%region_2.3_spmd, %region_3.4_spmd} | conditional | flops 16508780544 | bytes 41287688 | solution.py:1254
  502.4 24.7 %weight_sums.3 = bf16[2624,1024]{1,0:T(8,128)(2,1)} custom-call(bf16[3072,704]{1,0:T(8,128)(2,1)} %bitcast.148, bf16[3072,1024]{1,0:T(8,128)(2,1)} %bitcast.142, bf16[3072,704]{1,0:T(8,128)(2,1)} %bitcast.150, bf16[3072,704]{1,0:T(8,128)(2,1)} %bitcast.146, bf16[3072,1024]{1,0:T(8,128)(2,1)} %bitcast.141, bf16[3072,256]{1,0:T(8,128)(2,1)} %bitcast.156, ...), custom_call_target="tpu_custom_call" | custom-call | flops 16508780544 | bytes 41287680 | tf_op jit(solution)/shard_map/cond/branch_0_fun/weight_sums/pallas_call | solution.py:1140
  527.1 0.0 reduce-scatter.3.cloned.1.call-update
  527.1 0.0 reduce-scatter.5.cloned.1.call-start
  527.2 0.0 copy-start.3
  527.2 2.4 fusion.31
  529.6 1.9 collective-permute-start.1
  531.5 1.4 convert_element_type.84.refs_0_
  532.9 0.7 fusion.27.refs_4_
  533.7 1.3 collective-permute-done.1
  534.9 3.2 add_convert_fusion.1
  538.1 80.6 %self_back_stage.1 = (f32[3,256,1024]{2,1,0:T(8,128)}, bf16[3,1024,1024]{2,1,0:T(8,128)(2,1)}, bf16[3,1024,768]{2,1,0:T(8,128)(2,1)}) custom-call(bf16[3,256,1024]{2,1,0:T(8,128)(2,1)} %convert_element_type.84.refs_0_, bf16[1024,768]{1,0:T(8,128)(2,1)} %copy.29.refs_1_, bf16[256,1024]{1,0:T(8,128)(2,1)} %bitcast.136, ...), custom_call_target="tpu_custom_call" | custom-call | flops 38654705664 | bytes 33554432 | tf_op jit(solution)/shard_map/self_back_stage/pallas_call | solution.py:273
  618.8 13.1 %weight_sums.5 = bf16[1024,1024]{1,0:T(8,128)(2,1)} custom-call(bf16[3072,1024]{1,0:T(8,128)(2,1)} %bitcast.137, bf16[3072,768]{1,0:T(8,128)(2,1)} %bitcast.152, bf16[3072,1024]{1,0:T(8,128)(2,1)} %bitcast.145, bf16[3072,256]{1,0:T(8,128)(2,1)} %bitcast.154), custom_call_target="tpu_custom_call" | custom-call | flops 6442450944 | bytes 18874368 | tf_op jit(solution)/shard_map/weight_sums/pallas_call | solution.py:1140
  631.9 76.3 %reduce-scatter.3.cloned.1.call-done = bf16[2624,256]{1,0:T(8,128)(2,1)} async-done(((bf16[2624,1024]{1,0:T(8,128)(2,1)}), bf16[2624,256]{1,0:T(8,128)(2,1)}) %reduce-scatter.3.cloned.1.call-update) | async-done | bytes 1343504 | tf_op jit(solution)/shard_map/reduce_scatter | solution.py:1252
  708.2 0.0 reduce-scatter.5.cloned.1.call-update
  708.2 1.9 collective-permute-start
  710.2 3.4 collective-permute-start.2
  713.6 3.1 fusion.10
  716.7 0.3 collective-permute-start.3
  717.0 1.0 collective-permute-done.3
  718.0 0.6 collective-permute-start.4
  718.6 30.9 %collective-permute-done.4 = f32[3,1024]{1,0:T(4,128)S(1)} collective-permute-done((f32[3,1024]{1,0:T(4,128)S(1)}, f32[3,1024]{1,0:T(4,128)S(1)}, u32[]{:S(2)}, u32[]{:S(2)}) %collective-permute-start.4) | collective-permute-done | bytes 12320 | tf_op jit(solution)/shard_map/ppermute | solution.py:1303
  749.5 1.5 collective-permute-start.5
  751.1 3.9 collective-permute-done.5
  755.0 1.8 collective-permute-start.6
  756.8 5.3 fusion.1
  762.2 0.0 collective-permute-done.6
  762.2 0.1 dynamic-slice_add_fusion
  762.2 0.6 broadcast_in_dim.83
  762.8 0.0 collective-permute-done
  762.8 0.0 collective-permute-done.2
  762.9 5.3 fusion.14
  768.1 0.2 convert_element_type.87
  768.4 1.0 copy.37
  769.4 1.0 slice_bitcast_fusion
  770.4 1.2 maximum_bitcast_fusion
  771.6 1.1 slice.94
  772.7 0.3 copy.33
  773.0 1.1 copy.35
  774.1 0.1 convert_element_type.86
  774.3 0.8 copy.36
  (51 shorter events, 0.3 us)
Async XLA Ops:
  7.2 701.0 %reduce-scatter.3.cloned.1.call-start = ((), (), s32[]{:S(2)}) async-start(), calls=%async_computation.2 | async-start | bytes 6717440 | tf_op jit(solution)/shard_map/reduce_scatter | solution.py:1252
  9.5 6.5 copy-start.9
  11.3 0.6 copy-start.14
  11.9 4.2 copy-start.11
  12.6 3.4 copy-start
  101.7 4.1 copy-start.6
  108.8 5.1 copy-start.2
  527.1 244.5 %reduce-scatter.5.cloned.1.call-start = ((), (), s32[]{:S(2)}) async-start(), calls=%async_computation.3 | async-start | bytes 2621440 | tf_op jit(solution)/shard_map/reduce_scatter | solution.py:1252
  527.2 4.4 copy-start.3
  529.6 5.3 collective-permute-start.1
  618.7 91.4 %copy-start.13 = (f32[2,8,1024]{2,1,0:T(8,128)S(1)}, f32[2,8,1024]{2,1,0:T(8,128)}, u32[]{:S(2)}) copy-start(f32[2,8,1024]{2,1,0:T(8,128)} %get-tuple-element.118) | copy-start | bytes 196612
  618.7 94.9 %copy-start.10 = (f32[1,1,1024]{2,0,1:T(1,128)S(1)}, f32[1,1,1024]{2,0,1:T(1,128)}, u32[]{:S(2)}) copy-start(f32[1,1,1024]{2,0,1:T(1,128)} %copy-done.9) | copy-start | bytes 12292
  618.8 94.9 %copy-start.12 = (f32[3,256]{1,0:T(4,128)S(1)}, f32[3,256]{1,0:T(4,128)}, u32[]{:S(2)}) copy-start(f32[3,256]{1,0:T(4,128)} %copy-done.11) | copy-start | bytes 9220
  631.9 81.8 %copy-start.1 = (bf16[1,256,3,1024]{3,1,2,0:T(8,128)(2,1)S(1)}, bf16[1,256,3,1024]{3,1,2,0:T(8,128)(2,1)}, u32[]{:S(2)}) copy-start(bf16[1,256,3,1024]{3,1,2,0:T(8,128)(2,1)} %param.11) | copy-start | bytes 4718596
  631.9 119.2 %copy-start.15 = (f32[3,256]{1,0:T(4,128)S(1)}, f32[3,256]{1,0:T(4,128)}, u32[]{:S(2)}) copy-start(f32[3,256]{1,0:T(4,128)} %copy-done.14) | copy-start | bytes 9220
  708.2 54.6 %collective-permute-start = (bf16[3,256,1024]{2,1,0:T(8,128)(2,1)S(1)}, bf16[3,256,1024]{2,1,0:T(8,128)(2,1)}, u32[]{:S(2)}, u32[]{:S(2)}) collective-permute-start(bf16[3,256,1024]{2,1,0:T(8,128)(2,1)S(1)} %get-tuple-element.139), channel_id=1, source_target_pairs={{16,17},{17,16},{18,19},{19,18},{20,21},{21,20},{22,23},{23,22},{2... | collective-permute-start | bytes 4718600 | tf_op jit(solution)/shard_map/ppermute | solution.py:1268
  710.2 52.6 %collective-permute-start.2 = (bf16[3,256,1024]{2,1,0:T(8,128)(2,1)}, bf16[3,256,1024]{2,1,0:T(8,128)(2,1)}, u32[]{:S(2)}, u32[]{:S(2)}) collective-permute-start(bf16[3,256,1024]{2,1,0:T(8,128)(2,1)} %add_convert_fusion.1), channel_id=1, source_target_pairs={{16,18},{17,19},{18,16},{19,17},{20,22},{21,23},{22,20},{23,21},{2... | collective-permute-start | bytes 4718600 | tf_op jit(solution)/shard_map/ppermute | solution.py:1268
  716.7 1.2 collective-permute-start.3
  718.0 31.5 %collective-permute-start.4 = (f32[3,1024]{1,0:T(4,128)S(1)}, f32[3,1024]{1,0:T(4,128)S(1)}, u32[]{:S(2)}, u32[]{:S(2)}) collective-permute-start(f32[3,1024]{1,0:T(4,128)S(1)} %fusion.29), channel_id=1, source_target_pairs={{0,2},{1,3},{2,0},{3,1},{4,6},{5,7},{6,4},{7,5},{8,10},{9,11},{10,... | collective-permute-start | bytes 36872 | tf_op jit(solution)/shard_map/ppermute | solution.py:1303
  749.5 5.5 collective-permute-start.5
  755.0 7.8 %copy-start.5 = (f32[3,256,1024]{2,1,0:T(8,128)S(1)}, f32[3,256,1024]{2,1,0:T(8,128)}, u32[]{:S(2)}) copy-start(f32[3,256,1024]{2,1,0:T(8,128)} %get-tuple-element.91.refs_10_) | copy-start | bytes 9437188
  755.0 7.8 %copy-start.8 = (bf16[3,256,1024]{2,1,0:T(8,128)(2,1)S(1)}, bf16[3,256,1024]{2,1,0:T(8,128)(2,1)}, u32[]{:S(2)}) copy-start(bf16[3,256,1024]{2,1,0:T(8,128)(2,1)} %get-tuple-element.90.refs_0_) | copy-start | bytes 4718596
  755.0 7.2 collective-permute-start.6
  762.8 5.3 copy-start.7
  771.6 2.5 copy-start.4
Sparse Core Ops, SparseCore 0:
  527.2 180.9 reduce-scatter.2
  710.5 48.2 reduce-scatter.4

commit v4 on v3

--- a/solution.py
+++ b/solution.py
@@ -287,13 +287,13 @@
 
 
 def self_stage_kernel(n, *refs):
-    (x, w_qkv, w_out, query_aug, key_aug, tri) = refs[:6]
-    (total, full_out, qkv_out, mix_out, aug_out) = refs[6:11]
-    (got, out, back, qkv, mix, aug) = refs[11:17]
-    sems = refs[17:]
+    (x, gain, w_qkv, w_out, query_aug, key_aug, tri) = refs[:7]
+    (total, normed, full_out, qkv_out, mix_out, aug_out) = refs[7:13]
+    (own, got, out, back, qkv, mix, aug) = refs[13:20]
+    sems = refs[20:]
     rows, size = x.shape[:2]
     hid = w_out.shape[0]
-    gather = Gather(n, x, got, *sems[:2])
+    gather = Gather(n, own, got, *sems[:2])
     sums = Sums(n, out, back, *sems[2:4])
     save = sems[4]
     greet(n)
@@ -307,7 +307,14 @@
                 pair = (ref.at[r], dst.at[r])
             yield pltpu.make_async_copy(*pair, save.at[r, i])
 
+    def finish(r):
+        stream = x[r].astype(F32) + sums.total(r, total[r])
+        total[r] = stream
+        normed[r] = (stream * norm_parts(stream) * gain[1:2]).astype(BF)
+
     for r in range(rows):
+        stream = x[r].astype(F32)
+        own[r] = (stream * norm_parts(stream) * gain[0:1]).astype(BF)
         gather.start(r)
     gather.forward(0)
 
@@ -354,10 +361,10 @@
 
         @pl.when(r > 0)
         def _():
-            total[r - 1] = sums.total(r - 1, total[r - 1])
+            finish(r - 1)
 
     sums.forward(rows - 1)
-    total[rows - 1] = sums.total(rows - 1, total[rows - 1])
+    finish(rows - 1)
 
     @pl.loop(0, rows)
     def _(r):
@@ -367,7 +374,7 @@
             copy.wait()
 
 
-def self_stage(n, x, w_qkv, w_out, query_aug, key_aug, tri):
+def self_stage(n, x, gain, w_qkv, w_out, query_aug, key_aug, tri):
     rows, size, width = x.shape
     length, hid = n * size, w_out.shape[0]
     slots = (rows, n - 1)
@@ -375,15 +382,17 @@
         functools.partial(self_stage_kernel, n),
         "self_stage",
         1,
-        [(a, True) for a in (x, w_qkv, w_out, query_aug, key_aug, tri)],
+        [(a, True) for a in (x, gain, w_qkv, w_out, query_aug, key_aug, tri)],
         [
             ((rows, size, width), F32, True),
+            ((rows, size, width), BF, True),
             ((rows, length, width), BF, False),
             ((rows, length, 3 * hid), BF, False),
             ((rows, length, hid), BF, False),
             ((rows, length, hid), BF, False),
         ],
         [
+            pltpu.VMEM((rows, size, width), BF),
             *[pltpu.VMEM((*slots, size, width), BF)] * 3,
             pltpu.VMEM((rows, length, 3 * hid), BF),
             pltpu.VMEM((rows, length, hid), BF),
@@ -396,33 +405,50 @@
 
 
 def self_back_kernel(n, *refs):
-    (x, w_qkv, w_out, key_aug, tri_t, qkv_in, mix_in, aug_in) = refs[:8]
-    (total, full_out, dqkv_out) = refs[8:11]
-    (got, out, back, qkv, mix, aug, grad, dqkv) = refs[11:19]
-    sems = refs[19:]
+    (x, gain, slope, w_qkv, w_out, key_aug, tri_t, qkv_in, mix_in, aug_in, full_in) = refs[:11]
+    (total, gain_out, weights) = refs[11:14]
+    (own, got, out, back, qkv, mix, aug, grad, dqkv, full, acc) = refs[14:25]
+    sems = refs[25:]
     rows, size = x.shape[:2]
     hid = w_out.shape[0]
-    gather = Gather(n, x, got, *sems[:2])
+    gather = Gather(n, own, got, *sems[:2])
     sums = Sums(n, out, back, *sems[2:4])
-    save, load = sems[4:]
+    load, load_full = sems[4:]
     greet(n)
 
     def loads(r):
         for i, (src, dst) in enumerate(((qkv_in, qkv), (mix_in, mix), (aug_in, aug))):
             yield pltpu.make_async_copy(src.at[r], dst.at[r], load.at[r, i])
 
-    def saves(r, which):
-        for i in which:
-            if i < n:
-                pair = (gather.block(r, i), full_out.at[r, pl.ds(i * size, size)])
-            else:
-                pair = (dqkv.at[r], dqkv_out.at[r])
-            yield pltpu.make_async_copy(*pair, save.at[r, i])
+    def full_load(r):
+        return pltpu.make_async_copy(full_in.at[r], full, load_full.at[0])
+
+    def add_weights(r):
+        full_load(r).wait()
+        acc[:, : 3 * hid] += dot(full[...], dqkv[r], TN)
+        acc[:, 3 * hid :] += functools.reduce(
+            jnp.add,
+            [
+                dot(gather.block(r, j)[...], mix[r, j * size : (j + 1) * size, :], TN)
+                for j in range(n)
+            ],
+        )
+
+    def finish(r):
+        part, terms = norm_back_parts(
+            x[r].astype(F32), gain[0:1], sums.total(r, total[r])
+        )
+        gain_out[...] += gain_terms(terms)
+        total[r] = slope[r] + part
 
     for r in range(rows):
+        own[r] = slope[r].astype(BF)
         gather.start(r)
         for copy in loads(r):
             copy.start()
+    full_load(0).start()
+    gain_out[...] = jnp.zeros_like(gain_out)
+    acc[...] = jnp.zeros_like(acc)
     gather.forward(0)
 
     @pl.loop(0, rows)
@@ -432,8 +458,6 @@
             grad[j * size : (j + 1) * size, :] = dot(
                 gather.block(r, j)[...], w_out[...], NT
             ).astype(BF)
-        for copy in saves(r, range(n)):
-            copy.start()
         for copy in loads(r):
             copy.wait()
 
@@ -441,7 +465,7 @@
         def _():
             sums.forward(r - 1)
 
-        row, slope = qkv.at[r], dqkv.at[r]
+        row, result = qkv.at[r], dqkv.at[r]
         attend_back_into(
             size,
             hid // DK,
@@ -453,12 +477,10 @@
             (aug.at[r], 0),
             key_aug.at[r],
             tri_t,
-            (slope, 0),
-            (slope, hid),
-            (slope, 2 * hid),
+            (result, 0),
+            (result, hid),
+            (result, 2 * hid),
         )
-        for copy in saves(r, range(n, n + 1)):
-            copy.start()
 
         @pl.when(r + 1 < rows)
         def _():
@@ -473,20 +495,22 @@
 
         @pl.when(r > 0)
         def _():
-            total[r - 1] = sums.total(r - 1, total[r - 1])
+            add_weights(r - 1)
+            full_load(r).start()
+            finish(r - 1)
 
     sums.forward(rows - 1)
-    total[rows - 1] = sums.total(rows - 1, total[rows - 1])
+    add_weights(rows - 1)
+    weights[...] = acc[...].astype(BF)
+    finish(rows - 1)
 
     @pl.loop(0, rows)
     def _(r):
         gather.drain(r)
         sums.drain(r)
-        for copy in saves(r, range(n + 1)):
-            copy.wait()
-
-
-def self_back_stage(n, x, w_qkv, w_out, key_aug, tri_t, qkv, mix, aug):
+
+
+def self_back_stage(n, x, gain, slope, w_qkv, w_out, key_aug, tri_t, qkv, mix, aug, full):
     rows, size, width = x.shape
     length, hid = n * size, w_out.shape[0]
     slots = (rows, n - 1)
@@ -494,23 +518,26 @@
         functools.partial(self_back_kernel, n),
         "self_back_stage",
         2,
-        [(a, True) for a in (x, w_qkv, w_out, key_aug, tri_t)]
-        + [(a, False) for a in (qkv, mix, aug)],
+        [(a, True) for a in (x, gain, slope, w_qkv, w_out, key_aug, tri_t)]
+        + [(a, False) for a in (qkv, mix, aug, full)],
         [
             ((rows, size, width), F32, True),
-            ((rows, length, width), BF, False),
-            ((rows, length, 3 * hid), BF, False),
+            ((8, width), F32, True),
+            ((width, 4 * hid), BF, True),
         ],
         [
+            pltpu.VMEM((rows, size, width), BF),
             *[pltpu.VMEM((*slots, size, width), BF)] * 3,
             pltpu.VMEM((rows, length, 3 * hid), BF),
             pltpu.VMEM((rows, length, hid), BF),
             pltpu.VMEM((rows, length, hid), BF),
             pltpu.VMEM((length, hid), BF),
             pltpu.VMEM((rows, length, 3 * hid), BF),
+            pltpu.VMEM((length, width), BF),
+            pltpu.VMEM((width, 4 * hid), F32),
             *[pltpu.SemaphoreType.DMA(slots)] * 4,
-            pltpu.SemaphoreType.DMA((rows, n + 1)),
             pltpu.SemaphoreType.DMA((rows, 3)),
+            pltpu.SemaphoreType.DMA((1,)),
         ],
         rows * length * width * hid * 8 + rows * length * length * hid * 40,
     )
@@ -518,18 +545,29 @@
 
 def middle_kernel(n, *refs):
     (x, cot, mid1, gain, w_gate, w_up, w_down, w_cross, query_aug, key_aug) = refs[:10]
-    (mid2, third, full_a, full_b, full_cot, kv_out, q_out, mix_out, aug_out) = refs[10:19]
-    (got_a, got_b, got_c, out, back, kv, q, mix, aug) = refs[19:28]
-    sems = refs[28:]
+    (mid2, third, full_a, full_b, full_cot, full_t, w_kv_out) = refs[10:17]
+    (kv_out, q_out, mix_out, aug_out) = refs[17:21]
+    (got_a, got_b, got_c, out, back, memory, w_kv, kv, q, mix, aug) = refs[21:32]
+    sems = refs[32:]
     rows, size = x.shape[:2]
     hid = q.shape[2]
     enc = lax.axis_index("section") == 0
     gather_a = Gather(n, x, got_a, *sems[0:2])
-    gather_b = Gather(n, third, got_b, *sems[2:4])
+    gather_b = Gather(n, memory, got_b, *sems[2:4])
     gather_c = Gather(n, cot, got_c, *sems[4:6])
     sums = Sums(n, out, back, *sems[6:8])
-    pair_send, pair_recv, save_a, save_b, save_c, save_x = sems[8:]
+    gather_t = Gather(n, third, got_a, *sems[8:10])
+    pair_send, pair_recv, save_a, save_b, save_c, save_t, save_x, weight_sems = sems[10:]
     greet(n, True)
+    weight_copy = pltpu.make_async_remote_copy(
+        src_ref=w_cross,
+        dst_ref=w_kv,
+        send_sem=weight_sems.at[0],
+        recv_sem=weight_sems.at[1],
+        device_id={"section": 1 - lax.axis_index("section")},
+        device_id_type=MESH,
+    )
+    weight_save = pltpu.make_async_copy(w_kv, w_kv_out, weight_sems.at[2])
 
     def block_saves(gather, dst, sem, r):
         for j in range(n):
@@ -545,8 +583,8 @@
 
     def pair_copy(r):
         return pltpu.make_async_remote_copy(
-            src_ref=kv.at[r],
-            dst_ref=kv.at[r],
+            src_ref=third.at[r],
+            dst_ref=memory.at[r],
             send_sem=pair_send.at[r],
             recv_sem=pair_recv.at[r],
             device_id={"section": 1 - lax.axis_index("section")},
@@ -564,6 +602,8 @@
 
     @pl.when(enc)
     def _():
+        weight_copy.start()
+
         @pl.loop(0, rows)
         def _(r):
             gather_a.finish(r)
@@ -592,34 +632,20 @@
             @pl.when(r > 0)
             def _():
                 finish(r - 1)
-                gather_b.start(r - 1)
+                pair_copy(r - 1).start()
 
         sums.forward(rows - 1)
-        gather_b.forward(0)
         finish(rows - 1)
-        gather_b.start(rows - 1)
+        pair_copy(rows - 1).start()
 
         @pl.loop(0, rows)
         def _(r):
-            gather_b.finish(r)
-            for j in range(n):
-                kv[r, j * size : (j + 1) * size, :] = dot(
-                    gather_b.block(r, j)[...], w_cross[...]
-                ).astype(BF)
-            pair_copy(r).start()
-            for copy in block_saves(gather_b, full_b, save_b, r):
-                copy.start()
-
-            @pl.when(r + 1 < rows)
-            def _():
-                gather_b.forward(r + 1)
-
-        @pl.loop(0, rows)
-        def _(r):
-            gather_b.drain(r)
             pair_copy(r).wait_send()
-            for copy in block_saves(gather_b, full_b, save_b, r):
+            gather_a.drain(r)
+            for copy in block_saves(gather_a, full_a, save_a, r):
                 copy.wait()
+
+        weight_copy.wait_send()
 
     @pl.when(jnp.logical_not(enc))
     def _():
@@ -647,13 +673,33 @@
             for copy in block_saves(gather_c, full_cot, save_c, r):
                 copy.start()
 
+        def launch(r):
+            pair_copy(r).wait_recv()
+            gather_b.start(r)
+
+        weight_copy.wait_recv()
+        weight_save.start()
+        for r in range(min(2, rows)):
+            launch(r)
+        gather_b.forward(0)
+
         @pl.loop(0, rows)
         def _(r):
-            pair_copy(r).wait_recv()
+            gather_b.finish(r)
+            for copy in block_saves(gather_b, full_b, save_b, r):
+                copy.start()
+            for j in range(n):
+                kv[r, j * size : (j + 1) * size, :] = dot(
+                    gather_b.block(r, j)[...], w_kv[...]
+                ).astype(BF)
 
             @pl.when(r > 0)
             def _():
                 sums.forward(r - 1)
+
+            @pl.when(r + 2 < rows)
+            def _():
+                launch(r + 2)
 
             row = kv.at[r]
             attend_into(
@@ -670,6 +716,14 @@
             )
             for copy in cross_saves(r):
                 copy.start()
+
+            @pl.when(r + 1 < rows)
+            def _():
+                gather_b.forward(r + 1)
+
+            gather_a.drain(r)
+            for copy in block_saves(gather_a, full_a, save_a, r):
+                copy.wait()
             for j in reversed(range(n)):
                 part = dot(mix[r, j * size : (j + 1) * size, :], w_cross[:, hid:], NT)
                 if j:
@@ -681,11 +735,34 @@
             def _():
                 finish(r - 1)
 
+            @pl.when(r == 1)
+            def _():
+                gather_t.start(0)
+
+            @pl.when(r == 2)
+            def _():
+                gather_t.forward(0)
+
         sums.forward(rows - 1)
+        if rows > 1:
+            if rows == 2:
+                gather_t.forward(0)
+            gather_t.finish(0)
+            for copy in block_saves(gather_t, full_t, save_t, 0):
+                copy.start()
         finish(rows - 1)
+        if rows > 1:
+            gather_t.drain(0)
+            for copy in block_saves(gather_t, full_t, save_t, 0):
+                copy.wait()
+
+        weight_save.wait()
 
         @pl.loop(0, rows)
         def _(r):
+            gather_b.drain(r)
+            for copy in block_saves(gather_b, full_b, save_b, r):
+                copy.wait()
             gather_c.drain(r)
             for copy in block_saves(gather_c, full_cot, save_c, r):
                 copy.wait()
@@ -694,10 +771,7 @@
 
     @pl.loop(0, rows)
     def _(r):
-        gather_a.drain(r)
         sums.drain(r)
-        for copy in block_saves(gather_a, full_a, save_a, r):
-            copy.wait()
 
 
 def middle_stage(n, x, cot, mid1, gain, w_gate, w_up, w_down, w_cross, query_aug, key_aug):
@@ -718,6 +792,8 @@
             full,
             full,
             full,
+            full,
+            ((width, 2 * hid), BF, False),
             ((rows, length, 2 * hid), BF, False),
             head,
             head,
@@ -725,25 +801,30 @@
         ],
         [
             *[pltpu.VMEM((*slots, size, width), BF)] * 5,
+            pltpu.VMEM((rows, size, width), BF),
+            pltpu.VMEM((width, 2 * hid), BF),
             pltpu.VMEM((rows, length, 2 * hid), BF),
             *[pltpu.VMEM((rows, length, hid), BF)] * 3,
-            *[pltpu.SemaphoreType.DMA(slots)] * 8,
+            *[pltpu.SemaphoreType.DMA(slots)] * 10,
             *[pltpu.SemaphoreType.DMA((rows,))] * 2,
-            *[pltpu.SemaphoreType.DMA((rows, n))] * 3,
+            *[pltpu.SemaphoreType.DMA((rows, n))] * 4,
             pltpu.SemaphoreType.DMA((rows, 4)),
+            pltpu.SemaphoreType.DMA((3,)),
         ],
         rows * length * width * ffd * 6 + rows * length * length * hid * 16,
     )
 
 
 def middle_back_kernel(n, *refs):
-    (third, cot, gain2, gain1, w_gate, w_up, w_down, w_cross, key_aug) = refs[:9]
-    (mid1_in, mid2_in, fwd_in, cot_in, kv_in, q_in, mix_in, aug_in) = refs[9:17]
-    (grad, gain_out, parts_out, full_3, full_g) = refs[17:22]
-    (hidden_out, dgate_out, dup_out, dkv_out, dq_out) = refs[22:27]
-    (own, got, out, back, rest, dkv) = refs[27:33]
-    (mid, full, kv, q, mix, aug, dq, hidden_s, dgate_s, dup_s, part_s) = refs[33:44]
-    sems = refs[44:]
+    (third, cot, gain2, gain1, w_gate, w_up, w_down, w_cross, w_kv, key_aug) = refs[:10]
+    (mid1_in, mid2_in, fwd_in, cot_in, third_in) = refs[10:15]
+    (kv_in, q_in, mix_in, aug_in) = refs[15:19]
+    (grad, gain_out, parts_out, full_3, full_g) = refs[19:24]
+    (hidden_out, dgate_out, dup_out, dkv_out, dq_out) = refs[24:29]
+    (own, got, out, back, rest, dmem) = refs[29:35]
+    (mid, full, kv, q, mix, aug, dq, dkv, hidden_s, dgate_s, dup_s, part_s) = refs[35:47]
+    ready = refs[47]
+    sems = refs[48:]
     rows, size = third.shape[:2]
     hid = q.shape[1]
     enc = lax.axis_index("section") == 0
@@ -751,7 +832,8 @@
     gather_g = Gather(n, own, got, *sems[2:4])
     sums_a = Sums(n, out, back, *sems[4:6])
     sums_b = Sums(n, out, back, *sems[6:8])
-    pair_send, pair_recv, save_3, save_g, save_f, save_p, save_d, load_m, load_f, load_x = sems[8:]
+    sums_m = Sums(n, out, back, *sems[8:10])
+    pair_send, pair_recv, save_3, save_g, save_f, save_p, save_d, load_m, load_f, load_x = sems[10:]
     greet(n, True)
     gain_out[...] = jnp.zeros_like(gain_out)
 
@@ -763,8 +845,8 @@
 
     def pair_copy(r):
         return pltpu.make_async_remote_copy(
-            src_ref=dkv.at[r],
-            dst_ref=dkv.at[r],
+            src_ref=dmem.at[r],
+            dst_ref=dmem.at[r],
             send_sem=pair_send.at[r],
             recv_sem=pair_recv.at[r],
             device_id={"section": 1 - lax.axis_index("section")},
@@ -830,9 +912,10 @@
 
     def finish_third(r, sums, add_cot):
         mid_load(0, mid2_in, r).wait()
-        arriving = sums.total(r, rest[r])
         if add_cot:
-            arriving = arriving + cot[r].astype(F32)
+            arriving = dmem[r].astype(F32) + cot[r].astype(F32)
+        else:
+            arriving = sums.total(r, rest[r])
         part, terms = norm_back_parts(mid[0], gain2[...], arriving)
         gain_out[0] += gain_terms(terms)
         if not add_cot:
@@ -840,6 +923,16 @@
         grad[r] = part
         own[r] = part.astype(BF)
 
+    def dkv_save(r):
+        return pltpu.make_async_copy(dkv, dkv_out.at[r], save_d.at[0])
+
+    def dq_save(r):
+        return pltpu.make_async_copy(dq.at[r], dq_out.at[r], save_d.at[1 + r])
+
+    def finish_memory(r):
+        dmem[r] = sums_m.total(r, rest[r]).astype(BF)
+        pair_copy(r).start()
+
     def finish_second(r, sums):
         mid_load(1, mid1_in, r).wait()
         part, terms = norm_back_parts(mid[1], gain1[...], sums.total(r, rest[r]))
@@ -850,21 +943,43 @@
 
     @pl.when(jnp.logical_not(enc))
     def _():
-        for r in range(rows):
+        def third_loads(r):
+            for j in range(1, n):
+                yield pltpu.make_async_copy(
+                    third_in.at[r, pl.ds(j * size, size)], got.at[r, j - 1], save_3.at[r, j]
+                )
+
+        ahead = 1 if rows > 1 else 0
+        for r in range(ahead, rows):
             gather_3.start(r)
         full_load(cot_in, 0).start()
-        gather_3.forward(0)
+        if ahead:
+            for copy in third_loads(0):
+                copy.start()
+        else:
+            gather_3.forward(0)
 
         @pl.loop(0, rows)
         def _(r):
-            gather_3.finish(r)
+            @pl.when(r < ahead)
+            def _():
+                for copy in third_loads(r):
+                    copy.wait()
+
+            @pl.when(r >= ahead)
+            def _():
+                gather_3.finish(r)
+
             for copy in block_saves(gather_3, full_3, save_3, r):
                 copy.start()
             full_load(cot_in, r).wait()
 
+            @pl.when(r > ahead)
+            def _():
+                gather_3.drain(r - 1)
+
             @pl.when(r > 0)
             def _():
-                gather_3.drain(r - 1)
                 sums_a.forward(r - 1)
                 mid_load(0, mid2_in, r - 1).start()
 
@@ -910,9 +1025,8 @@
 
             @pl.when(r > 0)
             def _():
-                pltpu.make_async_copy(dq, dq_out.at[r - 1], save_d.at[0]).wait()
-                sums_b.forward(r - 1)
-                mid_load(1, mid1_in, r - 1).start()
+                dkv_save(r - 1).wait()
+                sums_m.forward(r - 1)
 
             attend_back_into(
                 size,
@@ -925,12 +1039,12 @@
                 (aug, 0),
                 key_aug.at[r],
                 None,
-                (dq, 0),
-                (dkv.at[r], 0),
-                (dkv.at[r], hid),
+                (dq.at[r], 0),
+                (dkv, 0),
+                (dkv, hid),
             )
-            pair_copy(r).start()
-            pltpu.make_async_copy(dq, dq_out.at[r], save_d.at[0]).start()
+            dkv_save(r).start()
+            dq_save(r).start()
 
             @pl.when(r + 1 < rows)
             def _():
@@ -940,7 +1054,37 @@
 
             sums_a.drain(r)
             for j in reversed(range(n)):
-                part = dot(dq[j * size : (j + 1) * size, :], w_cross[:, :hid], NT)
+                part = dot(dkv[j * size : (j + 1) * size, :], w_kv[...], NT)
+                if j:
+                    sums_m.put(r, j, part)
+                else:
+                    rest[r] = part
+
+            @pl.when(r > 0)
+            def _():
+                finish_memory(r - 1)
+
+        sums_m.forward(last)
+        finish_memory(last)
+
+        idx = lax.axis_index("mp")
+        bits = [j for j in range(1, n) if j == low_bit(j)]
+        for bit in bits:
+            pl.semaphore_signal(
+                ready, inc=1, device_id={"mp": flipped(idx, bit)}, device_id_type=MESH
+            )
+        pl.semaphore_wait(ready, len(bits))
+
+        @pl.loop(0, rows)
+        def _(r):
+            sums_m.drain(r)
+
+            @pl.when(r > 0)
+            def _():
+                mid_load(1, mid1_in, r - 1).start()
+
+            for j in reversed(range(n)):
+                part = dot(dq[r, j * size : (j + 1) * size, :], w_cross[:, :hid], NT)
                 if j:
                     sums_b.put(r, j, part)
                 else:
@@ -948,6 +1092,7 @@
 
             @pl.when(r > 0)
             def _():
+                sums_b.forward(r - 1)
                 finish_second(r - 1, sums_b)
 
         sums_b.forward(last)
@@ -957,10 +1102,11 @@
         @pl.loop(0, rows)
         def _(r):
             pair_copy(r).wait_send()
+            dq_save(r).wait()
 
         for j in range(n):
             part_save(last, j).wait()
-        pltpu.make_async_copy(dq, dq_out.at[last], save_d.at[0]).wait()
+        dkv_save(last).wait()
 
     @pl.when(enc)
     def _():
@@ -972,15 +1118,8 @@
             def _():
                 mid_load(0, mid2_in, t).start()
                 pair_copy(t).wait_recv()
-                pltpu.make_async_copy(dkv.at[t], dkv_out.at[t], save_d.at[1 + t]).start()
-                for j in reversed(range(n)):
-                    at = slice(j * size, (j + 1) * size)
-                    part = dot(dkv[t, at, :], w_cross[...], NT)
-                    if j:
-                        sums_a.put(t, j, part)
-                    else:
-                        rest[t] = part
-                sums_a.forward(t)
+                finish_third(t, None, True)
+                gather_g.start(t)
 
             @pl.when(t > 0)
             def _():
@@ -991,7 +1130,6 @@
                 for copy in block_saves(gather_g, full_g, save_g, r):
                     copy.start()
                 full_load(fwd_in, r).wait()
-                sums_a.drain(r)
                 feed_forward(
                     r,
                     lambda j: full[j * size : (j + 1) * size, :],
@@ -1004,19 +1142,8 @@
                 def _():
                     full_load(fwd_in, r + 1).start()
 
-            @pl.when(t < rows)
-            def _():
-                finish_third(t, sums_a, True)
-                gather_g.start(t)
-
-            @pl.when(t > 0)
-            def _():
-                sums_b.forward(t - 1)
-                finish_second(t - 1, sums_b)
-
-        @pl.loop(0, rows)
-        def _(r):
-            pltpu.make_async_copy(dkv.at[r], dkv_out.at[r], save_d.at[1 + r]).wait()
+                sums_b.forward(r)
+                finish_second(r, sums_b)
 
     for copy in ffn_saves(last):
         copy.wait()
@@ -1039,11 +1166,13 @@
     w_up,
     w_down,
     w_cross,
+    w_kv,
     key_aug,
     mid1,
     mid2,
     fwd,
     full_cot,
+    full_t,
     kv,
     q,
     mix,
@@ -1054,13 +1183,13 @@
     slots = (rows, n - 1)
     full = ((rows, length, width), BF, False)
     unit = ((rows, length, ffd), BF, False)
-    near = (third, cot, gain2, gain1, w_gate, w_up, w_down, w_cross, key_aug)
+    near = (third, cot, gain2, gain1, w_gate, w_up, w_down, w_cross, w_kv, key_aug)
     return call_stage(
         functools.partial(middle_back_kernel, n),
         "middle_back_stage",
         4,
         [(a, True) for a in near]
-        + [(a, False) for a in (mid1, mid2, fwd, full_cot, kv, q, mix, aug)],
+        + [(a, False) for a in (mid1, mid2, fwd, full_cot, full_t, kv, q, mix, aug)],
         [
             ((rows, size, width), F32, True),
             ((2, 8, width), F32, True),
@@ -1077,14 +1206,17 @@
             pltpu.VMEM((rows, size, width), BF),
             *[pltpu.VMEM((*slots, size, width), BF)] * 3,
             pltpu.VMEM((rows, size, width), F32),
-            pltpu.VMEM((rows, length, 2 * hid), BF),
+            pltpu.VMEM((rows, size, width), BF),
             pltpu.VMEM((2, size, width), F32),
             pltpu.VMEM((length, width), BF),
             pltpu.VMEM((length, 2 * hid), BF),
-            *[pltpu.VMEM((length, hid), BF)] * 4,
+            *[pltpu.VMEM((length, hid), BF)] * 3,
+            pltpu.VMEM((rows, length, hid), BF),
+            pltpu.VMEM((length, 2 * hid), BF),
             *[pltpu.VMEM((length, ffd), BF)] * 3,
             pltpu.VMEM((n, size, width), BF),
-            *[pltpu.SemaphoreType.DMA(slots)] * 8,
+            pltpu.SemaphoreType.REGULAR,
+            *[pltpu.SemaphoreType.DMA(slots)] * 10,
             *[pltpu.SemaphoreType.DMA((rows,))] * 2,
             *[pltpu.SemaphoreType.DMA((rows, n))] * 2,
             pltpu.SemaphoreType.DMA((rows, 3)),
@@ -1098,7 +1230,7 @@
     )
 
 
-def weight_kernel(places, stacked, *refs):
+def weight_kernel(places, stacked, extra, *refs):
     out, acc = refs[-2:]
     at = pl.program_id(0)
 
@@ -1116,10 +1248,12 @@
 
     @pl.when(at == pl.num_programs(0) - 1)
     def _():
-        out[...] = acc[...].astype(BF)
-
-
-def weight_sums(pairs, stacked):
+        out[: acc.shape[0], :] = acc[...].astype(BF)
+        if extra:
+            out[acc.shape[0] :, :] = jnp.zeros((extra, acc.shape[1]), BF)
+
+
+def weight_sums(pairs, stacked, extra=0):
     arrays, places, start = [], [], 0
 
     def index(array):
@@ -1137,12 +1271,13 @@
     other = pairs[0][1 if stacked else 0].shape[-1]
     shape = (start, other) if stacked else (other, start)
     tokens, step = flat[0].shape[0], 512
+    whole = (shape[0] + extra, shape[1])
     return pl.pallas_call(
-        functools.partial(weight_kernel, places, stacked),
+        functools.partial(weight_kernel, places, stacked, extra),
         grid=(tokens // step,),
         in_specs=[pl.BlockSpec((step, a.shape[1]), lambda i: (i, 0)) for a in flat],
-        out_specs=pl.BlockSpec(shape, lambda i: (0, 0)),
-        out_shape=jax.ShapeDtypeStruct(shape, BF),
+        out_specs=pl.BlockSpec(whole, lambda i: (0, 0)),
+        out_shape=jax.ShapeDtypeStruct(whole, BF),
         scratch_shapes=[pltpu.VMEM(shape, F32)],
         compiler_params=pltpu.CompilerParams(vmem_limit_bytes=VMEM_LIMIT),
         cost_estimate=pl.CostEstimate(
@@ -1174,8 +1309,7 @@
     w_down = ffn_out[0]
     w_cross = cross_weight[0].reshape(width, 2 * hid)
     gain = gains[0]
-    x_low = jnp.swapaxes(block_input[0], 0, 1)
-    x = x_low.astype(F32)
+    x = jnp.swapaxes(block_input[0], 0, 1)
     cot = jnp.swapaxes(cotangent[0], 0, 1)
 
     order = jnp.arange(n, dtype=jnp.int32) ^ idx
@@ -1203,19 +1337,19 @@
     tri = jnp.where(above & ~enc, BIG, 0.0).astype(F32)
     key_own, key_enc = key_features(own), key_features(local[0])
 
-    sum1, full1, qkv1, mix1, aug1 = self_stage(
+    mid1, normed2, full1, qkv1, mix1, aug1 = self_stage(
         n,
-        norm_scale(x, gain[0]).astype(BF),
+        x,
+        gain,
         w_qkv,
         w_out,
         query_features(own, ~enc),
         key_own,
         tri,
     )
-    mid1 = x + sum1
-    mid2, third, full_a, full_b, full_cot, kv, q, mix, aug = middle_stage(
+    mid2, third, full_a, full_b, full_cot, full_t, w_kv, kv, q, mix, aug = middle_stage(
         n,
-        norm_scale(mid1, gain[1]).astype(BF),
+        normed2,
         cot,
         mid1,
         gain[2:3],
@@ -1237,11 +1371,13 @@
         w_up,
         w_down,
         w_cross,
+        w_kv,
         key_enc,
         mid1,
         mid2,
         full_a,
         full_cot,
+        full_t,
         kv,
         q,
         mix,
@@ -1251,15 +1387,24 @@
     def over_rows(total, dim):
         return lax.psum_scatter(total, "dp", scatter_dimension=dim, tiled=True)
 
+    sum_kv = lax.cond(
+        enc,
+        lambda: jnp.zeros((2 * hid, width), BF),
+        lambda: weight_sums([(dkv, full_b)], True),
+    )
+    sum_kv = lax.ppermute(sum_kv, "section", [(1, 0)])
     early = lax.cond(
         enc,
         lambda: weight_sums(
-            [(dgate, full_a), (dup, full_a), (hidden, full_g), (dkv, full_b)], True
+            [(dgate, full_a), (dup, full_a), (hidden, full_g)], True, 2 * hid
         ),
         lambda: weight_sums(
             [(dgate, full_3), (dup, full_3), (hidden, full_cot), (dq, full_a), (mix, full_g)],
             True,
         ),
+    )
+    early = lax.dynamic_update_slice(
+        early, jnp.where(enc, sum_kv, early[3 * ffd :]), (3 * ffd, 0)
     )
     got_early = over_rows(early, 1)
 
@@ -1279,14 +1424,11 @@
     dec_out = mid2 + have[0].astype(F32)
     block_out = jnp.where(enc, third, dec_out.astype(BF))
 
-    grad1_low, _, _ = lax.optimization_barrier((grad1.astype(BF), early, first))
-    sum2, full_s, dqkv = self_back_stage(
-        n, grad1_low, w_qkv, w_out, key_own, tri.T, qkv1, mix1, aug1
+    grad1, _, _ = lax.optimization_barrier((grad1, early, first))
+    input_grad, gain_first, late = self_back_stage(
+        n, x, gain, grad1, w_qkv, w_out, key_own, tri.T, qkv1, mix1, aug1, full1
     )
-    part, gain_first = norm_back(x, gain[0], sum2)
-    input_grad = grad1 + part
-
-    late = weight_sums([(full1, dqkv), (full_s, mix1)], False)
+
     late, got_early = lax.optimization_barrier((late, got_early))
     got_late = over_rows(late, 0).astype(F32)
     got_early = got_early.astype(F32)
@@ -1297,7 +1439,7 @@
     out_qkv = got_late[:, : 3 * hid].reshape(quarter, 3, hid)
     out_out = got_late[:, 3 * hid :].T
     gain_parts = jnp.sum(gain_parts, axis=1)
-    gain_total = jnp.stack([gain_first, gain_parts[1], gain_parts[0]])
+    gain_total = jnp.stack([jnp.sum(gain_first, axis=0), gain_parts[1], gain_parts[0]])
     for axis, count in (("mp", n), ("dp", dp_size)):
         for bit in (1 << b for b in range(count.bit_length() - 1)):
             other = lax.ppermute(gain_total, axis, [(i, i ^ bit) for i in range(count)])

time: 791 us -> 715 us (0.904)
  waiting for transfers between devices: 113 us -> 41.1 us
  starting transfers between devices: 11.6 us -> 48.3 us
  Pallas kernels: 585 us -> 560 us
  other arithmetic: 34.9 us -> 17.6 us
    reduce_scatter x2, waiting for transfers between devices: 76.3 us -> 0.02 us  [over_rows(): return lax.psum_scatter(total, 'dp', scatter_dimension=dim, tiled=True)]
    ppermute x0 -> x1, starting transfers between devices: none -> 35 us  [body(): sum_kv = lax.ppermute(sum_kv, 'section', [(1, 0)])]
    pallas_call x4, Pallas kernels: 547 us -> 528 us  [call_stage(): pl.pallas_call(kernel, in_specs=[vmem if near else hbm for _, near in inp...]
    reduce_sum x3 -> x1, other arithmetic: 8.95 us -> 0.01 us  [body(): jnp.sum(gain_first, axis=0)]
  transfers between devices with their start and end apart: 9 -> 10, of which waited for: 5 -> 5; matrix products, arithmetic and copies ran while one was open for 3% -> 3% of each run, Pallas kernels for 12% -> 16%
where the time goes in v4:
time: 715 us; the launch traced here: 710 us
  Pallas kernels  560 us (78%)
  starting transfers between devices  48.3 us (7%)
  waiting for transfers between devices  41.1 us (6%)
  local copies, waits for them, and re-layouts  27.8 us (4%)
  other arithmetic  17.6 us (2%)
  between operations  14.6 us (2%)
    pallas_call x4, Pallas kernels, call_stage(): pl.pallas_call(kernel, in_specs=[vmem if near else hbm for _, near in inp...  528 us
    ppermute x4, waiting for transfers between devices, body(): other = lax.ppermute(gain_total, axis, [(i, i ^ bit) for i in range(count)])  38.4 us
    ppermute x1, starting transfers between devices, body(): sum_kv = lax.ppermute(sum_kv, 'section', [(1, 0)])  35 us
    pallas_call x2, Pallas kernels, weight_sums(): pl.pallas_call(functools.partial(weight_kernel, places, stacked, extra),...  32.5 us
  transfers between devices with their start and end apart: 10, of which 5 were waited for; matrix products, arithmetic and copies ran while one was open for 3% of the time, Pallas kernels for 16%

profile of v4, /device:TPU:2, one launch (start us, length us, event | category | flops | bytes accessed | tf_op | source)
XLA Modules:
  0.0 710.1 jit_solution(18092986549047094526)
XLA Ops:
  7.2 0.0 reduce-scatter.3.cloned.1.call-start
  7.2 0.8 constant_dynamic-slice_fusion
  8.1 1.3 copy.52
  9.4 1.3 slice_bitcast_fusion.6
  10.7 0.1 broadcast_bitcast_fusion
  10.8 0.7 fusion.12.refs_6_
  11.5 1.7 copy.24
  13.3 1.6 copy.29.refs_2_.refs_3_
  14.8 2.1 fusion.17
  16.9 1.6 copy.43
  18.5 1.6 copy.44
  20.0 0.0 copy-done.3
  20.0 1.2 copy.46
  21.2 0.2 broadcast_compare_fusion
  21.5 4.4 select_convert_fusion
  25.9 80.9 %self_stage.1 = (f32[3,256,1024]{2,1,0:T(8,128)}, bf16[3,256,1024]{2,1,0:T(8,128)(2,1)}, bf16[3,1024,1024]{2,1,0:T(8,128)(2,1)}, bf16[3,1024,768]{2,1,0:T(8,128)...) custom-call(bf16[3,256,1024]{2,1,0:T(8,128)(2,1)} %bitcast.95, f32[3,1024]{1,0:T(4,128)} %bitcast.91, ...), custom_call_target="tpu_custom_call" | custom-call | flops 19327352832 | bytes 33554432 | tf_op jit(solution)/shard_map/self_stage/pallas_call | solution.py:273
  106.7 163.9 %middle_stage.1 = (f32[3,256,1024]{2,1,0:T(8,128)}, bf16[3,256,1024]{2,1,0:T(8,128)(2,1)}, bf16[3,1024,1024]{2,1,0:T(8,128)(2,1)}, bf16[3,1024,1024]{2,1,0:T(8,1...) custom-call(bf16[3,256,1024]{2,1,0:T(8,128)(2,1)} %get-tuple-element, ...), custom_call_target="tpu_custom_call" | custom-call | flops 26172456960 | bytes 33554432 | tf_op jit(solution)/shard_map/middle_stage/pallas_call | solution.py:273
  270.6 0.0 copy-start.6
  270.6 196.0 %middle_back_stage.1 = (f32[3,256,1024]{2,1,0:T(8,128)}, f32[2,8,1024]{2,1,0:T(8,128)}, bf16[3,1024,1024]{2,1,0:T(8,128)(2,1)}, bf16[3,1024,1024]{2,1,0:T(8,128)...) custom-call(bf16[3,256,1024]{2,1,0:T(8,128)(2,1)} %get-tuple-element, ...), custom_call_target="tpu_custom_call" | custom-call | flops 67645734912 | bytes 33554432 | tf_op jit(solution)/shard_map/middle_back_stage/pallas_call | solution.py:273
  466.7 0.0 copy-done.6
  466.7 7.7 %conditional.3 = (bf16[512,1024]{1,0:T(8,128)(2,1)S(1)}) conditional(s32[]{:T(128)} %convert_element_type.62, (bf16[3,1024,512]{2,1,0:T(8,128)(2,1)}, bf16[3,1024,1024]{2,1,0:T(8,128)(2,1)}) %tuple.28, () %tuple.29), branch_computations={%region_2.3_spmd, %region_3.4_spmd} | conditional | flops 3221225472 | bytes 9437192 | solution.py:1390
  466.7 7.6 %weight_sums.5 = bf16[512,1024]{1,0:T(8,128)(2,1)S(1)} custom-call(bf16[3072,512]{1,0:T(8,128)(2,1)} %bitcast.114, bf16[3072,1024]{1,0:T(8,128)(2,1)} %bitcast.107), custom_call_target="tpu_custom_call" | custom-call | flops 3221225472 | bytes 9437184 | tf_op jit(solution)/shard_map/cond/branch_0_fun/weight_sums/pallas_call | solution.py:1275
  474.3 35.0 %collective-permute-start.3 = (bf16[512,1024]{1,0:T(8,128)(2,1)S(1)}, bf16[512,1024]{1,0:T(8,128)(2,1)S(1)}, u32[]{:S(2)}, u32[]{:S(2)}) collective-permute-start(bf16[512,1024]{1,0:T(8,128)(2,1)S(1)} %get-tuple-element.192), channel_id=1, source_target_pairs={{16,0},{17,1},{18,2},{19,3},{20,4},{21,5},{22,6},{23,7},{24,8},{25... | collective-permute-start | bytes 3145736 | tf_op jit(solution)/shard_map/ppermute | solution.py:1395
  509.4 26.6 %conditional.2 = (bf16[2624,1024]{1,0:T(8,128)(2,1)}, bf16[512,1024]{1,0:T(8,128)(2,1)S(1)}) conditional(s32[]{:T(128)} %convert_element_type.62, (bf16[3,1024,704]{2,1,0:T(8,128)(2,1)}, bf16[3,1024,1024]{2,1,0:T(8,128)(2,1)}, bf16[3,1024,704]{2,1,0:T(8,128)(2,1)}, bf16[3,1024,704]{2,1,0:T(8,128)(2,1)}, bf16[3,1024,1024]{2,1,0:T(8,128)(2,1)}, ...), branch_computations={%region_0.1_spmd, %region_1.2_spmd} | conditional | flops 16508780544 | bytes 43384848 | solution.py:1396
  509.8 24.8 %weight_sums.3 = bf16[2624,1024]{1,0:T(8,128)(2,1)} custom-call(bf16[3072,704]{1,0:T(8,128)(2,1)} %bitcast.110, bf16[3072,1024]{1,0:T(8,128)(2,1)} %bitcast.104, bf16[3072,704]{1,0:T(8,128)(2,1)} %bitcast.112, bf16[3072,704]{1,0:T(8,128)(2,1)} %bitcast.108, bf16[3072,1024]{1,0:T(8,128)(2,1)} %bitcast.103, bf16[3072,256]{1,0:T(8,128)(2,1)} %bitcast.116, ...), custom_call_target="tpu_custom_call" | custom-call | flops 16508780544 | bytes 41287680 | tf_op jit(solution)/shard_map/cond/branch_0_fun/weight_sums/pallas_call | solution.py:1275
  534.7 1.3 slice.92
  536.0 0.0 collective-permute-done.3
  536.0 1.4 select_dynamic-update-slice_fusion
  537.4 0.0 reduce-scatter.3.cloned.1.call-update
  537.4 0.0 reduce-scatter.5.cloned.1.call-start
  537.4 3.4 fusion.16
  540.8 1.9 collective-permute-start.1
  542.8 0.7 fusion.14.refs_6_
  543.5 2.6 collective-permute-done.1
  546.1 3.2 add_convert_fusion.1
  549.4 87.1 %self_back_stage.1 = (f32[3,256,1024]{2,1,0:T(8,128)}, f32[8,1024]{1,0:T(8,128)}, bf16[1024,1024]{1,0:T(8,128)(2,1)}) custom-call(bf16[3,256,1024]{2,1,0:T(8,128)(2,1)} %bitcast.96, f32[3,1024]{1,0:T(4,128)} %bitcast.92, f32[3,256,1024]{2,1,0:T(8,128)} %get-tuple-element.120.refs_2_, bf16[1024,768]{1,0:T(8,128)(2,1)} %copy.29.refs_2_.refs_3_, ...), custom_call_target="tpu_custom_call" | custom-call | flops 38654705664 | bytes 33554432 | tf_op jit(solution)/shard_map/self_back_stage/pallas_call | solution.py:273
  636.4 0.0 copy-start.4
  636.5 0.0 reduce-scatter.3.cloned.1.call-done
  636.5 0.0 reduce-scatter.5.cloned.1.call-update
  636.5 2.0 collective-permute-start
  638.5 3.8 collective-permute-start.2
  642.4 0.1 collective-permute-start.4
  642.6 1.1 collective-permute-done.4
  643.7 0.2 collective-permute-start.5
  643.9 33.9 %collective-permute-done.5 = f32[3,1024]{1,0:T(4,128)S(1)} collective-permute-done((f32[3,1024]{1,0:T(4,128)S(1)}, f32[3,1024]{1,0:T(4,128)S(1)}, u32[]{:S(2)}, u32[]{:S(2)}) %collective-permute-start.5) | collective-permute-done | bytes 12320 | tf_op jit(solution)/shard_map/ppermute | solution.py:1445
  677.8 2.1 collective-permute-start.6
  679.9 1.7 collective-permute-done.6
  681.6 3.0 collective-permute-start.7
  684.6 1.7 collective-permute-done.7
  686.3 0.1 dynamic-slice_add_fusion
  686.4 0.6 broadcast_in_dim.76
  687.0 0.0 collective-permute-done
  687.0 0.0 collective-permute-done.2
  687.0 5.2 fusion.1
  692.2 0.2 convert_element_type.64
  692.5 1.0 copy.37
  693.5 1.0 slice_bitcast_fusion
  694.4 1.2 maximum_bitcast_fusion
  695.6 1.0 slice.96
  696.7 0.3 copy.33
  697.0 1.1 copy.35
  698.1 0.1 convert_element_type.63
  698.3 0.8 copy.36
  699.1 4.0 copy.64
  (31 shorter events, 0.3 us)
Async XLA Ops:
  7.2 629.3 %reduce-scatter.3.cloned.1.call-start = ((), (), s32[]{:S(2)}) async-start(), calls=%async_computation.2 | async-start | bytes 6717440 | tf_op jit(solution)/shard_map/reduce_scatter | solution.py:1388
  18.5 1.6 copy-start.3
  270.6 196.0 %copy-start.6 = (bf16[3,1024,256]{2,1,0:T(8,128)(2,1)}, bf16[3,1024,256]{2,1,0:T(8,128)(2,1)S(1)}, u32[]{:S(2)}) copy-start(bf16[3,1024,256]{2,1,0:T(8,128)(2,1)S(1)} %get-tuple-element.106.refs_17_) | copy-start | bytes 4718596
  474.3 61.6 %collective-permute-start.3 = (bf16[512,1024]{1,0:T(8,128)(2,1)S(1)}, bf16[512,1024]{1,0:T(8,128)(2,1)S(1)}, u32[]{:S(2)}, u32[]{:S(2)}) collective-permute-start(bf16[512,1024]{1,0:T(8,128)(2,1)S(1)} %get-tuple-element.192), channel_id=1, source_target_pairs={{16,0},{17,1},{18,2},{19,3},{20,4},{21,5},{22,6},{23,7},{24,8},{25... | collective-permute-start | bytes 3145736 | tf_op jit(solution)/shard_map/ppermute | solution.py:1395
  537.4 158.3 %reduce-scatter.5.cloned.1.call-start = ((), (), s32[]{:S(2)}) async-start(), calls=%async_computation.3 | async-start | bytes 2621440 | tf_op jit(solution)/shard_map/reduce_scatter | solution.py:1388
  540.8 5.3 collective-permute-start.1
  549.4 137.6 %copy-start.1 = (f32[3,256,1024]{2,1,0:T(8,128)S(1)}, f32[3,256,1024]{2,1,0:T(8,128)}, u32[]{:S(2)}) copy-start(f32[3,256,1024]{2,1,0:T(8,128)} %get-tuple-element.99.refs_11_) | copy-start | bytes 9437188
  636.4 5.9 copy-start.4
  636.5 5.9 copy-start.5
  636.5 50.5 %collective-permute-start = (bf16[3,256,1024]{2,1,0:T(8,128)(2,1)}, bf16[3,256,1024]{2,1,0:T(8,128)(2,1)}, u32[]{:S(2)}, u32[]{:S(2)}) collective-permute-start(bf16[3,256,1024]{2,1,0:T(8,128)(2,1)} %get-tuple-element.147), channel_id=1, source_target_pairs={{16,17},{17,16},{18,19},{19,18},{20,21},{21,20},{22,23},{23,22},{2... | collective-permute-start | bytes 4718600 | tf_op jit(solution)/shard_map/ppermute | solution.py:1413
  638.5 48.5 %collective-permute-start.2 = (bf16[3,256,1024]{2,1,0:T(8,128)(2,1)}, bf16[3,256,1024]{2,1,0:T(8,128)(2,1)}, u32[]{:S(2)}, u32[]{:S(2)}) collective-permute-start(bf16[3,256,1024]{2,1,0:T(8,128)(2,1)} %add_convert_fusion.1), channel_id=1, source_target_pairs={{16,18},{17,19},{18,16},{19,17},{20,22},{21,23},{22,20},{23,21},{2... | collective-permute-start | bytes 4718600 | tf_op jit(solution)/shard_map/ppermute | solution.py:1413
  642.4 1.2 collective-permute-start.4
  643.7 34.1 %collective-permute-start.5 = (f32[3,1024]{1,0:T(4,128)S(1)}, f32[3,1024]{1,0:T(4,128)S(1)}, u32[]{:S(2)}, u32[]{:S(2)}) collective-permute-start(f32[3,1024]{1,0:T(4,128)S(1)} %fusion.15), channel_id=1, source_target_pairs={{0,2},{1,3},{2,0},{3,1},{4,6},{5,7},{6,4},{7,5},{8,10},{9,11},{10,... | collective-permute-start | bytes 36872 | tf_op jit(solution)/shard_map/ppermute | solution.py:1445
  677.8 3.8 collective-permute-start.6
  681.6 4.7 collective-permute-start.7
  687.0 5.2 copy-start.2
  696.7 1.4 copy-start
Sparse Core Ops, SparseCore 0:
  537.5 96.5 reduce-scatter.2
  636.6 45.8 reduce-scatter.4

commit v5 on v4

--- a/solution.py
+++ b/solution.py
@@ -405,20 +405,28 @@
 
 
 def self_back_kernel(n, *refs):
-    (x, gain, slope, w_qkv, w_out, key_aug, tri_t, qkv_in, mix_in, aug_in, full_in) = refs[:11]
-    (total, gain_out, weights) = refs[11:14]
-    (own, got, out, back, qkv, mix, aug, grad, dqkv, full, acc) = refs[14:25]
-    sems = refs[25:]
+    (x, gain, slope, w_qkv, w_out, key_aug, tri_t) = refs[:7]
+    (qkv_in, mix_in, aug_in, full_in, ahead_in) = refs[7:12]
+    (total, gain_out, weights) = refs[12:15]
+    (own, got, out, back, qkv, mix, aug, grad, dqkv, full, acc) = refs[15:26]
+    sems = refs[26:]
     rows, size = x.shape[:2]
     hid = w_out.shape[0]
     gather = Gather(n, own, got, *sems[:2])
     sums = Sums(n, out, back, *sems[2:4])
-    load, load_full = sems[4:]
+    load, load_full, load_ahead = sems[4:]
+    ahead = 1 if rows > 1 else 0
     greet(n)
 
     def loads(r):
         for i, (src, dst) in enumerate(((qkv_in, qkv), (mix_in, mix), (aug_in, aug))):
             yield pltpu.make_async_copy(src.at[r], dst.at[r], load.at[r, i])
+
+    def ahead_loads():
+        for j in range(1, n):
+            yield pltpu.make_async_copy(
+                ahead_in.at[pl.ds(j * size, size)], got.at[0, j - 1], load_ahead.at[j]
+            )
 
     def full_load(r):
         return pltpu.make_async_copy(full_in.at[r], full, load_full.at[0])
@@ -443,17 +451,30 @@
 
     for r in range(rows):
         own[r] = slope[r].astype(BF)
-        gather.start(r)
+        if r >= ahead:
+            gather.start(r)
+        else:
+            for copy in ahead_loads():
+                copy.start()
         for copy in loads(r):
             copy.start()
     full_load(0).start()
     gain_out[...] = jnp.zeros_like(gain_out)
     acc[...] = jnp.zeros_like(acc)
-    gather.forward(0)
+    if not ahead:
+        gather.forward(0)
 
     @pl.loop(0, rows)
     def _(r):
-        gather.finish(r)
+        @pl.when(r < ahead)
+        def _():
+            for copy in ahead_loads():
+                copy.wait()
+
+        @pl.when(r >= ahead)
+        def _():
+            gather.finish(r)
+
         for j in range(n):
             grad[j * size : (j + 1) * size, :] = dot(
                 gather.block(r, j)[...], w_out[...], NT
@@ -506,11 +527,16 @@
 
     @pl.loop(0, rows)
     def _(r):
-        gather.drain(r)
+        @pl.when(r >= ahead)
+        def _():
+            gather.drain(r)
+
         sums.drain(r)
 
 
-def self_back_stage(n, x, gain, slope, w_qkv, w_out, key_aug, tri_t, qkv, mix, aug, full):
+def self_back_stage(
+    n, x, gain, slope, w_qkv, w_out, key_aug, tri_t, qkv, mix, aug, full, first
+):
     rows, size, width = x.shape
     length, hid = n * size, w_out.shape[0]
     slots = (rows, n - 1)
@@ -519,7 +545,7 @@
         "self_back_stage",
         2,
         [(a, True) for a in (x, gain, slope, w_qkv, w_out, key_aug, tri_t)]
-        + [(a, False) for a in (qkv, mix, aug, full)],
+        + [(a, False) for a in (qkv, mix, aug, full, first)],
         [
             ((rows, size, width), F32, True),
             ((8, width), F32, True),
@@ -538,6 +564,7 @@
             *[pltpu.SemaphoreType.DMA(slots)] * 4,
             pltpu.SemaphoreType.DMA((rows, 3)),
             pltpu.SemaphoreType.DMA((1,)),
+            pltpu.SemaphoreType.DMA((n,)),
         ],
         rows * length * width * hid * 8 + rows * length * length * hid * 40,
     )
@@ -820,11 +847,11 @@
     (mid1_in, mid2_in, fwd_in, cot_in, third_in) = refs[10:15]
     (kv_in, q_in, mix_in, aug_in) = refs[15:19]
     (grad, gain_out, parts_out, full_3, full_g) = refs[19:24]
-    (hidden_out, dgate_out, dup_out, dkv_out, dq_out) = refs[24:29]
-    (own, got, out, back, rest, dmem) = refs[29:35]
-    (mid, full, kv, q, mix, aug, dq, dkv, hidden_s, dgate_s, dup_s, part_s) = refs[35:47]
-    ready = refs[47]
-    sems = refs[48:]
+    (hidden_out, dgate_out, dup_out, dkv_out, dq_out, ahead_out) = refs[24:30]
+    (own, got, out, back, rest, dmem) = refs[30:36]
+    (mid, full, kv, q, mix, aug, dq, dkv, hidden_s, dgate_s, dup_s, part_s) = refs[36:48]
+    ready = refs[48]
+    sems = refs[49:]
     rows, size = third.shape[:2]
     hid = q.shape[1]
     enc = lax.axis_index("section") == 0
@@ -833,7 +860,10 @@
     sums_a = Sums(n, out, back, *sems[4:6])
     sums_b = Sums(n, out, back, *sems[6:8])
     sums_m = Sums(n, out, back, *sems[8:10])
-    pair_send, pair_recv, save_3, save_g, save_f, save_p, save_d, load_m, load_f, load_x = sems[10:]
+    gather_s = Gather(n, own, got, *sems[10:12])
+    pair_send, pair_recv, save_3, save_g, save_f, save_p, save_d, load_m, load_f, load_x = sems[12:22]
+    save_s = sems[22]
+    ahead = 1 if rows > 1 else 0
     greet(n, True)
     gain_out[...] = jnp.zeros_like(gain_out)
 
@@ -941,6 +971,25 @@
 
     last = rows - 1
 
+    def lead():
+        own[0] = grad[0].astype(BF)
+        gather_s.start(0)
+
+    def lead_saves():
+        for j in range(n):
+            yield pltpu.make_async_copy(
+                gather_s.block(0, j), ahead_out.at[pl.ds(j * size, size)], save_s.at[j]
+            )
+
+    def finish_lead():
+        if ahead:
+            gather_s.finish(0)
+            for copy in lead_saves():
+                copy.start()
+            for copy in lead_saves():
+                copy.wait()
+            gather_s.drain(0)
+
     @pl.when(jnp.logical_not(enc))
     def _():
         def third_loads(r):
@@ -949,7 +998,6 @@
                     third_in.at[r, pl.ds(j * size, size)], got.at[r, j - 1], save_3.at[r, j]
                 )
 
-        ahead = 1 if rows > 1 else 0
         for r in range(ahead, rows):
             gather_3.start(r)
         full_load(cot_in, 0).start()
@@ -1078,6 +1126,9 @@
         @pl.loop(0, rows)
         def _(r):
             sums_m.drain(r)
+            gather_g.drain(r)
+            for copy in block_saves(gather_g, full_g, save_g, r):
+                copy.wait()
 
             @pl.when(r > 0)
             def _():
@@ -1095,9 +1146,16 @@
                 sums_b.forward(r - 1)
                 finish_second(r - 1, sums_b)
 
+            @pl.when(r == 1)
+            def _():
+                lead()
+
         sums_b.forward(last)
         mid_load(1, mid1_in, last).start()
+        if ahead:
+            gather_s.forward(0)
         finish_second(last, sums_b)
+        finish_lead()
 
         @pl.loop(0, rows)
         def _(r):
@@ -1121,15 +1179,20 @@
                 finish_third(t, None, True)
                 gather_g.start(t)
 
+            @pl.when(t > 1)
+            def _():
+                mid_load(1, mid1_in, t - 2).start()
+
             @pl.when(t > 0)
             def _():
                 r = t - 1
-                mid_load(1, mid1_in, r).start()
                 gather_g.forward(r)
                 gather_g.finish(r)
                 for copy in block_saves(gather_g, full_g, save_g, r):
                     copy.start()
                 full_load(fwd_in, r).wait()
+                for copy in block_saves(gather_g, full_g, save_g, r):
+                    copy.wait()
                 feed_forward(
                     r,
                     lambda j: full[j * size : (j + 1) * size, :],
@@ -1142,18 +1205,29 @@
                 def _():
                     full_load(fwd_in, r + 1).start()
 
+                gather_g.drain(r)
                 sums_b.forward(r)
-                finish_second(r, sums_b)
+
+            @pl.when(t > 1)
+            def _():
+                finish_second(t - 2, sums_b)
+
+            @pl.when(t == 2)
+            def _():
+                lead()
+
+        mid_load(1, mid1_in, last).start()
+        if ahead:
+            gather_s.forward(0)
+        finish_second(last, sums_b)
+        finish_lead()
 
     for copy in ffn_saves(last):
         copy.wait()
 
     @pl.loop(0, rows)
     def _(r):
-        gather_g.drain(r)
         sums_b.drain(r)
-        for copy in block_saves(gather_g, full_g, save_g, r):
-            copy.wait()
 
 
 def middle_back_stage(
@@ -1201,6 +1275,7 @@
             unit,
             ((rows, length, 2 * hid), BF, False),
             ((rows, length, hid), BF, False),
+            ((length, width), BF, False),
         ],
         [
             pltpu.VMEM((rows, size, width), BF),
@@ -1216,7 +1291,7 @@
             *[pltpu.VMEM((length, ffd), BF)] * 3,
             pltpu.VMEM((n, size, width), BF),
             pltpu.SemaphoreType.REGULAR,
-            *[pltpu.SemaphoreType.DMA(slots)] * 10,
+            *[pltpu.SemaphoreType.DMA(slots)] * 12,
             *[pltpu.SemaphoreType.DMA((rows,))] * 2,
             *[pltpu.SemaphoreType.DMA((rows, n))] * 2,
             pltpu.SemaphoreType.DMA((rows, 3)),
@@ -1225,6 +1300,7 @@
             pltpu.SemaphoreType.DMA((2,)),
             pltpu.SemaphoreType.DMA((1,)),
             pltpu.SemaphoreType.DMA((4,)),
+            pltpu.SemaphoreType.DMA((n,)),
         ],
         rows * length * width * ffd * 16 + rows * length * length * hid * 40,
     )
@@ -1361,7 +1437,7 @@
         key_enc,
     )
 
-    grad1, gain_parts, parts, full_3, full_g, hidden, dgate, dup, dkv, dq = middle_back_stage(
+    back_results = middle_back_stage(
         n,
         third,
         cot,
@@ -1384,6 +1460,8 @@
         aug,
     )
 
+    grad1, gain_parts, parts, full_3, full_g, hidden, dgate, dup, dkv, dq, lead = back_results
+
     def over_rows(total, dim):
         return lax.psum_scatter(total, "dp", scatter_dimension=dim, tiled=True)
 
@@ -1426,7 +1504,7 @@
 
     grad1, _, _ = lax.optimization_barrier((grad1, early, first))
     input_grad, gain_first, late = self_back_stage(
-        n, x, gain, grad1, w_qkv, w_out, key_own, tri.T, qkv1, mix1, aug1, full1
+        n, x, gain, grad1, w_qkv, w_out, key_own, tri.T, qkv1, mix1, aug1, full1, lead
     )
 
     late, got_early = lax.optimization_barrier((late, got_early))

time: 715 us -> 703 us (0.983)
  starting transfers between devices: 48.3 us -> 23.1 us
  waiting for transfers between devices: 41.1 us -> 52.4 us
    ppermute x1, starting transfers between devices: 35 us -> 11 us  [body(): sum_kv = lax.ppermute(sum_kv, 'section', [(1, 0)])]
    reduce_scatter x2, waiting for transfers between devices: 0.02 us -> 9.72 us  [over_rows(): return lax.psum_scatter(total, 'dp', scatter_dimension=dim, tiled=True)]
  transfers between devices with their start and end apart: 10 -> 10, of which waited for: 5 -> 6; matrix products, arithmetic and copies ran while one was open for 3% -> 3% of each run, Pallas kernels for 16% -> 14%
where the time goes in v5:
time: 703 us; the launch traced here: 699 us
  Pallas kernels  560 us (80%)
  waiting for transfers between devices  52.4 us (7%)
  local copies, waits for them, and re-layouts  27.8 us (4%)
  starting transfers between devices  23.1 us (3%)
  other arithmetic  17.6 us (3%)
  between operations  14.6 us (2%)
    pallas_call x4, Pallas kernels, call_stage(): pl.pallas_call(kernel, in_specs=[vmem if near else hbm for _, near in inp...  527 us
    ppermute x4, waiting for transfers between devices, body(): other = lax.ppermute(gain_total, axis, [(i, i ^ bit) for i in range(count)])  39.9 us
    pallas_call x2, Pallas kernels, weight_sums(): pl.pallas_call(functools.partial(weight_kernel, places, stacked, extra),...  32.5 us
  transfers between devices with their start and end apart: 10, of which 6 were waited for; matrix products, arithmetic and copies ran while one was open for 3% of the time, Pallas kernels for 14%

profile of v5, /device:TPU:2, one launch (start us, length us, event | category | flops | bytes accessed | tf_op | source)
XLA Modules:
  0.0 699.4 jit_solution(15137338931093693576)
XLA Ops:
  7.2 0.0 reduce-scatter.3.cloned.1.call-start
  7.2 0.8 constant_dynamic-slice_fusion
  8.1 1.3 copy.52
  9.4 1.3 slice_bitcast_fusion.6
  10.7 0.1 broadcast_bitcast_fusion
  10.8 0.7 fusion.12.refs_6_
  11.5 1.7 copy.24
  13.3 1.6 copy.29.refs_2_.refs_3_
  14.8 2.1 fusion.17
  16.9 1.6 copy.43
  18.5 1.6 copy.44
  20.1 0.0 copy-done.3
  20.1 1.2 copy.46
  21.3 0.2 broadcast_compare_fusion
  21.5 4.4 select_convert_fusion
  25.9 80.8 %self_stage.1 = (f32[3,256,1024]{2,1,0:T(8,128)}, bf16[3,256,1024]{2,1,0:T(8,128)(2,1)}, bf16[3,1024,1024]{2,1,0:T(8,128)(2,1)}, bf16[3,1024,768]{2,1,0:T(8,128)...) custom-call(bf16[3,256,1024]{2,1,0:T(8,128)(2,1)} %bitcast.95, f32[3,1024]{1,0:T(4,128)} %bitcast.91, ...), custom_call_target="tpu_custom_call" | custom-call | flops 19327352832 | bytes 33554432 | tf_op jit(solution)/shard_map/self_stage/pallas_call | solution.py:273
  106.7 163.8 %middle_stage.1 = (f32[3,256,1024]{2,1,0:T(8,128)}, bf16[3,256,1024]{2,1,0:T(8,128)(2,1)}, bf16[3,1024,1024]{2,1,0:T(8,128)(2,1)}, bf16[3,1024,1024]{2,1,0:T(8,1...) custom-call(bf16[3,256,1024]{2,1,0:T(8,128)(2,1)} %get-tuple-element, ...), custom_call_target="tpu_custom_call" | custom-call | flops 26172456960 | bytes 33554432 | tf_op jit(solution)/shard_map/middle_stage/pallas_call | solution.py:273
  270.5 0.0 copy-start.6
  270.5 207.5 %middle_back_stage.1 = (f32[3,256,1024]{2,1,0:T(8,128)}, f32[2,8,1024]{2,1,0:T(8,128)}, bf16[3,1024,1024]{2,1,0:T(8,128)(2,1)}, bf16[3,1024,1024]{2,1,0:T(8,128)...) custom-call(bf16[3,256,1024]{2,1,0:T(8,128)(2,1)} %get-tuple-element, ...), custom_call_target="tpu_custom_call" | custom-call | flops 67645734912 | bytes 33554432 | tf_op jit(solution)/shard_map/middle_back_stage/pallas_call | solution.py:273
  478.0 0.0 copy-done.6
  478.0 12.1 %conditional.3 = (bf16[512,1024]{1,0:T(8,128)(2,1)S(1)}) conditional(s32[]{:T(128)} %convert_element_type.62, (bf16[3,1024,512]{2,1,0:T(8,128)(2,1)}, bf16[3,1024,1024]{2,1,0:T(8,128)(2,1)}) %tuple.28, () %tuple.29), branch_computations={%region_2.3_spmd, %region_3.4_spmd} | conditional | flops 3221225472 | bytes 9437192 | solution.py:1468
  482.5 7.6 %weight_sums.5 = bf16[512,1024]{1,0:T(8,128)(2,1)S(1)} custom-call(bf16[3072,512]{1,0:T(8,128)(2,1)} %bitcast.114, bf16[3072,1024]{1,0:T(8,128)(2,1)} %bitcast.107), custom_call_target="tpu_custom_call" | custom-call | flops 3221225472 | bytes 9437184 | tf_op jit(solution)/shard_map/cond/branch_0_fun/weight_sums/pallas_call | solution.py:1351
  490.1 11.0 %collective-permute-start.3 = (bf16[512,1024]{1,0:T(8,128)(2,1)S(1)}, bf16[512,1024]{1,0:T(8,128)(2,1)S(1)}, u32[]{:S(2)}, u32[]{:S(2)}) collective-permute-start(bf16[512,1024]{1,0:T(8,128)(2,1)S(1)} %get-tuple-element.194), channel_id=1, source_target_pairs={{16,0},{17,1},{18,2},{19,3},{20,4},{21,5},{22,6},{23,7},{24,8},{25... | collective-permute-start | bytes 3145736 | tf_op jit(solution)/shard_map/ppermute | solution.py:1473
  501.1 26.1 %conditional.2 = (bf16[2624,1024]{1,0:T(8,128)(2,1)}, bf16[512,1024]{1,0:T(8,128)(2,1)S(1)}) conditional(s32[]{:T(128)} %convert_element_type.62, (bf16[3,1024,704]{2,1,0:T(8,128)(2,1)}, bf16[3,1024,1024]{2,1,0:T(8,128)(2,1)}, bf16[3,1024,704]{2,1,0:T(8,128)(2,1)}, bf16[3,1024,704]{2,1,0:T(8,128)(2,1)}, bf16[3,1024,1024]{2,1,0:T(8,128)(2,1)}, ...), branch_computations={%region_0.1_spmd, %region_1.2_spmd} | conditional | flops 16508780544 | bytes 43384848 | solution.py:1474
  501.1 24.8 %weight_sums.3 = bf16[2624,1024]{1,0:T(8,128)(2,1)} custom-call(bf16[3072,704]{1,0:T(8,128)(2,1)} %bitcast.110, bf16[3072,1024]{1,0:T(8,128)(2,1)} %bitcast.104, bf16[3072,704]{1,0:T(8,128)(2,1)} %bitcast.112, bf16[3072,704]{1,0:T(8,128)(2,1)} %bitcast.108, bf16[3072,1024]{1,0:T(8,128)(2,1)} %bitcast.103, bf16[3072,256]{1,0:T(8,128)(2,1)} %bitcast.116, ...), custom_call_target="tpu_custom_call" | custom-call | flops 16508780544 | bytes 41287680 | tf_op jit(solution)/shard_map/cond/branch_0_fun/weight_sums/pallas_call | solution.py:1351
  525.9 1.3 slice.92
  527.3 0.0 collective-permute-done.3
  527.3 1.4 select_dynamic-update-slice_fusion
  528.7 0.0 reduce-scatter.3.cloned.1.call-update
  528.7 0.0 reduce-scatter.5.cloned.1.call-start
  528.7 3.4 fusion.16
  532.1 1.9 collective-permute-start.1
  534.0 0.7 fusion.14.refs_6_
  534.8 2.6 collective-permute-done.1
  537.4 3.2 add_convert_fusion.1
  540.7 74.9 %self_back_stage.1 = (f32[3,256,1024]{2,1,0:T(8,128)}, f32[8,1024]{1,0:T(8,128)}, bf16[1024,1024]{1,0:T(8,128)(2,1)}) custom-call(bf16[3,256,1024]{2,1,0:T(8,128)(2,1)} %bitcast.96, f32[3,1024]{1,0:T(4,128)} %bitcast.92, f32[3,256,1024]{2,1,0:T(8,128)} %get-tuple-element.121.refs_2_, bf16[1024,768]{1,0:T(8,128)(2,1)} %copy.29.refs_2_.refs_3_, ...), custom_call_target="tpu_custom_call" | custom-call | flops 38654705664 | bytes 33554432 | tf_op jit(solution)/shard_map/self_back_stage/pallas_call | solution.py:273
  615.6 9.7 %reduce-scatter.3.cloned.1.call-done = bf16[2624,256]{1,0:T(8,128)(2,1)} async-done(((bf16[2624,1024]{1,0:T(8,128)(2,1)}), bf16[2624,256]{1,0:T(8,128)(2,1)}) %reduce-scatter.3.cloned.1.call-update) | async-done | bytes 1343504 | tf_op jit(solution)/shard_map/reduce_scatter | solution.py:1466
  625.4 0.0 reduce-scatter.5.cloned.1.call-update
  625.4 1.9 collective-permute-start
  627.3 3.4 collective-permute-start.2
  630.8 0.3 collective-permute-start.4
  631.1 1.0 collective-permute-done.4
  632.1 0.6 collective-permute-start.5
  632.7 33.9 %collective-permute-done.5 = f32[3,1024]{1,0:T(4,128)S(1)} collective-permute-done((f32[3,1024]{1,0:T(4,128)S(1)}, f32[3,1024]{1,0:T(4,128)S(1)}, u32[]{:S(2)}, u32[]{:S(2)}) %collective-permute-start.5) | collective-permute-done | bytes 12320 | tf_op jit(solution)/shard_map/ppermute | solution.py:1523
  666.6 1.6 collective-permute-start.6
  668.2 2.8 collective-permute-done.6
  671.0 2.3 collective-permute-start.7
  673.3 2.3 collective-permute-done.7
  675.6 0.1 dynamic-slice_add_fusion
  675.7 0.6 broadcast_in_dim.76
  676.3 0.0 collective-permute-done
  676.3 0.0 collective-permute-done.2
  676.3 5.2 fusion.1
  681.5 0.2 convert_element_type.64
  681.7 1.0 copy.37
  682.7 1.0 slice_bitcast_fusion
  683.7 1.2 maximum_bitcast_fusion
  684.9 1.0 slice.96
  686.0 0.3 copy.33
  686.3 1.1 copy.35
  687.4 0.0 copy-done
  687.4 0.1 convert_element_type.63
  687.6 0.8 copy.36
  688.4 4.0 copy.64
  (31 shorter events, 0.3 us)
Async XLA Ops:
  7.2 618.2 %reduce-scatter.3.cloned.1.call-start = ((), (), s32[]{:S(2)}) async-start(), calls=%async_computation.2 | async-start | bytes 6717440 | tf_op jit(solution)/shard_map/reduce_scatter | solution.py:1466
  18.5 1.6 copy-start.3
  270.5 207.6 %copy-start.6 = (bf16[3,1024,256]{2,1,0:T(8,128)(2,1)}, bf16[3,1024,256]{2,1,0:T(8,128)(2,1)S(1)}, u32[]{:S(2)}) copy-start(bf16[3,1024,256]{2,1,0:T(8,128)(2,1)S(1)} %get-tuple-element.107.refs_17_) | copy-start | bytes 4718596
  490.1 37.1 %collective-permute-start.3 = (bf16[512,1024]{1,0:T(8,128)(2,1)S(1)}, bf16[512,1024]{1,0:T(8,128)(2,1)S(1)}, u32[]{:S(2)}, u32[]{:S(2)}) collective-permute-start(bf16[512,1024]{1,0:T(8,128)(2,1)S(1)} %get-tuple-element.194), channel_id=1, source_target_pairs={{16,0},{17,1},{18,2},{19,3},{20,4},{21,5},{22,6},{23,7},{24,8},{25... | collective-permute-start | bytes 3145736 | tf_op jit(solution)/shard_map/ppermute | solution.py:1473
  528.7 156.2 %reduce-scatter.5.cloned.1.call-start = ((), (), s32[]{:S(2)}) async-start(), calls=%async_computation.3 | async-start | bytes 2621440 | tf_op jit(solution)/shard_map/reduce_scatter | solution.py:1466
  532.1 5.3 collective-permute-start.1
  540.7 135.6 %copy-start.1 = (f32[3,256,1024]{2,1,0:T(8,128)S(1)}, f32[3,256,1024]{2,1,0:T(8,128)}, u32[]{:S(2)}) copy-start(f32[3,256,1024]{2,1,0:T(8,128)} %get-tuple-element.100.refs_11_) | copy-start | bytes 9437188
  615.6 15.1 %copy-start.4 = (f32[2,8,1024]{2,1,0:T(8,128)S(1)}, f32[2,8,1024]{2,1,0:T(8,128)}, u32[]{:S(2)}) copy-start(f32[2,8,1024]{2,1,0:T(8,128)} %get-tuple-element.132) | copy-start | bytes 196612
  615.6 15.1 %copy-start.5 = (f32[8,1024]{1,0:T(8,128)S(1)}, f32[8,1024]{1,0:T(8,128)}, u32[]{:S(2)}) copy-start(f32[8,1024]{1,0:T(8,128)} %get-tuple-element.131) | copy-start | bytes 98308
  625.4 50.9 %collective-permute-start = (bf16[3,256,1024]{2,1,0:T(8,128)(2,1)}, bf16[3,256,1024]{2,1,0:T(8,128)(2,1)}, u32[]{:S(2)}, u32[]{:S(2)}) collective-permute-start(bf16[3,256,1024]{2,1,0:T(8,128)(2,1)} %get-tuple-element.149), channel_id=1, source_target_pairs={{16,17},{17,16},{18,19},{19,18},{20,21},{21,20},{22,23},{23,22},{2... | collective-permute-start | bytes 4718600 | tf_op jit(solution)/shard_map/ppermute | solution.py:1491
  627.3 49.0 %collective-permute-start.2 = (bf16[3,256,1024]{2,1,0:T(8,128)(2,1)}, bf16[3,256,1024]{2,1,0:T(8,128)(2,1)}, u32[]{:S(2)}, u32[]{:S(2)}) collective-permute-start(bf16[3,256,1024]{2,1,0:T(8,128)(2,1)} %add_convert_fusion.1), channel_id=1, source_target_pairs={{16,18},{17,19},{18,16},{19,17},{20,22},{21,23},{22,20},{23,21},{2... | collective-permute-start | bytes 4718600 | tf_op jit(solution)/shard_map/ppermute | solution.py:1491
  630.8 1.2 collective-permute-start.4
  632.1 34.5 %collective-permute-start.5 = (f32[3,1024]{1,0:T(4,128)S(1)}, f32[3,1024]{1,0:T(4,128)S(1)}, u32[]{:S(2)}, u32[]{:S(2)}) collective-permute-start(f32[3,1024]{1,0:T(4,128)S(1)} %fusion.15), channel_id=1, source_target_pairs={{0,2},{1,3},{2,0},{3,1},{4,6},{5,7},{6,4},{7,5},{8,10},{9,11},{10,... | collective-permute-start | bytes 36872 | tf_op jit(solution)/shard_map/ppermute | solution.py:1523
  666.6 4.4 collective-permute-start.6
  671.0 4.6 collective-permute-start.7
  676.3 5.2 copy-start.2
  686.0 1.4 copy-start
Sparse Core Ops, SparseCore 0:
  528.8 96.5 reduce-scatter.2
  627.6 44.3 reduce-scatter.4

commit v6 on v5

--- a/solution.py
+++ b/solution.py
@@ -406,15 +406,15 @@
 
 def self_back_kernel(n, *refs):
     (x, gain, slope, w_qkv, w_out, key_aug, tri_t) = refs[:7]
-    (qkv_in, mix_in, aug_in, full_in, ahead_in) = refs[7:12]
-    (total, gain_out, weights) = refs[12:15]
-    (own, got, out, back, qkv, mix, aug, grad, dqkv, full, acc) = refs[15:26]
-    sems = refs[26:]
+    (qkv_in, mix_in, aug_in, full_in, ahead_in, cross_in) = refs[7:13]
+    (total, gain_out, weights) = refs[13:16]
+    (own, got, out, back, qkv, mix, aug, grad, dqkv, full, acc) = refs[16:27]
+    sems = refs[27:]
     rows, size = x.shape[:2]
     hid = w_out.shape[0]
     gather = Gather(n, own, got, *sems[:2])
     sums = Sums(n, out, back, *sems[2:4])
-    load, load_full, load_ahead = sems[4:]
+    load, load_full, load_ahead, load_cross = sems[4:]
     ahead = 1 if rows > 1 else 0
     greet(n)
 
@@ -458,6 +458,10 @@
                 copy.start()
         for copy in loads(r):
             copy.start()
+    cross_load = pltpu.make_async_copy(
+        cross_in, weights.at[:, pl.ds(4 * hid, 2 * hid)], load_cross.at[0]
+    )
+    cross_load.start()
     full_load(0).start()
     gain_out[...] = jnp.zeros_like(gain_out)
     acc[...] = jnp.zeros_like(acc)
@@ -522,7 +526,8 @@
 
     sums.forward(rows - 1)
     add_weights(rows - 1)
-    weights[...] = acc[...].astype(BF)
+    weights[:, : 4 * hid] = acc[...].astype(BF)
+    cross_load.wait()
     finish(rows - 1)
 
     @pl.loop(0, rows)
@@ -535,7 +540,7 @@
 
 
 def self_back_stage(
-    n, x, gain, slope, w_qkv, w_out, key_aug, tri_t, qkv, mix, aug, full, first
+    n, x, gain, slope, w_qkv, w_out, key_aug, tri_t, qkv, mix, aug, full, first, cross
 ):
     rows, size, width = x.shape
     length, hid = n * size, w_out.shape[0]
@@ -545,11 +550,11 @@
         "self_back_stage",
         2,
         [(a, True) for a in (x, gain, slope, w_qkv, w_out, key_aug, tri_t)]
-        + [(a, False) for a in (qkv, mix, aug, full, first)],
+        + [(a, False) for a in (qkv, mix, aug, full, first, cross)],
         [
             ((rows, size, width), F32, True),
             ((8, width), F32, True),
-            ((width, 4 * hid), BF, True),
+            ((width, 6 * hid), BF, True),
         ],
         [
             pltpu.VMEM((rows, size, width), BF),
@@ -565,6 +570,7 @@
             pltpu.SemaphoreType.DMA((rows, 3)),
             pltpu.SemaphoreType.DMA((1,)),
             pltpu.SemaphoreType.DMA((n,)),
+            pltpu.SemaphoreType.DMA((1,)),
         ],
         rows * length * width * hid * 8 + rows * length * length * hid * 40,
     )
@@ -1465,25 +1471,24 @@
     def over_rows(total, dim):
         return lax.psum_scatter(total, "dp", scatter_dimension=dim, tiled=True)
 
-    sum_kv = lax.cond(
+    blank = jnp.zeros((width, 2 * hid), BF)
+    sum_kv, sum_qo = lax.cond(
         enc,
-        lambda: jnp.zeros((2 * hid, width), BF),
-        lambda: weight_sums([(dkv, full_b)], True),
+        lambda: (blank, blank),
+        lambda: (
+            weight_sums([(full_b, dkv)], False),
+            weight_sums([(full_a, dq), (full_g, mix)], False),
+        ),
     )
+    sum_kv, dgate = lax.optimization_barrier((sum_kv, dgate))
     sum_kv = lax.ppermute(sum_kv, "section", [(1, 0)])
     early = lax.cond(
         enc,
-        lambda: weight_sums(
-            [(dgate, full_a), (dup, full_a), (hidden, full_g)], True, 2 * hid
-        ),
-        lambda: weight_sums(
-            [(dgate, full_3), (dup, full_3), (hidden, full_cot), (dq, full_a), (mix, full_g)],
-            True,
-        ),
+        lambda: weight_sums([(dgate, full_a), (dup, full_a), (hidden, full_g)], True),
+        lambda: weight_sums([(dgate, full_3), (dup, full_3), (hidden, full_cot)], True),
     )
-    early = lax.dynamic_update_slice(
-        early, jnp.where(enc, sum_kv, early[3 * ffd :]), (3 * ffd, 0)
-    )
+    early, sum_kv = lax.optimization_barrier((early, sum_kv))
+    sum_cross = jnp.where(enc, sum_kv, sum_qo)
     got_early = over_rows(early, 1)
 
     def across(tensor, bit):
@@ -1502,9 +1507,9 @@
     dec_out = mid2 + have[0].astype(F32)
     block_out = jnp.where(enc, third, dec_out.astype(BF))
 
-    grad1, _, _ = lax.optimization_barrier((grad1, early, first))
+    grad1, _ = lax.optimization_barrier((grad1, early))
     input_grad, gain_first, late = self_back_stage(
-        n, x, gain, grad1, w_qkv, w_out, key_own, tri.T, qkv1, mix1, aug1, full1, lead
+        n, x, gain, grad1, w_qkv, w_out, key_own, tri.T, qkv1, mix1, aug1, full1, lead, sum_cross
     )
 
     late, got_early = lax.optimization_barrier((late, got_early))
@@ -1512,10 +1517,10 @@
     got_early = got_early.astype(F32)
     quarter = width // dp_size
     out_in = jnp.stack([got_early[:ffd].T, got_early[ffd : 2 * ffd].T], axis=1)
-    out_down = got_early[2 * ffd : 3 * ffd]
-    out_cross = got_early[3 * ffd :].T.reshape(quarter, 2, hid)
+    out_down = got_early[2 * ffd :]
+    out_cross = got_late[:, 4 * hid :].reshape(quarter, 2, hid)
     out_qkv = got_late[:, : 3 * hid].reshape(quarter, 3, hid)
-    out_out = got_late[:, 3 * hid :].T
+    out_out = got_late[:, 3 * hid : 4 * hid].T
     gain_parts = jnp.sum(gain_parts, axis=1)
     gain_total = jnp.stack([jnp.sum(gain_first, axis=0), gain_parts[1], gain_parts[0]])
     for axis, count in (("mp", n), ("dp", dp_size)):

time: 703 us -> 696 us (0.990)
  starting transfers between devices: 23.1 us -> 14.5 us
    ppermute x1, starting transfers between devices: 11 us -> 3.29 us  [body(): sum_kv = lax.ppermute(sum_kv, 'section', [(1, 0)])]
    pallas_call x2 -> x3, Pallas kernels: 32.5 us -> 37.2 us  [weight_sums(): pl.pallas_call(functools.partial(weight_kernel, places, stacked, extra),...]
  transfers between devices with their start and end apart: 10 -> 10, of which waited for: 6 -> 7; matrix products, arithmetic and copies ran while one was open for 3% -> 2% of each run, Pallas kernels for 14% -> 14%
where the time goes in v6:
time: 696 us; the launch traced here: 693 us
  Pallas kernels  564 us (81%)
  waiting for transfers between devices  51.6 us (7%)
  local copies, waits for them, and re-layouts  27.1 us (4%)
  other arithmetic  17 us (2%)
  between operations  14.6 us (2%)
  starting transfers between devices  14.5 us (2%)
    pallas_call x4, Pallas kernels, call_stage(): pl.pallas_call(kernel, in_specs=[vmem if near else hbm for _, near in inp...  527 us
    ppermute x4, waiting for transfers between devices, body(): other = lax.ppermute(gain_total, axis, [(i, i ^ bit) for i in range(count)])  43.9 us
    pallas_call x3, Pallas kernels, weight_sums(): pl.pallas_call(functools.partial(weight_kernel, places, stacked, extra),...  37.2 us
  transfers between devices with their start and end apart: 10, of which 7 were waited for; matrix products, arithmetic and copies ran while one was open for 2% of the time, Pallas kernels for 14%

profile of v6, /device:TPU:2, one launch (start us, length us, event | category | flops | bytes accessed | tf_op | source)
XLA Modules:
  0.0 692.6 jit_solution(1676277370768946871)
XLA Ops:
  7.2 0.0 copy-start.2
  7.2 0.0 reduce-scatter.3.cloned.1.call-start
  7.3 1.4 slice_bitcast_fusion.6
  8.7 1.3 copy.49
  10.0 0.7 constant_dynamic-slice_fusion
  10.8 0.1 broadcast_bitcast_fusion
  10.9 0.8 fusion.12
  11.7 2.4 copy.43
  14.2 0.0 copy-done.2
  14.2 0.9 copy.23
  15.0 1.6 copy.28.refs_2_.refs_3_
  16.6 2.1 fusion.17
  18.7 1.6 copy.41
  20.3 1.6 copy.40
  21.8 0.2 broadcast_compare_fusion
  22.1 4.3 select_convert_fusion
  26.4 80.8 %self_stage.1 = (f32[3,256,1024]{2,1,0:T(8,128)}, bf16[3,256,1024]{2,1,0:T(8,128)(2,1)}, bf16[3,1024,1024]{2,1,0:T(8,128)(2,1)}, bf16[3,1024,768]{2,1,0:T(8,128)...) custom-call(bf16[3,256,1024]{2,1,0:T(8,128)(2,1)} %bitcast.97, f32[3,1024]{1,0:T(4,128)} %bitcast.93, ...), custom_call_target="tpu_custom_call" | custom-call | flops 19327352832 | bytes 33554432 | tf_op jit(solution)/shard_map/self_stage/pallas_call | solution.py:273
  107.3 163.7 %middle_stage.1 = (f32[3,256,1024]{2,1,0:T(8,128)}, bf16[3,256,1024]{2,1,0:T(8,128)(2,1)}, bf16[3,1024,1024]{2,1,0:T(8,128)(2,1)}, bf16[3,1024,1024]{2,1,0:T(8,1...) custom-call(bf16[3,256,1024]{2,1,0:T(8,128)(2,1)} %get-tuple-element, ...), custom_call_target="tpu_custom_call" | custom-call | flops 26172456960 | bytes 33554432 | tf_op jit(solution)/shard_map/middle_stage/pallas_call | solution.py:273
  271.0 207.1 %middle_back_stage.1 = (f32[3,256,1024]{2,1,0:T(8,128)}, f32[2,8,1024]{2,1,0:T(8,128)}, bf16[3,1024,1024]{2,1,0:T(8,128)(2,1)}, bf16[3,1024,1024]{2,1,0:T(8,128)...) custom-call(bf16[3,256,1024]{2,1,0:T(8,128)(2,1)} %get-tuple-element, ...), custom_call_target="tpu_custom_call" | custom-call | flops 67645734912 | bytes 33554432 | tf_op jit(solution)/shard_map/middle_back_stage/pallas_call | solution.py:273
  478.0 20.7 %conditional.2 = (bf16[1024,512]{1,0:T(8,128)(2,1)}, bf16[1024,512]{1,0:T(8,128)(2,1)S(1)}) conditional(s32[]{:T(128)} %convert_element_type.62, (bf16[3,1024,1024]{2,1,0:T(8,128)(2,1)}, bf16[3,1024,512]{2,1,0:T(8,128)(2,1)}, bf16[3,1024,1024]{2,1,0:T(8,128)(2,1)}, bf16[3,1024,256]{2,1,0:T(8,128)(2,1)}, bf16[3,1024,1024]{2,1,0:T(8,128)(2,1)}, ...), branch_computations={%region_0.1_spmd, %region_1.2_spmd} | conditional | flops 6442450944 | bytes 25165840 | solution.py:1475
  481.5 8.5 %weight_sums.4 = bf16[1024,512]{1,0:T(8,128)(2,1)} custom-call(bf16[3072,1024]{1,0:T(8,128)(2,1)} %bitcast.105, bf16[3072,512]{1,0:T(8,128)(2,1)} %bitcast.112), custom_call_target="tpu_custom_call" | custom-call | flops 3221225472 | bytes 9437184 | tf_op jit(solution)/shard_map/cond/branch_0_fun/weight_sums/pallas_call | solution.py:1357
  490.1 8.7 %weight_sums.5 = bf16[1024,512]{1,0:T(8,128)(2,1)S(1)} custom-call(bf16[3072,1024]{1,0:T(8,128)(2,1)} %bitcast.74, bf16[3072,256]{1,0:T(8,128)(2,1)} %bitcast.81, bf16[3072,1024]{1,0:T(8,128)(2,1)} %bitcast.76, bf16[3072,256]{1,0:T(8,128)(2,1)S(1)} %bitcast.80), custom_call_target="tpu_custom_call" | custom-call | flops 3221225472 | bytes 15728640 | tf_op jit(solution)/shard_map/cond/branch_0_fun/weight_sums/pallas_call | solution.py:1357
  498.8 3.3 collective-permute-start.3
  502.1 20.0 %conditional.3 = (bf16[2112,1024]{1,0:T(8,128)(2,1)}) conditional(s32[]{:T(128)} %convert_element_type.62, (bf16[3,1024,704]{2,1,0:T(8,128)(2,1)}, bf16[3,1024,1024]{2,1,0:T(8,128)(2,1)}, bf16[3,1024,704]{2,1,0:T(8,128)(2,1)}, bf16[3,1024,704]{2,1,0:T(8,128)(2,1)}, bf16[3,1024,1024]{2,1,0:T(8,128)(2,1)}) %tuple.29, (bf16[3,1024,704]{2,1,0:T(8,128)(2,1)}, ...), branch_computations={%region_2.3_spmd, %region_3.4_spmd} | conditional | flops 13287555072 | bytes 25559048 | solution.py:1485
  502.1 20.0 %weight_sums.6 = bf16[2112,1024]{1,0:T(8,128)(2,1)} custom-call(bf16[3072,704]{1,0:T(8,128)(2,1)} %bitcast.108, bf16[3072,1024]{1,0:T(8,128)(2,1)} %bitcast.104, bf16[3072,704]{1,0:T(8,128)(2,1)} %bitcast.110, bf16[3072,704]{1,0:T(8,128)(2,1)} %bitcast.106, bf16[3072,1024]{1,0:T(8,128)(2,1)} %bitcast.103), custom_call_target="tpu_custom_call" | custom-call | flops 13287555072 | bytes 25559040 | tf_op jit(solution)/shard_map/cond/branch_0_fun/weight_sums/pallas_call | solution.py:1357
  522.1 2.9 collective-permute-done.3
  525.0 0.0 reduce-scatter.3.cloned.1.call-update
  525.0 0.0 reduce-scatter.5.cloned.1.call-start
  525.1 1.1 broadcast_select_fusion.refs_12_
  526.2 75.4 %self_back_stage.1 = (f32[3,256,1024]{2,1,0:T(8,128)}, f32[8,1024]{1,0:T(8,128)}, bf16[1024,1536]{1,0:T(8,128)(2,1)}) custom-call(bf16[3,256,1024]{2,1,0:T(8,128)(2,1)} %bitcast.98, f32[3,1024]{1,0:T(4,128)} %bitcast.94, f32[3,256,1024]{2,1,0:T(8,128)} %get-tuple-element.125.refs_2_, bf16[1024,768]{1,0:T(8,128)(2,1)} %copy.28.refs_2_.refs_3_, ...), custom_call_target="tpu_custom_call" | custom-call | flops 38654705664 | bytes 33554432 | tf_op jit(solution)/shard_map/self_back_stage/pallas_call | solution.py:273
  601.5 4.1 reduce-scatter.3.cloned.1.call-done
  605.7 0.0 reduce-scatter.5.cloned.1.call-update
  605.7 3.4 fusion.16
  609.1 1.9 collective-permute-start.1
  611.0 0.0 copy-start.4
  611.0 2.7 collective-permute-start
  613.7 0.7 collective-permute-done.1
  614.4 3.6 add_convert_fusion.1
  617.9 3.4 collective-permute-start.2
  621.4 0.1 collective-permute-start.4
  621.5 1.2 collective-permute-done.4
  622.7 0.6 collective-permute-start.5
  623.3 33.5 %collective-permute-done.5 = f32[3,1024]{1,0:T(4,128)S(1)} collective-permute-done((f32[3,1024]{1,0:T(4,128)S(1)}, f32[3,1024]{1,0:T(4,128)S(1)}, u32[]{:S(2)}, u32[]{:S(2)}) %collective-permute-start.5) | collective-permute-done | bytes 12320 | tf_op jit(solution)/shard_map/ppermute | solution.py:1528
  656.9 1.5 collective-permute-start.6
  658.4 4.5 collective-permute-done.6
  662.9 1.0 collective-permute-start.7
  663.9 4.7 collective-permute-done.7
  668.6 0.1 dynamic-slice_add_fusion
  668.7 0.6 broadcast_in_dim.79
  669.2 0.0 collective-permute-done
  669.2 0.0 collective-permute-done.2
  669.2 5.2 fusion.1
  674.4 0.0 copy-done.3
  674.4 0.2 convert_element_type.64
  674.6 1.0 slice_bitcast_fusion
  675.6 1.2 maximum_bitcast_fusion
  676.8 1.1 slice.92
  677.9 1.1 broadcast_in_dim_reshape.8
  679.0 0.1 slice.87
  679.1 0.3 copy.32
  679.3 1.1 copy.33
  680.5 0.2 convert_element_type.63
  680.7 0.8 copy.34
  681.5 4.0 copy.60
  (28 shorter events, 0.2 us)
Async XLA Ops:
  7.2 7.0 %copy-start.2 = (bf16[1,1024,3,256]{3,1,2,0:T(8,128)(2,1)S(1)}, bf16[1,1024,3,256]{3,1,2,0:T(8,128)(2,1)}, u32[]{:S(2)}) copy-start(bf16[1,1024,3,256]{3,1,2,0:T(8,128)(2,1)} %param.16) | copy-start | bytes 4718596
  7.2 598.5 %reduce-scatter.3.cloned.1.call-start = ((), (), s32[]{:S(2)}) async-start(), calls=%async_computation.2 | async-start | bytes 5406720 | tf_op jit(solution)/shard_map/reduce_scatter | solution.py:1472
  498.8 26.2 %collective-permute-start.3 = (bf16[1024,512]{1,0:T(8,128)(2,1)}, bf16[1024,512]{1,0:T(8,128)(2,1)S(1)}, u32[]{:S(2)}, u32[]{:S(2)}) collective-permute-start(bf16[1024,512]{1,0:T(8,128)(2,1)} %get-tuple-element.123), channel_id=1, source_target_pairs={{16,0},{17,1},{18,2},{19,3},{20,4},{21,5},{22,6},{23,7},{24,8},{25... | collective-permute-start | bytes 3145736 | tf_op jit(solution)/shard_map/ppermute | solution.py:1484
  525.0 151.8 %reduce-scatter.5.cloned.1.call-start = ((), (), s32[]{:S(2)}) async-start(), calls=%async_computation.3 | async-start | bytes 3932160 | tf_op jit(solution)/shard_map/reduce_scatter | solution.py:1472
  609.1 5.3 collective-permute-start.1
  611.0 10.3 %copy-start.4 = (f32[2,8,1024]{2,1,0:T(8,128)S(1)}, f32[2,8,1024]{2,1,0:T(8,128)}, u32[]{:S(2)}) copy-start(f32[2,8,1024]{2,1,0:T(8,128)} %get-tuple-element.138) | copy-start | bytes 196612
  611.0 10.4 %copy-start.5 = (f32[8,1024]{1,0:T(8,128)S(1)}, f32[8,1024]{1,0:T(8,128)}, u32[]{:S(2)}) copy-start(f32[8,1024]{1,0:T(8,128)} %get-tuple-element.137) | copy-start | bytes 98308
  611.0 58.2 %copy-start.1 = (f32[3,256,1024]{2,1,0:T(8,128)S(1)}, f32[3,256,1024]{2,1,0:T(8,128)}, u32[]{:S(2)}) copy-start(f32[3,256,1024]{2,1,0:T(8,128)} %get-tuple-element.102.refs_11_) | copy-start | bytes 9437188
  611.0 58.2 %collective-permute-start = (bf16[3,256,1024]{2,1,0:T(8,128)(2,1)}, bf16[3,256,1024]{2,1,0:T(8,128)(2,1)}, u32[]{:S(2)}, u32[]{:S(2)}) collective-permute-start(bf16[3,256,1024]{2,1,0:T(8,128)(2,1)} %get-tuple-element.155), channel_id=1, source_target_pairs={{16,17},{17,16},{18,19},{19,18},{20,21},{21,20},{22,23},{23,22},{2... | collective-permute-start | bytes 4718600 | tf_op jit(solution)/shard_map/ppermute | solution.py:1496
  617.9 51.3 %collective-permute-start.2 = (bf16[3,256,1024]{2,1,0:T(8,128)(2,1)}, bf16[3,256,1024]{2,1,0:T(8,128)(2,1)}, u32[]{:S(2)}, u32[]{:S(2)}) collective-permute-start(bf16[3,256,1024]{2,1,0:T(8,128)(2,1)} %add_convert_fusion.1), channel_id=1, source_target_pairs={{16,18},{17,19},{18,16},{19,17},{20,22},{21,23},{22,20},{23,21},{2... | collective-permute-start | bytes 4718600 | tf_op jit(solution)/shard_map/ppermute | solution.py:1496
  621.4 1.2 collective-permute-start.4
  622.7 34.1 %collective-permute-start.5 = (f32[3,1024]{1,0:T(4,128)S(1)}, f32[3,1024]{1,0:T(4,128)S(1)}, u32[]{:S(2)}, u32[]{:S(2)}) collective-permute-start(f32[3,1024]{1,0:T(4,128)S(1)} %fusion.15), channel_id=1, source_target_pairs={{0,2},{1,3},{2,0},{3,1},{4,6},{5,7},{6,4},{7,5},{8,10},{9,11},{10,... | collective-permute-start | bytes 36872 | tf_op jit(solution)/shard_map/ppermute | solution.py:1528
  656.9 6.1 collective-permute-start.6
  662.9 5.7 collective-permute-start.7
  669.2 5.2 copy-start.3
  676.8 2.2 copy-start
Sparse Core Ops, SparseCore 0:
  525.1 80.4 reduce-scatter.2
  608.0 61.4 reduce-scatter.4
